TPU v7x, 32 devices: a whole 2x2x4 slice. The times are simulated.
32 devices in a mesh: dp: 8 (over y, x, core), section: 4 (over z).
Axes of the slice: x: 2, y: 2, z: 4, core: 2. Of those that a mesh axis runs over, the one named last changes fastest.
Arguments:
- saved_inputs: bfloat16 [4, 2, 48, 6144], P('section', None, 'dp'), may hold values from -6 to 6
- carried: bfloat16 [4, 48, 6144], P('section', 'dp'), may hold values from -6 to 6
- head_grad: bfloat16 [48, 6144], P('dp'), may hold values from -6 to 6
- routing: int32 [4, 2, 48, 2], P('section', None, 'dp'), may hold values from 0 to 7, as said below
- replica_counts: int32 [8], replicated, may hold values from 2 to 5
- router: float32 [4, 6144, 8], P('section'), may hold values from -0.21875 to 0.21875
- w_in: bfloat16 [4, 8, 1536, 4096], P('section', 'dp'), may hold values from -0.078125 to 0.078125
- w_out: bfloat16 [4, 8, 4096, 1536], P('section', 'dp'), may hold values from -0.0625 to 0.0625
Outputs:
- input_grad: bfloat16 [2, 4, 48, 6144], P(None, 'section', 'dp')
- grad_in: bfloat16 [4, 8, 1536, 4096], P('section', 'dp')
- grad_out: bfloat16 [4, 8, 4096, 1536], P('section', 'dp')
- grad_router: float32 [4, 6144, 8], P('section')
Inputs may be any that keep to these rules, and one draw needn't show every extreme that they name: `routing`: each row names 2 different experts; in every section and step at most 2 of one device's 6 tokens name expert 0, and exactly 2 on some device.
All inputs are finite; a program needn't handle non-finite values.
Results may differ from a plain program's by a relative error of at most 0.0057.
Values may be sent and summed in bfloat16 or wider, within the bound.
No kernel may reach another device: no remote copies, remote signals or barrier semaphores. Data moves between devices by JAX's collectives and lax.ppermute only.
A program may use at most 128 MiB of HBM per device.

v0:
```python
import jax
import jax.numpy as jnp
from jax import lax
from jax.sharding import PartitionSpec as P

STEPS = 2
CAP = 2


def shifted(array, axis, by):
    devices = lax.axis_size(axis)
    pairs = [(i, i + by) for i in range(devices) if 0 <= i + by < devices]
    return lax.ppermute(array, axis, pairs)


def from_partner(block, axis, distance):
    count = lax.axis_size(axis)
    route = []
    for low in range(count):
        high = low | 1 << distance
        if high != low and high < count:
            route += [(low, high), (high, low)]
    return lax.ppermute(block, axis, route)


def silu_grad(value):
    sig = jax.nn.sigmoid(value)
    return sig * (1.0 + value * (1.0 - sig))


def local(saved_inputs, carried, head_grad, routing, replica_counts, router, w_in, w_out):
    hi = lax.Precision.HIGHEST
    section_count = lax.axis_size("section")
    section_index = lax.axis_index("section")
    dev_count = lax.axis_size("dp")
    dev_index = lax.axis_index("dp")
    groups = dev_count // 4
    width = head_grad.shape[1]
    part = w_in.shape[2]
    hidden = w_in.shape[3]
    experts = router.shape[2]
    rows = dev_count * CAP
    weight_in = w_in[0, 0]
    weight_out = w_out[0, 0]
    router_w = router[0]
    quarter = dev_index % 4
    my_count = replica_counts[dev_index]
    first = (jnp.arange(experts) == 0).astype(jnp.float32)
    slots = jnp.arange(CAP, dtype=jnp.int32)

    def prepare(step):
        xin = saved_inputs[0, step]
        ids = routing[0, step]
        live = step + section_index < my_count
        xf = xin.astype(jnp.float32)
        logits = jnp.dot(xf, router_w, precision=hi)
        expo = jnp.exp(logits)
        prob = expo / jnp.sum(expo, axis=1, keepdims=True)
        routed = ((ids[:, 0] == 0) | (ids[:, 1] == 0)) & live
        flags = routed.astype(jnp.int32)
        slot = jnp.cumsum(flags, dtype=jnp.int32) - 1
        table = ((slot[None, :] == slots[:, None]) & routed[None, :]).astype(jnp.float32)
        xs = jnp.dot(table.astype(jnp.bfloat16), xin, preferred_element_type=jnp.float32).astype(
            jnp.bfloat16
        )
        gate = jnp.dot(table, prob[:, 0], precision=hi).astype(jnp.bfloat16)
        xsend = jnp.broadcast_to(
            xs.reshape(CAP, 4, part).transpose(1, 0, 2)[None], (groups, 4, CAP, part)
        ).reshape(dev_count, CAP, part)
        gsend = jnp.broadcast_to(gate[None], (dev_count, CAP))
        return (xf, prob, table, live, xsend, gsend)

    prepared = [prepare(step) for step in range(STEPS)]
    acc_in = jnp.zeros((part, hidden), jnp.float32)
    acc_out = jnp.zeros((hidden, part), jnp.float32)
    acc_router = jnp.zeros((width, experts), jnp.float32)
    outputs = []
    incoming = carried[0]
    for step in range(STEPS):
        xf, prob, table, live, xsend, gsend = prepared[step]
        if step == 1:
            passed = shifted(outputs[0], "section", -1)
            incoming = jnp.where(section_index == section_count - 1, head_grad, passed)
        grad_in_tok = jnp.where(live, incoming, jnp.zeros_like(incoming))
        ys = jnp.dot(
            table.astype(jnp.bfloat16), grad_in_tok, preferred_element_type=jnp.float32
        ).astype(jnp.bfloat16)
        ysend = jnp.broadcast_to(
            ys.reshape(CAP, 4, part).transpose(1, 0, 2)[None], (groups, 4, CAP, part)
        ).reshape(dev_count, CAP, part)
        recv_x, recv_y, recv_g = (
            lax.all_to_all(xsend, "dp", split_axis=0, concat_axis=0, tiled=True),
            lax.all_to_all(ysend, "dp", split_axis=0, concat_axis=0, tiled=True),
            lax.all_to_all(gsend, "dp", split_axis=0, concat_axis=0, tiled=True),
        )
        rows_x = recv_x.reshape(rows, part)
        rows_y = recv_y.reshape(rows, part)
        gate_f = recv_g.reshape(rows).astype(jnp.float32)[:, None]
        pre = jnp.dot(rows_x, weight_in, preferred_element_type=jnp.float32)
        upper = lax.dot_general(
            rows_y, weight_out, (((1,), (1,)), ((), ())), preferred_element_type=jnp.float32
        )
        for bit in range(2):
            other_pre, other_upper = from_partner((pre, upper), "dp", bit)
            pre = pre + other_pre
            upper = upper + other_upper
        act = jax.nn.silu(pre)
        dpre = (gate_f * upper * silu_grad(pre)).astype(jnp.bfloat16)
        scaled = (gate_f * act).astype(jnp.bfloat16)
        block_sum = jnp.sum(act * upper, axis=1)
        block_sum = jnp.where(quarter == 0, block_sum, jnp.zeros_like(block_sum)).astype(
            jnp.bfloat16
        )
        acc_in = acc_in + lax.dot_general(
            rows_x, dpre, (((0,), (0,)), ((), ())), preferred_element_type=jnp.float32
        )
        acc_out = acc_out + lax.dot_general(
            scaled, rows_y, (((0,), (0,)), ((), ())), preferred_element_type=jnp.float32
        )
        dx_part = lax.dot_general(
            dpre, weight_in, (((1,), (1,)), ((), ())), preferred_element_type=jnp.float32
        ).astype(jnp.bfloat16)
        back_x, back_g = (
            lax.all_to_all(
                dx_part.reshape(dev_count, CAP, part), "dp", split_axis=0, concat_axis=0, tiled=True
            ),
            lax.all_to_all(
                block_sum.reshape(dev_count, CAP), "dp", split_axis=0, concat_axis=0, tiled=True
            ),
        )
        summed = jnp.sum(back_x.astype(jnp.float32).reshape(groups, 4, CAP, part), axis=0)
        dxs = summed.transpose(1, 0, 2).reshape(CAP, width)
        dgate = jnp.sum(back_g.astype(jnp.float32), axis=0)
        dxe = lax.dot_general(table, dxs, (((0,), (0,)), ((), ())), precision=hi)
        dg_tok = lax.dot_general(table, dgate, (((0,), (0,)), ((), ())), precision=hi)
        dlog = (dg_tok * prob[:, 0])[:, None] * (first[None, :] - prob)
        result = grad_in_tok.astype(jnp.float32) + dxe + jnp.dot(dlog, router_w.T, precision=hi)
        outputs.append(result.astype(jnp.bfloat16))
        router_term = jnp.dot(xf.T, dlog, precision=hi)
        acc_router = acc_router + lax.psum(router_term, "dp")
    input_grad = jnp.stack(outputs)[:, None]
    grad_in = acc_in.astype(jnp.bfloat16)[None, None]
    grad_out = acc_out.astype(jnp.bfloat16)[None, None]
    return (input_grad, grad_in, grad_out, acc_router[None])


def solution(mesh):
    in_specs = (
        P("section", None, "dp", None),
        P("section", "dp", None),
        P("dp", None),
        P("section", None, "dp", None),
        P(),
        P("section", None, None),
        P("section", "dp", None, None),
        P("section", "dp", None, None),
    )
    out_specs = (
        P(None, "section", "dp", None),
        P("section", "dp", None, None),
        P("section", "dp", None, None),
        P("section", None, None),
    )
    return jax.shard_map(local, mesh=mesh, in_specs=in_specs, out_specs=out_specs, check_vma=False)
```

profile of v0, /device:TPU:0, one launch (start us, length us, event | category | flops | bytes accessed | tf_op | source)
XLA Modules:
  0.0 254.0 jit_solution(5481240463229272586)
XLA Ops:
  11.8 5.2 %all-to-all-start.1 = ((bf16[8,2,1536]{2,1,0:T(2,128)(2,1)}), bf16[8,2,1536]{2,1,0:T(2,128)(2,1)S(1)}, u32[]{:S(2)}, u32[]{:S(2)}) async-start(bf16[8,2,1536]{2,1,0:T(2,128)(2,1)} %bitcast.9), calls=%async_computation.1 | async-start | bytes 98304 | tf_op jit(solution)/shard_map/all_to_all | solution.py:93
  22.5 3.3 %all-to-all-start.2 = ((bf16[8,2,1536]{2,1,0:T(2,128)(2,1)}), bf16[8,2,1536]{2,1,0:T(2,128)(2,1)S(1)}, u32[]{:S(2)}, u32[]{:S(2)}) async-start(bf16[8,2,1536]{2,1,0:T(2,128)(2,1)} %bitcast.12), calls=%async_computation.2 | async-start | bytes 98304 | tf_op jit(solution)/shard_map/all_to_all | solution.py:92
  25.9 7.9 %fusion.12 = f32[16,4096]{1,0:T(8,128)S(1)} fusion(bf16[16,1536]{1,0:T(8,128)(2,1)S(1)} %reshape.242, bf16[1,1,4096,1536]{3,2,1,0:T(8,128)(2,1)} %param.15), kind=kOutput, calls=%fused_computation.14 | convolution fusion | flops 201326592 | bytes 12894208 | tf_op jit(solution)/shard_map/dot_general | solution.py:100
  34.9 3.9 %all-to-all-start = ((bf16[8,1,2]{2,1,0:T(2,128)(2,1)}), bf16[8,1,2]{2,1,0:T(2,128)(2,1)S(1)}, u32[]{:S(2)}, u32[]{:S(2)}) async-start(bf16[8,1,2]{2,1,0:T(2,128)(2,1)} %broadcast_in_dim.20), calls=%async_computation | async-start | bytes 8192 | tf_op jit(solution)/shard_map/all_to_all | solution.py:94
  38.8 6.3 %fusion.8 = f32[16,4096]{1,0:T(8,128)S(1)} fusion(bf16[16,1536]{1,0:T(8,128)(2,1)S(1)} %reshape.245, bf16[1,1,1536,4096]{3,2,1,0:T(8,128)(2,1)} %param.14), kind=kOutput, calls=%fused_computation.10 | convolution fusion | flops 201326592 | bytes 12894208 | tf_op jit(solution)/shard_map/dot_general | solution.py:99
  46.5 3.9 %all-to-all-start.7 = ((bf16[8,2,1536]{2,1,0:T(2,128)(2,1)}), bf16[8,2,1536]{2,1,0:T(2,128)(2,1)S(1)}, u32[]{:S(2)}, u32[]{:S(2)}) async-start(bf16[8,2,1536]{2,1,0:T(2,128)(2,1)} %bitcast.28), calls=%async_computation.7 | async-start | bytes 98304 | tf_op jit(solution)/shard_map/all_to_all | solution.py:92
  50.4 4.8 %all-to-all-done.7 = bf16[8,2,1536]{2,1,0:T(2,128)(2,1)S(1)} async-done(((bf16[8,2,1536]{2,1,0:T(2,128)(2,1)}), bf16[8,2,1536]{2,1,0:T(2,128)(2,1)S(1)}, u32[]{:S(2)}, u32[]{:S(2)}) %all-to-all-start.7) | async-done | bytes 49184 | tf_op jit(solution)/shard_map/all_to_all | solution.py:92
  57.5 6.3 %fusion.4 = f32[16,4096]{1,0:T(8,128)S(1)} fusion(bf16[16,1536]{1,0:T(8,128)(2,1)S(1)} %reshape.255, bf16[1,1,1536,4096]{3,2,1,0:T(8,128)(2,1)} %param.14), kind=kOutput, calls=%fused_computation.6 | convolution fusion | flops 201326592 | bytes 12894208 | tf_op jit(solution)/shard_map/dot_general | solution.py:99
  64.6 4.3 %collective-permute-done.3 = f32[16,4096]{1,0:T(8,128)S(1)} collective-permute-done((f32[16,4096]{1,0:T(8,128)S(1)}, f32[16,4096]{1,0:T(8,128)S(1)}, u32[]{:S(2)}, u32[]{:S(2)}) %collective-permute-start.3) | collective-permute-done | bytes 262176 | tf_op jit(solution)/shard_map/ppermute | solution.py:23
  69.8 3.3 %all-to-all-start.4 = ((bf16[8,1,2]{2,1,0:T(2,128)(2,1)}), bf16[8,1,2]{2,1,0:T(2,128)(2,1)S(1)}, u32[]{:S(2)}, u32[]{:S(2)}) async-start(bf16[8,1,2]{2,1,0:T(2,128)(2,1)} %convert_element_type.182), calls=%async_computation.4 | async-start | bytes 8192 | tf_op jit(solution)/shard_map/all_to_all | solution.py:127
  73.2 7.9 %fusion.16 = bf16[16,1536]{1,0:T(8,128)(2,1)S(1)} fusion(bf16[16,4096]{1,0:T(8,128)(2,1)S(1)} %get-tuple-element.23, bf16[1,1,1536,4096]{3,2,1,0:T(8,128)(2,1)} %param.14), kind=kOutput, calls=%fused_computation.25 | convolution fusion | flops 201351168 | bytes 12763136 | tf_op jit(solution)/shard_map/dot_general | solution.py:120
  81.7 4.1 %all-to-all-start.3 = ((bf16[8,2,1536]{2,1,0:T(2,128)(2,1)}), bf16[8,2,1536]{2,1,0:T(2,128)(2,1)S(1)}, u32[]{:S(2)}, u32[]{:S(2)}) async-start(bf16[8,2,1536]{2,1,0:T(2,128)(2,1)} %reshape.246), calls=%async_computation.3 | async-start | bytes 98304 | tf_op jit(solution)/shard_map/all_to_all | solution.py:124
  86.0 4.8 %all-to-all-done.3 = bf16[8,2,1536]{2,1,0:T(2,128)(2,1)S(1)} async-done(((bf16[8,2,1536]{2,1,0:T(2,128)(2,1)}), bf16[8,2,1536]{2,1,0:T(2,128)(2,1)S(1)}, u32[]{:S(2)}, u32[]{:S(2)}) %all-to-all-start.3) | async-done | bytes 49184 | tf_op jit(solution)/shard_map/all_to_all | solution.py:124
  103.4 3.8 %all-to-all-start.6 = ((bf16[8,2,1536]{2,1,0:T(2,128)(2,1)}), bf16[8,2,1536]{2,1,0:T(2,128)(2,1)S(1)}, u32[]{:S(2)}, u32[]{:S(2)}) async-start(bf16[8,2,1536]{2,1,0:T(2,128)(2,1)} %bitcast.26), calls=%async_computation.6 | async-start | bytes 98304 | tf_op jit(solution)/shard_map/all_to_all | solution.py:93
  107.5 4.6 %all-to-all-done.6 = bf16[8,2,1536]{2,1,0:T(2,128)(2,1)S(1)} async-done(((bf16[8,2,1536]{2,1,0:T(2,128)(2,1)}), bf16[8,2,1536]{2,1,0:T(2,128)(2,1)S(1)}, u32[]{:S(2)}, u32[]{:S(2)}) %all-to-all-start.6) | async-done | bytes 49184 | tf_op jit(solution)/shard_map/all_to_all | solution.py:93
  112.2 7.9 %fusion.10 = f32[16,4096]{1,0:T(8,128)S(1)} fusion(bf16[16,1536]{1,0:T(8,128)(2,1)S(1)} %reshape.252, bf16[1,1,4096,1536]{3,2,1,0:T(8,128)(2,1)} %param.15), kind=kOutput, calls=%fused_computation.12 | convolution fusion | flops 201326592 | bytes 12894208 | tf_op jit(solution)/shard_map/dot_general | solution.py:100
  120.1 10.2 %fusion.33 = f32[4096,1536]{1,0:T(8,128)} fusion(bf16[16,1536]{1,0:T(8,128)(2,1)S(1)} %reshape.252, f32[16]{0:T(128)S(1)} %reshape.263, f32[16,4096]{1,0:T(8,128)S(1)} %add.99, f32[16,4096]{1,0:T(8,128)S(1)} %collective-permute-done.8), kind=kOutput, calls=%fused_computation.54 | convolution fusion | flops 201785344 | bytes 25739328 | tf_op jit(solution)/shard_map/dot_general | solution.py:117
  130.9 14.4 %fusion.1 = bf16[1,1,4096,1536]{3,2,1,0:T(8,128)(2,1)} fusion(f32[4096,1536]{1,0:T(8,128)} %fusion.33, bf16[16,1536]{1,0:T(8,128)(2,1)S(1)} %reshape.242, f32[16]{0:T(128)S(1)} %reshape.260, f32[16,4096]{1,0:T(8,128)S(1)} %add.89, f32[16,4096]{1,0:T(8,128)S(1)} %collective-permute-done.3), kind=kOutput, calls=%fused_computation.3 | convolution fusion | flops 214368256 | bytes 38322240 | tf_op jit(solution)/shard_map/dot_general | solution.py:117
  145.6 7.9 %fusion.19 = bf16[16,1536]{1,0:T(8,128)(2,1)S(1)} fusion(bf16[16,4096]{1,0:T(8,128)(2,1)S(1)} %get-tuple-element.21, bf16[1,1,1536,4096]{3,2,1,0:T(8,128)(2,1)} %param.14), kind=kOutput, calls=%fused_computation.26 | convolution fusion | flops 201351168 | bytes 12763136 | tf_op jit(solution)/shard_map/dot_general | solution.py:120
  153.5 10.1 %fusion.66 = f32[1536,4096]{1,0:T(8,128)} fusion(bf16[16,1536]{1,0:T(8,128)(2,1)S(1)} %reshape.255, bf16[16,4096]{1,0:T(8,128)(2,1)S(1)} %get-tuple-element.21), kind=kOutput, calls=%fused_computation.112 | convolution fusion | flops 201326592 | bytes 25346048 | tf_op jit(solution)/shard_map/dot_general | solution.py:114
  168.3 14.6 %fusion = bf16[1,1,1536,4096]{3,2,1,0:T(8,128)(2,1)} fusion(f32[1536,4096]{1,0:T(8,128)} %fusion.66, bf16[16,1536]{1,0:T(8,128)(2,1)S(1)} %reshape.245, bf16[16,4096]{1,0:T(8,128)(2,1)S(1)} %get-tuple-element.23), kind=kOutput, calls=%fused_computation.2 | convolution fusion | flops 213909504 | bytes 37928960 | tf_op jit(solution)/shard_map/dot_general | solution.py:114
  182.9 4.1 %all-to-all-start.8 = ((bf16[8,2,1536]{2,1,0:T(2,128)(2,1)}), bf16[8,2,1536]{2,1,0:T(2,128)(2,1)S(1)}, u32[]{:S(2)}, u32[]{:S(2)}) async-start(bf16[8,2,1536]{2,1,0:T(2,128)(2,1)} %reshape.256), calls=%async_computation.8 | async-start | bytes 98304 | tf_op jit(solution)/shard_map/all_to_all | solution.py:124
  188.3 3.7 %all-to-all-done.8 = bf16[8,2,1536]{2,1,0:T(2,128)(2,1)S(1)} async-done(((bf16[8,2,1536]{2,1,0:T(2,128)(2,1)}), bf16[8,2,1536]{2,1,0:T(2,128)(2,1)S(1)}, u32[]{:S(2)}, u32[]{:S(2)}) %all-to-all-start.8) | async-done | bytes 49184 | tf_op jit(solution)/shard_map/all_to_all | solution.py:124
  193.5 52.0 %all-reduce.2.cloned.1.call-done = f32[6144,8]{0,1:T(8,128)} async-done(((f32[6144,8]{0,1:T(8,128)}), f32[6144,8]{0,1:T(8,128)}) %all-reduce.2.cloned.1.call-update) | async-done | bytes 196624 | tf_op jit(solution)/shard_map/psum | solution.py:140
  (106 shorter events, 38.9 us)
Async XLA Ops:
  7.2 12.1 %copy-start = (f32[1,6144,8]{1,2,0:T(8,128)S(1)}, f32[1,6144,8]{1,2,0:T(8,128)}, u32[]{:S(2)}) copy-start(f32[1,6144,8]{1,2,0:T(8,128)} %param.13) | copy-start | bytes 589828
  11.8 10.1 %all-to-all-start.1 = ((bf16[8,2,1536]{2,1,0:T(2,128)(2,1)}), bf16[8,2,1536]{2,1,0:T(2,128)(2,1)S(1)}, u32[]{:S(2)}, u32[]{:S(2)}) async-start(bf16[8,2,1536]{2,1,0:T(2,128)(2,1)} %bitcast.9), calls=%async_computation.1 | async-start | bytes 98304 | tf_op jit(solution)/shard_map/all_to_all | solution.py:93
  22.5 11.7 %all-to-all-start.2 = ((bf16[8,2,1536]{2,1,0:T(2,128)(2,1)}), bf16[8,2,1536]{2,1,0:T(2,128)(2,1)S(1)}, u32[]{:S(2)}, u32[]{:S(2)}) async-start(bf16[8,2,1536]{2,1,0:T(2,128)(2,1)} %bitcast.12), calls=%async_computation.2 | async-start | bytes 98304 | tf_op jit(solution)/shard_map/all_to_all | solution.py:92
  33.8 21.4 %collective-permute-start = (f32[16,4096]{1,0:T(8,128)S(1)}, f32[16,4096]{1,0:T(8,128)S(1)}, u32[]{:S(2)}, u32[]{:S(2)}) collective-permute-start(f32[16,4096]{1,0:T(8,128)S(1)} %fusion.12), channel_id=1, source_target_pairs={{0,4},{4,0},{8,12},{12,8},{16,20},{20,16},{24,28},{28,24},{1,5},{5... | collective-permute-start | bytes 786440 | tf_op jit(solution)/shard_map/ppermute | solution.py:23
  34.9 10.9 %all-to-all-start = ((bf16[8,1,2]{2,1,0:T(2,128)(2,1)}), bf16[8,1,2]{2,1,0:T(2,128)(2,1)S(1)}, u32[]{:S(2)}, u32[]{:S(2)}) async-start(bf16[8,1,2]{2,1,0:T(2,128)(2,1)} %broadcast_in_dim.20), calls=%async_computation | async-start | bytes 8192 | tf_op jit(solution)/shard_map/all_to_all | solution.py:94
  45.1 10.9 %collective-permute-start.2 = (f32[16,4096]{1,0:T(8,128)S(1)}, f32[16,4096]{1,0:T(8,128)S(1)}, u32[]{:S(2)}, u32[]{:S(2)}) collective-permute-start(f32[16,4096]{1,0:T(8,128)S(1)} %fusion.8), channel_id=1, source_target_pairs={{0,4},{4,0},{8,12},{12,8},{16,20},{20,16},{24,28},{28,24},{1,5},{5... | collective-permute-start | bytes 786440 | tf_op jit(solution)/shard_map/ppermute | solution.py:23
  46.5 8.8 %all-to-all-start.7 = ((bf16[8,2,1536]{2,1,0:T(2,128)(2,1)}), bf16[8,2,1536]{2,1,0:T(2,128)(2,1)S(1)}, u32[]{:S(2)}, u32[]{:S(2)}) async-start(bf16[8,2,1536]{2,1,0:T(2,128)(2,1)} %bitcast.28), calls=%async_computation.7 | async-start | bytes 98304 | tf_op jit(solution)/shard_map/all_to_all | solution.py:92
  55.3 9.3 %collective-permute-start.1 = (f32[16,4096]{1,0:T(8,128)S(1)}, f32[16,4096]{1,0:T(8,128)S(1)}, u32[]{:S(2)}, u32[]{:S(2)}) collective-permute-start(f32[16,4096]{1,0:T(8,128)S(1)} %add.87), channel_id=1, source_target_pairs={{0,8},{8,0},{4,12},{12,4},{16,24},{24,16},{20,28},{28,20},{1,9},{9... | collective-permute-start | bytes 786440 | tf_op jit(solution)/shard_map/ppermute | solution.py:23
  56.0 38.8 %copy-start.1 = (bf16[1,6,6144]{2,1,0:T(8,128)(2,1)S(1)}, bf16[1,6,6144]{2,1,0:T(8,128)(2,1)}, u32[]{:S(2)}) copy-start(bf16[1,6,6144]{2,1,0:T(8,128)(2,1)} %param.9) | copy-start | bytes 221188
  56.0 12.9 %collective-permute-start.3 = (f32[16,4096]{1,0:T(8,128)S(1)}, f32[16,4096]{1,0:T(8,128)S(1)}, u32[]{:S(2)}, u32[]{:S(2)}) collective-permute-start(f32[16,4096]{1,0:T(8,128)S(1)} %add.89), channel_id=1, source_target_pairs={{0,8},{8,0},{4,12},{12,4},{16,24},{24,16},{20,28},{28,20},{1,9},{9... | collective-permute-start | bytes 786440 | tf_op jit(solution)/shard_map/ppermute | solution.py:23
  63.9 38.6 %copy-start.2 = (bf16[6,6144]{1,0:T(8,128)(2,1)S(1)}, bf16[6,6144]{1,0:T(8,128)(2,1)}, u32[]{:S(2)}) copy-start(bf16[6,6144]{1,0:T(8,128)(2,1)} %param.10) | copy-start | bytes 221188
  63.9 35.5 %collective-permute-start.7 = (f32[16,4096]{1,0:T(8,128)S(1)}, f32[16,4096]{1,0:T(8,128)S(1)}, u32[]{:S(2)}, u32[]{:S(2)}) collective-permute-start(f32[16,4096]{1,0:T(8,128)S(1)} %fusion.4), channel_id=1, source_target_pairs={{0,4},{4,0},{8,12},{12,8},{16,20},{20,16},{24,28},{28,24},{1,5},{5... | collective-permute-start | bytes 786440 | tf_op jit(solution)/shard_map/ppermute | solution.py:23
  69.8 11.9 %all-to-all-start.4 = ((bf16[8,1,2]{2,1,0:T(2,128)(2,1)}), bf16[8,1,2]{2,1,0:T(2,128)(2,1)S(1)}, u32[]{:S(2)}, u32[]{:S(2)}) async-start(bf16[8,1,2]{2,1,0:T(2,128)(2,1)} %convert_element_type.182), calls=%async_computation.4 | async-start | bytes 8192 | tf_op jit(solution)/shard_map/all_to_all | solution.py:127
  81.7 9.1 %all-to-all-start.3 = ((bf16[8,2,1536]{2,1,0:T(2,128)(2,1)}), bf16[8,2,1536]{2,1,0:T(2,128)(2,1)S(1)}, u32[]{:S(2)}, u32[]{:S(2)}) async-start(bf16[8,2,1536]{2,1,0:T(2,128)(2,1)} %reshape.246), calls=%async_computation.3 | async-start | bytes 98304 | tf_op jit(solution)/shard_map/all_to_all | solution.py:124
  91.4 7.8 %all-to-all-start.5 = ((bf16[8,1,2]{2,1,0:T(2,128)(2,1)}), bf16[8,1,2]{2,1,0:T(2,128)(2,1)S(1)}, u32[]{:S(2)}, u32[]{:S(2)}) async-start(bf16[8,1,2]{2,1,0:T(2,128)(2,1)} %broadcast_in_dim.23), calls=%async_computation.5 | async-start | bytes 8192 | tf_op jit(solution)/shard_map/all_to_all | solution.py:94
  95.5 7.0 %collective-permute-start.4 = (bf16[6,6144]{1,0:T(8,128)(2,1)S(1)}, bf16[6,6144]{1,0:T(8,128)(2,1)S(1)}, u32[]{:S(2)}, u32[]{:S(2)}) collective-permute-start(bf16[6,6144]{1,0:T(8,128)(2,1)S(1)} %fusion.15), channel_id=1, source_target_pairs={{1,0},{2,1},{3,2},{5,4},{6,5},{7,6},{9,8},{10,9},{11,10},{13,12},{... | collective-permute-start | bytes 221192 | tf_op jit(solution)/shard_map/ppermute | solution.py:13
  99.4 20.7 %collective-permute-start.8 = (f32[16,4096]{1,0:T(8,128)S(1)}, f32[16,4096]{1,0:T(8,128)S(1)}, u32[]{:S(2)}, u32[]{:S(2)}) collective-permute-start(f32[16,4096]{1,0:T(8,128)S(1)} %add.99), channel_id=1, source_target_pairs={{0,8},{8,0},{4,12},{12,4},{16,24},{24,16},{20,28},{28,20},{1,9},{9... | collective-permute-start | bytes 786440 | tf_op jit(solution)/shard_map/ppermute | solution.py:23
  103.4 8.8 %all-to-all-start.6 = ((bf16[8,2,1536]{2,1,0:T(2,128)(2,1)}), bf16[8,2,1536]{2,1,0:T(2,128)(2,1)S(1)}, u32[]{:S(2)}, u32[]{:S(2)}) async-start(bf16[8,2,1536]{2,1,0:T(2,128)(2,1)} %bitcast.26), calls=%async_computation.6 | async-start | bytes 98304 | tf_op jit(solution)/shard_map/all_to_all | solution.py:93
  120.1 10.2 %collective-permute-start.5 = (f32[16,4096]{1,0:T(8,128)S(1)}, f32[16,4096]{1,0:T(8,128)S(1)}, u32[]{:S(2)}, u32[]{:S(2)}) collective-permute-start(f32[16,4096]{1,0:T(8,128)S(1)} %fusion.10), channel_id=1, source_target_pairs={{0,4},{4,0},{8,12},{12,8},{16,20},{20,16},{24,28},{28,24},{1,5},{5... | collective-permute-start | bytes 786440 | tf_op jit(solution)/shard_map/ppermute | solution.py:23
  130.3 15.1 %collective-permute-start.6 = (f32[16,4096]{1,0:T(8,128)S(1)}, f32[16,4096]{1,0:T(8,128)S(1)}, u32[]{:S(2)}, u32[]{:S(2)}) collective-permute-start(f32[16,4096]{1,0:T(8,128)S(1)} %add.97), channel_id=1, source_target_pairs={{0,8},{8,0},{4,12},{12,4},{16,24},{24,16},{20,28},{28,20},{1,9},{9... | collective-permute-start | bytes 786440 | tf_op jit(solution)/shard_map/ppermute | solution.py:23
  164.4 18.5 %all-to-all-start.9 = ((bf16[8,1,2]{2,1,0:T(2,128)(2,1)}), bf16[8,1,2]{2,1,0:T(2,128)(2,1)S(1)}, u32[]{:S(2)}, u32[]{:S(2)}) async-start(bf16[8,1,2]{2,1,0:T(2,128)(2,1)} %convert_element_type.183), calls=%async_computation.9 | async-start | bytes 8192 | tf_op jit(solution)/shard_map/all_to_all | solution.py:127
  182.9 9.1 %all-to-all-start.8 = ((bf16[8,2,1536]{2,1,0:T(2,128)(2,1)}), bf16[8,2,1536]{2,1,0:T(2,128)(2,1)S(1)}, u32[]{:S(2)}, u32[]{:S(2)}) async-start(bf16[8,2,1536]{2,1,0:T(2,128)(2,1)} %reshape.256), calls=%async_computation.8 | async-start | bytes 98304 | tf_op jit(solution)/shard_map/all_to_all | solution.py:124
  187.0 58.6 %all-reduce.2.cloned.1.call-start = ((), (), s32[]{:S(2)}) async-start(), calls=%async_computation.10 | async-start | bytes 393216 | tf_op jit(solution)/shard_map/psum | solution.py:140
Sparse Core Ops, SparseCore 0:
  191.5 54.0 all-reduce.1
where the time goes:
time: 255 us; the launch traced here: 254 us
  matrix products  99.2 us (39%)
  waiting for transfers between devices  80.7 us (32%)
  starting transfers between devices  44.2 us (17%)
  between operations  15.7 us (6%)
  local copies, waits for them, and re-layouts  12.8 us (5%)
    psum x1, waiting for transfers between devices, local(): acc_router = acc_router + lax.psum(router_term, 'dp')  52 us
    dot_general x2, matrix products, local(): lax.dot_general(rows_x, dpre, (((0,), (0,)), ((), ())), preferred_element...  24.7 us
    dot_general x2, matrix products, local(): lax.dot_general(scaled, rows_y, (((0,), (0,)), ((), ())), preferred_eleme...  24.6 us
    dot_general x2, matrix products, local(): lax.dot_general(rows_y, weight_out, (((1,), (1,)), ((), ())), preferred_e...  15.8 us
    dot_general x2, matrix products, local(): lax.dot_general(dpre, weight_in, (((1,), (1,)), ((), ())), preferred_elem...  15.8 us
    dot_general x2, matrix products, local(): pre = jnp.dot(rows_x, weight_in, preferred_element_type=jnp.float32)  12.6 us
    all_to_all x2, starting transfers between devices, local(): lax.all_to_all(ysend, 'dp', split_axis=0, concat_axis=0, tiled=True)  9.02 us
    all_to_all x2, waiting for transfers between devices, local(): lax.all_to_all(dx_part.reshape(dev_count, CAP, part), 'dp', split_axis=0,...  8.46 us
  transfers between devices with their start and end apart: 20, of which 10 were waited for; matrix products, arithmetic and copies ran while one was open for 35% of the time, Pallas kernels for 0%

commit v1 on v0

v1 whole, which is shorter than its diff:
```python
import functools

import jax
import jax.numpy as jnp
from jax import lax
from jax.experimental import pallas as pl
from jax.experimental.pallas import tpu as pltpu
from jax.sharding import PartitionSpec as P

STEPS = 2
CAP = 2
QUARTERS = 4
LANES = 128
SLAB = 8
BF = jnp.bfloat16
F32 = jnp.float32
MIB = 1 << 20

NN = (((1,), (0,)), ((), ()))
NT = (((1,), (1,)), ((), ()))
TN = (((0,), (0,)), ((), ()))

VMEM = pl.BlockSpec(memory_space=pltpu.VMEM)
SMEM = pl.BlockSpec(memory_space=pltpu.SMEM)
ANY = pl.BlockSpec(memory_space=pl.ANY)


def dot(a, b, dims=NN):
    return lax.dot_general(a, b, dims, preferred_element_type=F32)


def dot_hi(a, b, dims=NN):
    return lax.dot_general(
        a, b, dims, preferred_element_type=F32, precision=lax.Precision.HIGHEST
    )


def iota(shape, dim):
    return lax.broadcasted_iota(jnp.int32, shape, dim)


def one_hot(cond):
    return jnp.where(cond, 1.0, 0.0).astype(BF)


def sds(shape, dtype):
    return jax.ShapeDtypeStruct(shape, dtype)


def call(body, args, specs, outs, flops=0, data=0, limit=12, scratch=(), out_specs=None):
    many = isinstance(outs, tuple)
    if out_specs is None:
        out_specs = tuple(VMEM for _ in outs) if many else VMEM
    return pl.pallas_call(
        body,
        in_specs=specs,
        out_specs=out_specs,
        out_shape=outs,
        scratch_shapes=scratch,
        cost_estimate=pl.CostEstimate(flops=flops, bytes_accessed=data, transcendentals=0),
        compiler_params=pltpu.CompilerParams(vmem_limit_bytes=limit * MIB),
    )(*args)


def in_vmem(weight):
    return pltpu.with_memory_space_constraint(weight, pltpu.VMEM)


def chunk_of(size, most):
    while size % most:
        most //= 2
    return most


def permuted(array, bit):
    count = lax.axis_size("dp")
    return lax.ppermute(array, "dp", [(i, i ^ (1 << bit)) for i in range(count)])


def from_next_section(array):
    count = lax.axis_size("section")
    return lax.ppermute(array, "section", [(i + 1, i) for i in range(count - 1)])


def slot_tokens(ids, step, live):
    tokens = ids.shape[2]
    count = jnp.int32(0)
    held = [jnp.int32(-1)] * CAP
    for t in range(tokens):
        routed = ((ids[step, 0, t] == 0) | (ids[step, 1, t] == 0)) & live
        for c in range(CAP):
            held[c] = jnp.where(routed & (count == c), jnp.int32(t), held[c])
        count = count + routed.astype(jnp.int32)
    return held


def silu_parts(pre):
    sig = jax.nn.sigmoid(pre)
    return pre * sig, sig * (1.0 + pre * (1.0 - sig))


def softmax_rows(logits, experts):
    lane = iota(logits.shape, 1)
    expo = jnp.where(lane < experts, jnp.exp(logits), 0.0)
    return expo / jnp.sum(expo, axis=1, keepdims=True)


def first_minus(prob):
    lane = iota(prob.shape, 1)
    return jnp.where(lane == 0, 1.0, 0.0) - prob


def local(saved_inputs, carried, head_grad, routing, replica_counts, router, w_in, w_out):
    sections = lax.axis_size("section")
    n = lax.axis_size("dp")
    groups = n // QUARTERS
    width = head_grad.shape[1]
    tokens = head_grad.shape[0]
    part = w_in.shape[2]
    hidden = w_in.shape[3]
    half = hidden // 2
    experts = router.shape[2]
    rows = n * CAP
    w1 = in_vmem(w_in[0, 0])
    w2 = in_vmem(w_out[0, 0])
    router_t = router[0].T
    x_tok = saved_inputs[0].transpose(1, 0, 2)
    carried_tok = carried[0]
    ids = routing[0].transpose(0, 2, 1)
    last_section = sections - 1

    def where_am_i():
        return lax.axis_index("section"), lax.axis_index("dp")

    def quarter_lanes():
        return pl.ds(pl.multiple_of(lax.rem(lax.axis_index("dp"), QUARTERS) * part, LANES), part)

    def half_lanes(core):
        return pl.ds(pl.multiple_of(core * half, LANES), half)

    def pick(held, value):
        row = iota((SLAB, value.shape[0]), 0)
        col = iota((SLAB, value.shape[0]), 1)
        chosen = jnp.zeros((SLAB, value.shape[0]), F32)
        for c in range(len(held)):
            chosen = chosen + jnp.where((row == c) & (col == held[c]), 1.0, 0.0)
        return dot(chosen.astype(BF), value)

    def send_quarters(slab, out_ref):
        for q in range(QUARTERS):
            piece = slab[:, q * part:(q + 1) * part]
            for g in range(groups):
                out_ref[g * QUARTERS + q] = piece

    def dispatch_body(ids_ref, counts_ref, x_ref, dy_ref, out_ref):
        section, dev = where_am_i()
        count = counts_ref[dev]
        held = [slot_tokens(ids_ref, step, step + section < count) for step in range(STEPS)]
        slab = pick([-1] * (STEPS * CAP) + held[0], dy_ref[...])
        row = iota((SLAB, width), 0)
        for step in range(STEPS):
            for c in range(CAP):
                value = x_ref[jnp.maximum(held[step][c], 0), step:step + 1, :].astype(F32)
                wanted = (row == step * CAP + c) & (held[step][c] >= 0)
                slab = jnp.where(wanted, jnp.broadcast_to(value, (SLAB, width)), slab)
        send_quarters(slab.astype(BF), out_ref)

    sent = call(
        dispatch_body,
        (ids, replica_counts, x_tok, carried_tok),
        [SMEM, SMEM, VMEM, VMEM],
        sds((n, SLAB, part), BF),
        data=4 * MIB,
    )
    carried_next = from_next_section(carried_tok)
    ids_next = from_next_section(ids)
    came = lax.all_to_all(sent, "dp", split_axis=0, concat_axis=0, tiled=True)

    wide = half + LANES

    def first_body(came_ref, w1_ref, w2_ref, router_ref, xs_ref, ys_ref, keep_ref, send_ref):
        core = lax.rem(lax.axis_index("dp"), 2)
        flat = came_ref[...].reshape(n * SLAB, part)
        row = iota((STEPS * rows, n * SLAB), 0)
        col = iota((STEPS * rows, n * SLAB), 1)
        slot = row % rows
        want = (slot // CAP) * SLAB + (row // rows) * CAP + slot % CAP
        xs = dot(one_hot(col == want), flat).astype(BF)
        row = iota((rows, n * SLAB), 0)
        col = iota((rows, n * SLAB), 1)
        ys = dot(one_hot(col == (row // CAP) * SLAB + 2 * CAP + row % CAP), flat).astype(BF)
        xs_ref[...] = xs
        ys_ref[...] = ys
        logits = dot_hi(xs.astype(F32), router_ref[:, quarter_lanes()], NT)
        logits = jnp.concatenate(
            [logits, jnp.zeros((STEPS * rows, LANES - experts), F32)], axis=1
        )
        zero = jnp.zeros((rows, LANES), F32)
        both = STEPS * rows
        step = chunk_of(half, 512)
        for ref, which in ((send_ref, 1 - core), (keep_ref, core)):
            for at in range(0, half, step):
                lanes = pl.ds(pl.multiple_of(which * half + at, LANES), step)
                ref[0:both, at:at + step] = dot(xs, w1_ref[:, lanes])
            for at in range(0, half, step):
                lanes = pl.ds(pl.multiple_of(which * half + at, LANES), step)
                ref[both:both + rows, at:at + step] = dot(ys, w2_ref[lanes, :], NT)
            ref[0:both, half:wide] = logits
            ref[both:both + rows, half:wide] = zero

    xs, ys0, keep, send = call(
        first_body,
        (came, w1, w2, router_t),
        [VMEM] * 4,
        (
            sds((STEPS * rows, part), BF),
            sds((rows, part), BF),
            sds((3 * rows, wide), F32),
            sds((3 * rows, wide), F32),
        ),
        flops=2 * 3 * rows * part * hidden,
        data=2 * part * hidden * 2,
    )
    pair = keep + permuted(send, 0)
    mine0 = jnp.concatenate([pair[0:rows], pair[2 * rows:3 * rows]], axis=0)
    mine1 = pair[rows:2 * rows]
    other0 = permuted(mine0, 1)

    def gated(pre, upper, gate):
        act, slope = silu_parts(pre)
        dpre = (gate * upper * slope).astype(BF)
        block = jnp.sum(act * upper, axis=1, keepdims=True)
        return act, dpre, block

    def split_sum(block):
        high = block.astype(BF)
        low = (block - high.astype(F32)).astype(BF)
        lane = iota((rows, LANES), 1)
        zero = jnp.zeros((rows, LANES), BF)
        return jnp.where(lane == 0, high, jnp.where(lane == 1, low, zero))

    def gate_of(prob):
        return prob[:, 0:1].astype(BF).astype(F32)

    def act0_body(a_ref, b_ref, out_ref, prob_ref, block_ref):
        prob = softmax_rows(a_ref[0:rows, half:wide] + b_ref[0:rows, half:wide], experts)
        gate = gate_of(prob)
        pre = a_ref[0:rows, 0:half] + b_ref[0:rows, 0:half]
        upper = a_ref[rows:2 * rows, 0:half] + b_ref[rows:2 * rows, 0:half]
        act, dpre, block = gated(pre, upper, gate)
        out_ref[:, 0:half] = dpre
        out_ref[:, half:wide] = split_sum(block)
        out_ref[:, wide:wide + half] = (gate * act).astype(BF)
        prob_ref[...] = prob
        block_ref[...] = jnp.broadcast_to(block, (rows, LANES))

    hid0, prob0, block0 = call(
        act0_body,
        (mine0, other0),
        [VMEM] * 2,
        (sds((rows, wide + half), BF), sds((rows, LANES), F32), sds((rows, LANES), F32)),
    )
    hid0_pair = permuted(hid0, 0)

    def block_sum(block, pair_ref):
        extra = pair_ref[:, half:half + 1].astype(F32) + pair_ref[:, half + 1:half + 2].astype(F32)
        return (block[:, 0:1] + extra).astype(BF)

    def in_order(own, pair, core):
        return (
            jnp.where(core == 0, own, pair),
            jnp.where(core == 0, pair, own),
        )

    def dx_of(own_ref, pair_ref, w1_ref, core):
        low, high = in_order(own_ref[:, 0:half], pair_ref[:, 0:half], core)
        step = chunk_of(part, 256)
        pieces = []
        for at in range(0, part, step):
            pieces.append(
                dot(low, w1_ref[at:at + step, 0:half], NT)
                + dot(high, w1_ref[at:at + step, half:hidden], NT)
            )
        return jnp.concatenate(pieces, axis=1)

    def dx0_body(own_ref, pair_ref, block_ref, w1_ref, out_ref):
        core = lax.rem(lax.axis_index("dp"), 2)
        out_ref[:, 0:part] = dx_of(own_ref, pair_ref, w1_ref, core).astype(BF)
        dgate = block_sum(block_ref[...], pair_ref)
        lane = iota((rows, LANES), 1)
        out_ref[:, part:part + LANES] = jnp.where(
            lane == 0, jnp.broadcast_to(dgate, (rows, LANES)), jnp.zeros((rows, LANES), BF)
        )

    dx0 = call(
        dx0_body,
        (hid0, hid0_pair, block0, w1),
        [VMEM] * 4,
        sds((rows, part + LANES), BF),
        flops=2 * rows * part * hidden,
        data=2 * part * hidden,
    )
    total0, bit = dx0, 2
    while (1 << (bit + 1)) < n:
        total0 = total0.astype(F32) + permuted(total0, bit).astype(F32)
        bit += 1
    other_total0 = permuted(total0, bit) if groups > 1 else jnp.zeros_like(total0)

    def sum0_body(a_ref, b_ref, prob_ref, router_ref, out_ref, dlog_ref):
        total = a_ref[...].astype(F32) + b_ref[...].astype(F32)
        prob = prob_ref[...]
        dlog = total[:, part:part + 1] * prob[:, 0:1] * first_minus(prob)
        dlog_ref[...] = dlog
        back = dot_hi(dlog[:, 0:experts], router_ref[:, quarter_lanes()])
        out_ref[...] = (total[:, 0:part] + back).astype(BF)

    dxs0, dlog0 = call(
        sum0_body,
        (total0, other_total0, prob0, router_t),
        [VMEM] * 4,
        (sds((rows, part), BF), sds((rows, LANES), F32)),
    )
    dxs_next = from_next_section(dxs0)

    def base_body(ids_ref, next_ref, counts_ref, dy_ref, head_ref, out_ref):
        section, dev = where_am_i()
        live = 1 + section < counts_ref[dev]
        last = section == last_section
        held = slot_tokens(ids_ref, 1, live)
        before = slot_tokens(next_ref, 0, live & jnp.logical_not(last))
        slab = pick(held, jnp.where(last, head_ref[...], dy_ref[...]))
        row = iota((SLAB, width), 0)
        lane = lax.rem(iota((SLAB, width), 1), part)
        for c in range(CAP):
            for b in range(CAP):
                same = (held[c] >= 0) & (held[c] == before[b])
                slab = jnp.where((row == CAP + c) & (lane == b) & same, 1.0, slab)
        send_quarters(slab.astype(BF), out_ref)

    base_sent = call(
        base_body,
        (ids, ids_next, replica_counts, carried_next, head_grad),
        [SMEM, SMEM, SMEM, VMEM, VMEM],
        sds((n, SLAB, part), BF),
        data=4 * MIB,
    )
    base = lax.all_to_all(base_sent, "dp", split_axis=0, concat_axis=0, tiled=True)
    other1 = permuted(mine1, 1)

    def up1_body(base_ref, dxs_ref, w2_ref, ys_ref, keep_ref, send_ref):
        core = lax.rem(lax.axis_index("dp"), 2)
        flat = base_ref[...].reshape(n * SLAB, part)
        row = iota((rows, n * SLAB), 0)
        col = iota((rows, n * SLAB), 1)
        want = (row // CAP) * SLAB + row % CAP
        value = dot(one_hot(col == want), flat)
        match = dot(one_hot(col == want + CAP), flat[:, 0:LANES])
        row = iota((rows, rows), 0)
        col = iota((rows, rows), 1)
        place = jnp.zeros((rows, rows), F32)
        for b in range(CAP):
            place = place + jnp.where(
                (row // CAP == col // CAP) & (col % CAP == b), match[:, b:b + 1], 0.0
            )
        ys = (value + dot(place.astype(BF), dxs_ref[...])).astype(BF)
        ys_ref[...] = ys
        step = chunk_of(half, 512)
        for ref, which in ((send_ref, 1 - core), (keep_ref, core)):
            for at in range(0, half, step):
                lanes = pl.ds(pl.multiple_of(which * half + at, LANES), step)
                ref[:, at:at + step] = dot(ys, w2_ref[lanes, :], NT)

    ys1, keep1, send1 = call(
        up1_body,
        (base, dxs_next, w2),
        [VMEM] * 3,
        (sds((rows, part), BF), sds((rows, half), F32), sds((rows, half), F32)),
        flops=2 * rows * part * hidden,
        data=2 * part * hidden,
    )
    up1 = keep1 + permuted(send1, 0)
    other_up1 = permuted(up1, 1)

    def act1_body(a_ref, b_ref, out_ref, prob_ref):
        prob = softmax_rows(a_ref[:, half:wide] + b_ref[:, half:wide], experts)
        act, _ = silu_parts(a_ref[:, 0:half] + b_ref[:, 0:half])
        out_ref[...] = (gate_of(prob) * act).astype(BF)
        prob_ref[...] = prob

    scaled1, prob1 = call(
        act1_body,
        (mine1, other1),
        [VMEM] * 2,
        (sds((rows, half), BF), sds((rows, LANES), F32)),
    )
    scaled1_pair = permuted(scaled1, 0)

    both = STEPS * rows

    def outer(body, args, height, across, flops):
        return call(
            body,
            args,
            [VMEM] * len(args),
            sds((height, across), BF),
            flops=flops,
            data=2 * height * across,
            limit=22,
            out_specs=ANY,
            scratch=[
                pltpu.VMEM((height, across), BF),
                pltpu.SemaphoreType.DMA((SLAB,)),
            ],
        )

    def write_out(a, b, out_ref, held_ref, sems):
        height = held_ref.shape[0]
        step = height // SLAB
        copies = []
        for i in range(SLAB):
            at = pl.ds(i * step, step)
            held_ref[i * step:(i + 1) * step, :] = dot(
                a[:, i * step:(i + 1) * step], b, TN
            ).astype(BF)
            copy = pltpu.make_async_copy(held_ref.at[at], out_ref.at[at], sems.at[i])
            copy.start()
            copies.append(copy)
        for copy in copies:
            copy.wait()

    def grad_out_body(own0, pair0, own1, pair1, ys0_ref, ys1_ref, out_ref, held_ref, sems):
        core = lax.rem(lax.axis_index("dp"), 2)
        a0, b0 = in_order(own0[:, wide:wide + half], pair0[:, wide:wide + half], core)
        a1, b1 = in_order(own1[...], pair1[...], core)
        scaled = jnp.concatenate(
            [jnp.concatenate([a0, b0], axis=1), jnp.concatenate([a1, b1], axis=1)], axis=0
        )
        ys = jnp.concatenate([ys0_ref[...], ys1_ref[...]], axis=0)
        write_out(scaled, ys, out_ref, held_ref, sems)

    grad_out = outer(
        grad_out_body,
        (hid0, hid0_pair, scaled1, scaled1_pair, ys0, ys1),
        hidden,
        part,
        2 * both * part * hidden,
    )

    def act2_body(a_ref, b_ref, up_ref, other_ref, prob_ref, out_ref, block_ref):
        pre = a_ref[:, 0:half] + b_ref[:, 0:half]
        upper = up_ref[...] + other_ref[...]
        _, dpre, block = gated(pre, upper, gate_of(prob_ref[...]))
        out_ref[:, 0:half] = dpre
        out_ref[:, half:wide] = split_sum(block)
        block_ref[...] = jnp.broadcast_to(block, (rows, LANES))

    hid1, block1 = call(
        act2_body,
        (mine1, other1, up1, other_up1, prob1),
        [VMEM] * 5,
        (sds((rows, wide), BF), sds((rows, LANES), F32)),
    )
    hid1_pair = permuted(hid1, 0)

    back_rows = 2 * SLAB

    def dx1_body(
        own_ref, pair_ref, block_ref, prob_ref, dlog0_ref, xs_ref, dxs0_ref, next_ref, router_ref, w1_ref, out_ref
    ):
        dev = lax.axis_index("dp")
        core = lax.rem(dev, 2)
        group = dev // QUARTERS
        dx = dx_of(own_ref, pair_ref, w1_ref, core)
        prob = prob_ref[...]
        dgate = block_sum(block_ref[...], pair_ref).astype(F32)
        dlog = dgate * prob[:, 0:1] * first_minus(prob)
        dx = (dx + dot_hi(dlog[:, 0:experts], router_ref[:, quarter_lanes()])).astype(BF)
        aux = jnp.where(group == 0, dxs0_ref[...], next_ref[...])
        dlogs = jnp.concatenate(
            [jnp.where(group == 0, dlog0_ref[...], 0.0), dlog], axis=0
        )
        grad = dot_hi(dlogs, xs_ref[...].astype(F32), TN)[0:experts, :].astype(BF)
        source = jnp.concatenate([dx, aux, grad], axis=0)
        count = 2 * rows + experts
        row = iota((n * back_rows, count), 0)
        col = iota((n * back_rows, count), 1)
        home = row // back_rows
        kind = row % back_rows
        want = jnp.where(
            kind < 2 * CAP,
            (kind // CAP) * rows + home * CAP + kind % CAP,
            jnp.where(kind >= SLAB, 2 * rows + kind - SLAB, -1),
        )
        out_ref[...] = dot(one_hot(col == want), source).astype(BF).reshape(n, back_rows, part)

    back_sent = call(
        dx1_body,
        (hid1, hid1_pair, block1, prob1, dlog0, xs, dxs0, dxs_next, router_t, w1),
        [VMEM] * 10,
        sds((n, back_rows, part), BF),
        flops=2 * rows * part * hidden,
        data=2 * part * hidden,
        limit=16,
    )
    back = lax.all_to_all(back_sent, "dp", split_axis=0, concat_axis=0, tiled=True)

    def grad_in_body(own0, pair0, own1, pair1, xs_ref, out_ref, held_ref, sems):
        core = lax.rem(lax.axis_index("dp"), 2)
        a0, b0 = in_order(own0[:, 0:half], pair0[:, 0:half], core)
        a1, b1 = in_order(own1[:, 0:half], pair1[:, 0:half], core)
        dpre = jnp.concatenate(
            [jnp.concatenate([a0, b0], axis=1), jnp.concatenate([a1, b1], axis=1)], axis=0
        )
        write_out(xs_ref[...], dpre, out_ref, held_ref, sems)

    grad_in = outer(
        grad_in_body,
        (hid0, hid0_pair, hid1, hid1_pair, xs),
        part,
        hidden,
        2 * both * part * hidden,
    )

    def final_body(
        ids_ref, next_ids_ref, counts_ref, back_ref, dy_ref, dy_next_ref, head_ref, out_ref, router_out_ref
    ):
        section, dev = where_am_i()
        count = counts_ref[dev]
        last = section == last_section
        live0 = section < count
        live1 = 1 + section < count
        held0 = slot_tokens(ids_ref, 0, live0)
        held1 = slot_tokens(ids_ref, 1, live1)
        before = slot_tokens(next_ids_ref, 0, live1 & jnp.logical_not(last))
        wide_dy = jnp.where(live0, dy_ref[...].astype(F32), 0.0)
        dy1 = jnp.where(last, head_ref[...].astype(F32), dy_next_ref[...].astype(F32))
        wide_dy1 = jnp.where(live1, dy1, 0.0)

        def put(held, at, value):
            row = iota((tokens, 2 * SLAB), 0)
            col = iota((tokens, 2 * SLAB), 1)
            place = jnp.zeros((tokens, 2 * SLAB), F32)
            for c in range(CAP):
                place = place + jnp.where((row == held[c]) & (col == at + c), 1.0, 0.0)
            return dot(place.astype(BF), value)

        for q in range(QUARTERS):
            lanes = slice(q * part, (q + 1) * part)
            blocks = [back_ref[g * QUARTERS + q] for g in range(groups)]
            grad = blocks[0][SLAB:SLAB + experts].astype(F32)
            for block in blocks[1:]:
                grad = grad + block[SLAB:SLAB + experts].astype(F32)
            router_out_ref[:, lanes] = grad
            out0 = wide_dy[:, lanes] + put(held0, CAP, blocks[0])
            out1 = wide_dy1[:, lanes]
            if groups > 1:
                out1 = out1 + put(before, CAP, blocks[1])
            out1 = out1.astype(BF).astype(F32)
            for block in blocks:
                out1 = out1 + put(held1, 0, block)
            out0 = out0.astype(BF)
            out1 = out1.astype(BF)
            for t in range(tokens):
                out_ref[t, 0:1, lanes] = out0[t:t + 1]
                out_ref[t, 1:2, lanes] = out1[t:t + 1]

    grads, router_grad = call(
        final_body,
        (ids, ids_next, replica_counts, back, carried_tok, carried_next, head_grad),
        [SMEM, SMEM, SMEM, VMEM, VMEM, VMEM, VMEM],
        (sds((tokens, STEPS, width), BF), sds((experts, width), F32)),
        limit=24,
    )
    input_grad = grads.transpose(1, 0, 2)[:, None]
    return (input_grad, grad_in[None, None], grad_out[None, None], router_grad.T[None])


def solution(mesh):
    in_specs = (
        P("section", None, "dp", None),
        P("section", "dp", None),
        P("dp", None),
        P("section", None, "dp", None),
        P(),
        P("section", None, None),
        P("section", "dp", None, None),
        P("section", "dp", None, None),
    )
    out_specs = (
        P(None, "section", "dp", None),
        P("section", "dp", None, None),
        P("section", "dp", None, None),
        P("section", None, None),
    )
    return jax.shard_map(local, mesh=mesh, in_specs=in_specs, out_specs=out_specs, check_vma=False)
```

time: 255 us -> 119 us (0.47)
  matrix products: 99.2 us -> 0 us
  waiting for transfers between devices: 80.7 us -> 29.3 us
  Pallas kernels: 0 us -> 32.5 us
  starting transfers between devices: 44.2 us -> 17.7 us
  between operations: 15.7 us -> 0.83 us
  local copies, waits for them, and re-layouts: 12.8 us -> 27 us
  blocking collectives: 0 us -> 11.2 us
    dot_general x26 -> x0, matrix products: 99.2 us -> none  [the longest x2 24.7 us: local(): lax.dot_general(rows_x, dpre, (((0,), (0,)), ((), ())), preferred_element...]
    psum x1 -> x0, waiting for transfers between devices: 52 us -> none  [local(): acc_router = acc_router + lax.psum(router_term, 'dp')]
    pallas_call x0 -> x13, Pallas kernels: none -> 32.5 us  [call(): pl.pallas_call(body, in_specs=specs, out_specs=out_specs, out_shape=outs,...]
    all_to_all x10 -> x2, starting transfers between devices: 38.3 us -> 7.34 us  [the longest x1 3.95 us: local(): lax.all_to_all(back_sent, 'dp', split_axis=0, concat_axis=0, tiled=True)]
    unnamed x8 -> x30, local copies, waits for them, and re-layouts: 2.45 us -> 27 us
    ppermute x9 -> x12, waiting for transfers between devices: 7.56 us -> 29.3 us  [the longest x9 19.8 us: permuted(): return lax.ppermute(array, 'dp', [(i, i ^ 1 << bit) for i in range(count)])]
    all_to_all x10 -> x2, waiting for transfers between devices: 21.1 us -> 0.01 us  [the longest x1 0.01 us: local(): lax.all_to_all(base_sent, 'dp', split_axis=0, concat_axis=0, tiled=True)]
    all_to_all x0 -> x1, blocking collectives: none -> 11.2 us  [local(): came = lax.all_to_all(sent, 'dp', split_axis=0, concat_axis=0, tiled=True)]
  transfers between devices with their start and end apart: 20 -> 14, of which waited for: 10 -> 9; matrix products, arithmetic and copies ran while one was open for 35% -> 0% of each run, Pallas kernels for 0% -> 13%
where the time goes in v1:
time: 119 us
  Pallas kernels  32.5 us (27%)
  waiting for transfers between devices  29.3 us (25%)
  local copies, waits for them, and re-layouts  27 us (23%)
  starting transfers between devices  17.7 us (15%)
  blocking collectives  11.2 us (9%)
    pallas_call x13, Pallas kernels, call(): pl.pallas_call(body, in_specs=specs, out_specs=out_specs, out_shape=outs,...  32.5 us
    unnamed x30, local copies, waits for them, and re-layouts  27 us
    ppermute x9, waiting for transfers between devices, permuted(): return lax.ppermute(array, 'dp', [(i, i ^ 1 << bit) for i in range(count)])  19.8 us
    all_to_all x1, blocking collectives, local(): came = lax.all_to_all(sent, 'dp', split_axis=0, concat_axis=0, tiled=True)  11.2 us
    ppermute x3, waiting for transfers between devices, from_next_section(): lax.ppermute(array, 'section', [(i + 1, i) for i in range(count - 1)])  9.49 us
    ppermute x9, starting transfers between devices, permuted(): return lax.ppermute(array, 'dp', [(i, i ^ 1 << bit) for i in range(count)])  6.53 us
    all_to_all x1, starting transfers between devices, local(): lax.all_to_all(back_sent, 'dp', split_axis=0, concat_axis=0, tiled=True)  3.95 us
    ppermute x3, starting transfers between devices, from_next_section(): lax.ppermute(array, 'section', [(i + 1, i) for i in range(count - 1)])  3.88 us
  transfers between devices with their start and end apart: 14, of which 9 were waited for; matrix products, arithmetic and copies ran while one was open for 0% of the time, Pallas kernels for 13%

profile of v1, /device:TPU:0, one launch (start us, length us, event | category | flops | bytes accessed | tf_op | source)
XLA Modules:
  0.0 118.7 jit_solution(8649973630778931176)
XLA Ops:
  4.6 11.2 %all_to_all.15.came_ref = bf16[8,8,1536]{2,1,0:T(8,128)(2,1)S(1)} all-to-all(bf16[8,8,1536]{2,1,0:T(8,128)(2,1)S(1)} %shard_map.111), channel_id=1, replica_groups=mesh['dp'=8,'section'=4] {'dp'}, dimensions={0} | all-to-all | bytes 393216 | tf_op jit(solution)/shard_map/all_to_all | solution.py:177
  15.8 4.6 %copy-done = bf16[1,1,1536,4096]{3,2,1,0:T(8,128)(2,1)S(1)} copy-done((bf16[1,1,1536,4096]{3,2,1,0:T(8,128)(2,1)S(1)}, bf16[1,1,1536,4096]{3,2,1,0:T(8,128)(2,1)}, u32[]{:S(2)}) %copy-start) | copy-done | bytes 12582936
  20.3 4.6 %copy-done.3 = bf16[1,1,4096,1536]{3,2,1,0:T(8,128)(2,1)S(1)} copy-done((bf16[1,1,4096,1536]{3,2,1,0:T(8,128)(2,1)S(1)}, bf16[1,1,4096,1536]{3,2,1,0:T(8,128)(2,1)}, u32[]{:S(2)}) %copy-start.3) | copy-done | bytes 12582936
  25.9 5.3 %shard_map.112 = (bf16[32,1536]{1,0:T(8,128)(2,1)S(1)}, bf16[16,1536]{1,0:T(8,128)(2,1)S(1)}, f32[48,2176]{1,0:T(8,128)S(1)}, f32[48,2176]{1,0:T(8,128)S(1)}) custom-call(bf16[8,8,1536]{2,1,0:T(8,128)(2,1)S(1)} %all_to_all.15.came_ref, bf16[1536,4096]{1,0:T(8,128)(2,1)S(1)} %bitcast.20, bf16[4096,1536]{1,0:T(8,128)(2,1)S(1)} %bitcast.23, f32[8,6144]{1,0:T(8,128)S(1)} %bitcast.25), custom_call_target="tpu_custom_call" | custom-call | flops 603979776 | bytes 25165824 | tf_op jit(solution)/shard_map/pallas_call | solution.py:54
  31.2 1.8 %collective-permute-done.1 = f32[48,2176]{1,0:T(8,128)S(1)} collective-permute-done((f32[48,2176]{1,0:T(8,128)S(1)}, f32[48,2176]{1,0:T(8,128)S(1)}, u32[]{:S(2)}, u32[]{:S(2)}) %collective-permute-start.1) | collective-permute-done | bytes 417824 | tf_op jit(solution)/shard_map/ppermute | solution.py:77
  33.7 8.1 %collective-permute-done.4.b_ref = f32[32,2176]{1,0:T(8,128)S(1)} collective-permute-done((f32[32,2176]{1,0:T(8,128)S(1)}, f32[32,2176]{1,0:T(8,128)S(1)}, u32[]{:S(2)}, u32[]{:S(2)}) %collective-permute-start.4) | collective-permute-done | bytes 278560 | tf_op jit(solution)/shard_map/ppermute | solution.py:77
  44.7 4.8 %collective-permute-done.next_ref.next_ids_ref = s32[2,2,6]{2,1,0:T(2,128)S(1)} collective-permute-done((s32[2,2,6]{2,1,0:T(2,128)S(1)}, s32[2,2,6]{2,1,0:T(2,128)S(1)}, u32[]{:S(2)}, u32[]{:S(2)}) %collective-permute-start) | collective-permute-done | bytes 128 | tf_op jit(solution)/shard_map/ppermute | solution.py:82
  51.1 3.4 %all-to-all-start.1 = ((bf16[8,8,1536]{2,1,0:T(8,128)(2,1)}), bf16[8,8,1536]{2,1,0:T(8,128)(2,1)S(1)}, u32[]{:S(2)}, u32[]{:S(2)}) async-start(bf16[8,8,1536]{2,1,0:T(8,128)(2,1)} %shard_map.113), calls=%async_computation.1 | async-start | bytes 393216 | tf_op jit(solution)/shard_map/all_to_all | solution.py:347
  54.5 4.6 %copy-done.1 = bf16[1,1,1536,4096]{3,2,1,0:T(8,128)(2,1)S(1)} copy-done((bf16[1,1,1536,4096]{3,2,1,0:T(8,128)(2,1)S(1)}, bf16[1,1,1536,4096]{3,2,1,0:T(8,128)(2,1)}, u32[]{:S(2)}) %copy-start.1) | copy-done | bytes 12582936
  59.1 3.3 %shard_map.115.a_ref = bf16[16,1664]{1,0:T(8,128)(2,1)S(1)} custom-call(bf16[16,4224]{1,0:T(8,128)(2,1)S(1)} %get-tuple-element.24.own_ref.own0, bf16[16,4224]{1,0:T(8,128)(2,1)S(1)} %collective-permute-done.5.pair_ref.pair0, f32[16,128]{1,0:T(8,128)S(1)} %get-tuple-element.25.block_ref, bf16[1536,4096]{1,0:T(8,128)(2,1)S(1)} %bitcast.21), custom_call_target="tpu_custom_call" | custom-call | flops 201326592 | bytes 12582912 | tf_op jit(solution)/shard_map/pallas_call | solution.py:54
  62.4 1.9 %collective-permute-start.6 = (bf16[16,1664]{1,0:T(8,128)(2,1)S(1)}, bf16[16,1664]{1,0:T(8,128)(2,1)S(1)}, u32[]{:S(2)}, u32[]{:S(2)}) collective-permute-start(bf16[16,1664]{1,0:T(8,128)(2,1)S(1)} %shard_map.115.a_ref), channel_id=1, source_target_pairs={{0,16},{4,20},{8,24},{12,28},{16,0},{20,4},{24,8},{28,12},{1,17},{... | collective-permute-start | bytes 159752 | tf_op jit(solution)/shard_map/ppermute | solution.py:77
  64.4 2.2 %collective-permute-done.6.b_ref = bf16[16,1664]{1,0:T(8,128)(2,1)S(1)} collective-permute-done((bf16[16,1664]{1,0:T(8,128)(2,1)S(1)}, bf16[16,1664]{1,0:T(8,128)(2,1)S(1)}, u32[]{:S(2)}, u32[]{:S(2)}) %collective-permute-start.6) | collective-permute-done | bytes 53280 | tf_op jit(solution)/shard_map/ppermute | solution.py:77
  68.2 4.7 %collective-permute-done.7.dxs_ref.next_ref = bf16[16,1536]{1,0:T(8,128)(2,1)S(1)} collective-permute-done((bf16[16,1536]{1,0:T(8,128)(2,1)S(1)}, bf16[16,1536]{1,0:T(8,128)(2,1)S(1)}, u32[]{:S(2)}, u32[]{:S(2)}) %collective-permute-start.7) | collective-permute-done | bytes 49184 | tf_op jit(solution)/shard_map/ppermute | solution.py:82
  72.9 4.6 %copy-done.4 = bf16[1,1,4096,1536]{3,2,1,0:T(8,128)(2,1)S(1)} copy-done((bf16[1,1,4096,1536]{3,2,1,0:T(8,128)(2,1)S(1)}, bf16[1,1,4096,1536]{3,2,1,0:T(8,128)(2,1)}, u32[]{:S(2)}) %copy-start.4) | copy-done | bytes 12582936
  77.5 3.6 %shard_map.117 = (bf16[16,1536]{1,0:T(8,128)(2,1)S(1)}, f32[16,2048]{1,0:T(8,128)S(1)}, f32[16,2048]{1,0:T(8,128)S(1)}) custom-call(bf16[8,8,1536]{2,1,0:T(8,128)(2,1)S(1)} %all-to-all-done.1.base_ref, bf16[16,1536]{1,0:T(8,128)(2,1)S(1)} %collective-permute-done.7.dxs_ref.next_ref, bf16[4096,1536]{1,0:T(8,128)(2,1)S(1)} %bitcast.24), custom_call_target="tpu_custom_call" | custom-call | flops 201326592 | bytes 12582912 | tf_op jit(solution)/shard_map/pallas_call | solution.py:54
  81.1 1.9 %collective-permute-start.2 = (f32[16,2176]{1,0:T(8,128)S(1)}, f32[16,2176]{1,0:T(8,128)S(1)}, u32[]{:S(2)}, u32[]{:S(2)}) collective-permute-start(f32[16,2176]{1,0:T(8,128)S(1)} %get-tuple-element.42.a_ref), channel_id=1, source_target_pairs={{0,8},{4,12},{8,0},{12,4},{16,24},{20,28},{24,16},{28,20},{1,9},{5... | collective-permute-start | bytes 417800 | tf_op jit(solution)/shard_map/ppermute | solution.py:77
  84.4 3.2 %collective-permute-done.2.b_ref = f32[16,2176]{1,0:T(8,128)S(1)} collective-permute-done((f32[16,2176]{1,0:T(8,128)S(1)}, f32[16,2176]{1,0:T(8,128)S(1)}, u32[]{:S(2)}, u32[]{:S(2)}) %collective-permute-start.2) | collective-permute-done | bytes 139296 | tf_op jit(solution)/shard_map/ppermute | solution.py:77
  87.8 2.4 %collective-permute-done.9.other_ref = f32[16,2048]{1,0:T(8,128)S(1)} collective-permute-done((f32[16,2048]{1,0:T(8,128)S(1)}, f32[16,2048]{1,0:T(8,128)S(1)}, u32[]{:S(2)}, u32[]{:S(2)}) %collective-permute-start.9) | collective-permute-done | bytes 131104 | tf_op jit(solution)/shard_map/ppermute | solution.py:77
  91.6 4.6 %copy-done.2 = bf16[1,1,1536,4096]{3,2,1,0:T(8,128)(2,1)S(1)} copy-done((bf16[1,1,1536,4096]{3,2,1,0:T(8,128)(2,1)S(1)}, bf16[1,1,1536,4096]{3,2,1,0:T(8,128)(2,1)}, u32[]{:S(2)}) %copy-start.2) | copy-done | bytes 12582936
  96.2 5.0 %shard_map.120 = bf16[8,16,1536]{2,1,0:T(8,128)(2,1)} custom-call(bf16[16,2176]{1,0:T(8,128)(2,1)S(1)} %get-tuple-element.31.own_ref.own1, bf16[16,2176]{1,0:T(8,128)(2,1)S(1)} %collective-permute-done.10.pair_ref.pair1, f32[16,128]{1,0:T(8,128)S(1)} %get-tuple-element.32.block_ref, f32[16,128]{1,0:T(8,128)S(1)} %get-tuple-element.30.prob_ref, ...), custom_call_target="tpu_custom_call" | custom-call | flops 201326592 | bytes 12582912 | tf_op jit(solution)/shard_map/pallas_call | solution.py:54
  101.1 3.9 %all-to-all-start.2 = ((bf16[8,16,1536]{2,1,0:T(8,128)(2,1)}), bf16[8,16,1536]{2,1,0:T(8,128)(2,1)S(1)}, u32[]{:S(2)}, u32[]{:S(2)}) async-start(bf16[8,16,1536]{2,1,0:T(8,128)(2,1)} %shard_map.120), calls=%async_computation.2 | async-start | bytes 786432 | tf_op jit(solution)/shard_map/all_to_all | solution.py:505
  106.5 5.3 %shard_map.123 = bf16[4096,1536]{1,0:T(8,128)(2,1)} custom-call(bf16[16,4224]{1,0:T(8,128)(2,1)S(1)} %get-tuple-element.24.own_ref.own0, bf16[16,4224]{1,0:T(8,128)(2,1)S(1)} %collective-permute-done.5.pair_ref.pair0, bf16[16,2048]{1,0:T(8,128)(2,1)S(1)} %get-tuple-element.36.own1, bf16[16,2048]{1,0:T(8,128)(2,1)S(1)} %collective-permute-done.11.pair1, ...), custom_call_target="tpu_custom_call" | custom-call | flops 402653184 | bytes 12582912 | tf_op jit(solution)/shard_map/pallas_call | solution.py:54
  111.8 5.3 %shard_map.122 = bf16[1536,4096]{1,0:T(8,128)(2,1)} custom-call(bf16[16,4224]{1,0:T(8,128)(2,1)S(1)} %get-tuple-element.24.own_ref.own0, bf16[16,4224]{1,0:T(8,128)(2,1)S(1)} %collective-permute-done.5.pair_ref.pair0, bf16[16,2176]{1,0:T(8,128)(2,1)S(1)} %get-tuple-element.31.own_ref.own1, bf16[16,2176]{1,0:T(8,128)(2,1)S(1)} %collective-permute-done.10.pair_ref.pair1, ...), custom_call_target="tpu_custom_call" | custom-call | flops 402653184 | bytes 12582912 | tf_op jit(solution)/shard_map/pallas_call | solution.py:54
  117.0 1.7 %shard_map.121 = (bf16[6,2,6144]{2,1,0:T(2,128)(2,1)}, f32[8,6144]{1,0:T(8,128)}) custom-call(s32[2,2,6]{2,1,0:T(2,128)S(1)} %bitcast.35, s32[2,2,6]{2,1,0:T(2,128)S(1)} %collective-permute-done.next_ref.next_ids_ref, s32[8]{0:T(128)S(1)} %copy-done.14, bf16[8,16,1536]{2,1,0:T(8,128)(2,1)S(1)} %all-to-all-done.2.back_ref, bf16[6,6144]{1,0:T(8,128)(2,1)S(1)} %bitcast.30, ...), custom_call_target="tpu_custom_call" | custom-call | tf_op jit(solution)/shard_map/pallas_call | solution.py:54
  (52 shorter events, 16.0 us)
Async XLA Ops:
  15.8 4.6 %copy-start = (bf16[1,1,1536,4096]{3,2,1,0:T(8,128)(2,1)S(1)}, bf16[1,1,1536,4096]{3,2,1,0:T(8,128)(2,1)}, u32[]{:S(2)}) copy-start(bf16[1,1,1536,4096]{3,2,1,0:T(8,128)(2,1)} %param.14) | copy-start | bytes 37748740
  20.3 4.6 %copy-start.3 = (bf16[1,1,4096,1536]{3,2,1,0:T(8,128)(2,1)S(1)}, bf16[1,1,4096,1536]{3,2,1,0:T(8,128)(2,1)}, u32[]{:S(2)}) copy-start(bf16[1,1,4096,1536]{3,2,1,0:T(8,128)(2,1)} %param.15) | copy-start | bytes 37748740
  25.8 16.2 %copy-start.8 = (bf16[1,6,6144]{2,1,0:T(8,128)(2,1)S(1)}, bf16[1,6,6144]{2,1,0:T(8,128)(2,1)}, u32[]{:S(2)}) copy-start(bf16[1,6,6144]{2,1,0:T(8,128)(2,1)} %param.9) | copy-start | bytes 221188
  25.9 17.5 %copy-start.12 = (s32[1,2,6,2]{2,3,1,0:T(2,128)S(1)}, s32[1,2,6,2]{2,3,1,0:T(2,128)}, u32[]{:S(2)}) copy-start(s32[1,2,6,2]{2,3,1,0:T(2,128)} %param.11) | copy-start | bytes 292
  25.9 23.7 %copy-start.9 = (bf16[6,6144]{1,0:T(8,128)(2,1)S(1)}, bf16[6,6144]{1,0:T(8,128)(2,1)}, u32[]{:S(2)}) copy-start(bf16[6,6144]{1,0:T(8,128)(2,1)} %head_ref.3) | copy-start | bytes 221188
  25.9 23.7 %copy-start.14 = (s32[8]{0:T(128)S(1)}, s32[8]{0:T(128)}, u32[]{:S(2)}) copy-start(s32[8]{0:T(128)} %counts_ref.5) | copy-start | bytes 100
  31.1 35.5 %copy-start.6 = (f32[1,6144,8]{1,2,0:T(8,128)S(1)}, f32[1,6144,8]{1,2,0:T(8,128)}, u32[]{:S(2)}) copy-start(f32[1,6144,8]{1,2,0:T(8,128)} %param.13) | copy-start | bytes 589828
  31.1 1.8 %collective-permute-start.1 = (f32[48,2176]{1,0:T(8,128)S(1)}, f32[48,2176]{1,0:T(8,128)S(1)}, u32[]{:S(2)}, u32[]{:S(2)}) collective-permute-start(f32[48,2176]{1,0:T(8,128)S(1)} %get-tuple-element.23), channel_id=1, source_target_pairs={{0,4},{4,0},{8,12},{12,8},{16,20},{20,16},{24,28},{28,24},{1,5},{5... | collective-permute-start | bytes 1253384 | tf_op jit(solution)/shard_map/ppermute | solution.py:77
  33.0 8.8 %collective-permute-start.4 = (f32[32,2176]{1,0:T(8,128)S(1)}, f32[32,2176]{1,0:T(8,128)S(1)}, u32[]{:S(2)}, u32[]{:S(2)}) collective-permute-start(f32[32,2176]{1,0:T(8,128)S(1)} %pad_maximum_fusion.a_ref), channel_id=1, source_target_pairs={{0,8},{4,12},{8,0},{12,4},{16,24},{20,28},{24,16},{28,20},{1,9},{5... | collective-permute-start | bytes 835592 | tf_op jit(solution)/shard_map/ppermute | solution.py:77
  42.0 12.5 %collective-permute-start.5 = (bf16[16,4224]{1,0:T(8,128)(2,1)S(1)}, bf16[16,4224]{1,0:T(8,128)(2,1)S(1)}, u32[]{:S(2)}, u32[]{:S(2)}) collective-permute-start(bf16[16,4224]{1,0:T(8,128)(2,1)S(1)} %get-tuple-element.24.own_ref.own0), channel_id=1, source_target_pairs={{0,4},{4,0},{8,12},{12,8},{16,20},{20,16},{24,28},{28,24},{1,5},{5... | collective-permute-start | bytes 405512 | tf_op jit(solution)/shard_map/ppermute | solution.py:77
  42.1 7.4 %collective-permute-start.3 = (bf16[6,6144]{1,0:T(8,128)(2,1)S(1)}, bf16[6,6144]{1,0:T(8,128)(2,1)S(1)}, u32[]{:S(2)}, u32[]{:S(2)}) collective-permute-start(bf16[6,6144]{1,0:T(8,128)(2,1)S(1)} %bitcast.29), channel_id=1, source_target_pairs={{1,0},{2,1},{3,2},{5,4},{6,5},{7,6},{9,8},{10,9},{11,10},{13,12},{... | collective-permute-start | bytes 221192 | tf_op jit(solution)/shard_map/ppermute | solution.py:82
  43.4 6.1 %collective-permute-start = (s32[2,2,6]{2,1,0:T(2,128)S(1)}, s32[2,2,6]{2,1,0:T(2,128)S(1)}, u32[]{:S(2)}, u32[]{:S(2)}) collective-permute-start(s32[2,2,6]{2,1,0:T(2,128)S(1)} %bitcast.33), channel_id=1, source_target_pairs={{1,0},{2,1},{3,2},{5,4},{6,5},{7,6},{9,8},{10,9},{11,10},{13,12},{... | collective-permute-start | bytes 296 | tf_op jit(solution)/shard_map/ppermute | solution.py:82
  51.1 17.1 %all-to-all-start.1 = ((bf16[8,8,1536]{2,1,0:T(8,128)(2,1)}), bf16[8,8,1536]{2,1,0:T(8,128)(2,1)S(1)}, u32[]{:S(2)}, u32[]{:S(2)}) async-start(bf16[8,8,1536]{2,1,0:T(8,128)(2,1)} %shard_map.113), calls=%async_computation.1 | async-start | bytes 393216 | tf_op jit(solution)/shard_map/all_to_all | solution.py:347
  54.5 4.6 %copy-start.1 = (bf16[1,1,1536,4096]{3,2,1,0:T(8,128)(2,1)S(1)}, bf16[1,1,1536,4096]{3,2,1,0:T(8,128)(2,1)}, u32[]{:S(2)}) copy-start(bf16[1,1,1536,4096]{3,2,1,0:T(8,128)(2,1)} %param.14) | copy-start | bytes 37748740
  62.4 4.2 %collective-permute-start.6 = (bf16[16,1664]{1,0:T(8,128)(2,1)S(1)}, bf16[16,1664]{1,0:T(8,128)(2,1)S(1)}, u32[]{:S(2)}, u32[]{:S(2)}) collective-permute-start(bf16[16,1664]{1,0:T(8,128)(2,1)S(1)} %shard_map.115.a_ref), channel_id=1, source_target_pairs={{0,16},{4,20},{8,24},{12,28},{16,0},{20,4},{24,8},{28,12},{1,17},{... | collective-permute-start | bytes 159752 | tf_op jit(solution)/shard_map/ppermute | solution.py:77
  66.9 6.0 %collective-permute-start.7 = (bf16[16,1536]{1,0:T(8,128)(2,1)S(1)}, bf16[16,1536]{1,0:T(8,128)(2,1)S(1)}, u32[]{:S(2)}, u32[]{:S(2)}) collective-permute-start(bf16[16,1536]{1,0:T(8,128)(2,1)S(1)} %get-tuple-element.27.dxs0_ref), channel_id=1, source_target_pairs={{1,0},{2,1},{3,2},{5,4},{6,5},{7,6},{9,8},{10,9},{11,10},{13,12},{... | collective-permute-start | bytes 147464 | tf_op jit(solution)/shard_map/ppermute | solution.py:82
  72.9 4.6 %copy-start.4 = (bf16[1,1,4096,1536]{3,2,1,0:T(8,128)(2,1)S(1)}, bf16[1,1,4096,1536]{3,2,1,0:T(8,128)(2,1)}, u32[]{:S(2)}) copy-start(bf16[1,1,4096,1536]{3,2,1,0:T(8,128)(2,1)} %param.15) | copy-start | bytes 37748740
  81.1 1.9 %collective-permute-start.8 = (f32[16,2048]{1,0:T(8,128)S(1)}, f32[16,2048]{1,0:T(8,128)S(1)}, u32[]{:S(2)}, u32[]{:S(2)}) collective-permute-start(f32[16,2048]{1,0:T(8,128)S(1)} %get-tuple-element.29), channel_id=1, source_target_pairs={{0,4},{4,0},{8,12},{12,8},{16,20},{20,16},{24,28},{28,24},{1,5},{5... | collective-permute-start | bytes 393224 | tf_op jit(solution)/shard_map/ppermute | solution.py:77
  81.1 6.5 %collective-permute-start.2 = (f32[16,2176]{1,0:T(8,128)S(1)}, f32[16,2176]{1,0:T(8,128)S(1)}, u32[]{:S(2)}, u32[]{:S(2)}) collective-permute-start(f32[16,2176]{1,0:T(8,128)S(1)} %get-tuple-element.42.a_ref), channel_id=1, source_target_pairs={{0,8},{4,12},{8,0},{12,4},{16,24},{20,28},{24,16},{28,20},{1,9},{5... | collective-permute-start | bytes 417800 | tf_op jit(solution)/shard_map/ppermute | solution.py:77
  83.0 7.1 %collective-permute-start.9 = (f32[16,2048]{1,0:T(8,128)S(1)}, f32[16,2048]{1,0:T(8,128)S(1)}, u32[]{:S(2)}, u32[]{:S(2)}) collective-permute-start(f32[16,2048]{1,0:T(8,128)S(1)} %add.7.up_ref), channel_id=1, source_target_pairs={{0,8},{4,12},{8,0},{12,4},{16,24},{20,28},{24,16},{28,20},{1,9},{5... | collective-permute-start | bytes 393224 | tf_op jit(solution)/shard_map/ppermute | solution.py:77
  90.3 1.3 %collective-permute-start.10 = (bf16[16,2176]{1,0:T(8,128)(2,1)S(1)}, bf16[16,2176]{1,0:T(8,128)(2,1)S(1)}, u32[]{:S(2)}, u32[]{:S(2)}) collective-permute-start(bf16[16,2176]{1,0:T(8,128)(2,1)S(1)} %get-tuple-element.31.own_ref.own1), channel_id=1, source_target_pairs={{0,4},{4,0},{8,12},{12,8},{16,20},{20,16},{24,28},{28,24},{1,5},{5... | collective-permute-start | bytes 208904 | tf_op jit(solution)/shard_map/ppermute | solution.py:77
  91.6 4.6 %copy-start.2 = (bf16[1,1,1536,4096]{3,2,1,0:T(8,128)(2,1)S(1)}, bf16[1,1,1536,4096]{3,2,1,0:T(8,128)(2,1)}, u32[]{:S(2)}) copy-start(bf16[1,1,1536,4096]{3,2,1,0:T(8,128)(2,1)} %param.14) | copy-start | bytes 37748740
  101.1 15.9 %all-to-all-start.2 = ((bf16[8,16,1536]{2,1,0:T(8,128)(2,1)}), bf16[8,16,1536]{2,1,0:T(8,128)(2,1)S(1)}, u32[]{:S(2)}, u32[]{:S(2)}) async-start(bf16[8,16,1536]{2,1,0:T(8,128)(2,1)} %shard_map.120), calls=%async_computation.2 | async-start | bytes 786432 | tf_op jit(solution)/shard_map/all_to_all | solution.py:505
  105.1 1.4 %collective-permute-start.11 = (bf16[16,2048]{1,0:T(8,128)(2,1)S(1)}, bf16[16,2048]{1,0:T(8,128)(2,1)S(1)}, u32[]{:S(2)}, u32[]{:S(2)}) collective-permute-start(bf16[16,2048]{1,0:T(8,128)(2,1)S(1)} %get-tuple-element.36.own1), channel_id=1, source_target_pairs={{0,4},{4,0},{8,12},{12,8},{16,20},{20,16},{24,28},{28,24},{1,5},{5... | collective-permute-start | bytes 196616 | tf_op jit(solution)/shard_map/ppermute | solution.py:77
  (5 other events, 4.1 us)

commit v2 on v1

--- a/solution.py
+++ b/solution.py
@@ -62,8 +62,40 @@
     )(*args)
 
 
-def in_vmem(weight):
-    return pltpu.with_memory_space_constraint(weight, pltpu.VMEM)
+def in_hbm(array):
+    return pltpu.with_memory_space_constraint(array, pltpu.HBM)
+
+
+def copy_all(pairs, sems):
+    copies = [
+        pltpu.make_async_copy(source, target, sems.at[i])
+        for i, (source, target) in enumerate(pairs)
+    ]
+    for copy in copies:
+        copy.start()
+    return copies
+
+
+def wait_all(copies):
+    for copy in copies:
+        copy.wait()
+
+
+def fetch(weight):
+    def body(source, target, sem):
+        copy = pltpu.make_async_copy(source, target, sem)
+        copy.start()
+        copy.wait()
+
+    return call(
+        body,
+        (in_hbm(weight),),
+        [ANY],
+        pltpu.VMEM(weight.shape, weight.dtype),
+        data=2 * weight.size,
+        limit=4,
+        scratch=[pltpu.SemaphoreType.DMA],
+    )
 
 
 def chunk_of(size, most):
@@ -72,9 +104,13 @@
     return most
 
 
+def exchanged(array, mask):
+    count = lax.axis_size("dp")
+    return lax.ppermute(array, "dp", [(i, i ^ mask) for i in range(count)])
+
+
 def permuted(array, bit):
-    count = lax.axis_size("dp")
-    return lax.ppermute(array, "dp", [(i, i ^ (1 << bit)) for i in range(count)])
+    return exchanged(array, 1 << bit)
 
 
 def from_next_section(array):
@@ -121,13 +157,12 @@
     half = hidden // 2
     experts = router.shape[2]
     rows = n * CAP
-    w1 = in_vmem(w_in[0, 0])
-    w2 = in_vmem(w_out[0, 0])
     router_t = router[0].T
     x_tok = saved_inputs[0].transpose(1, 0, 2)
     carried_tok = carried[0]
     ids = routing[0].transpose(0, 2, 1)
     last_section = sections - 1
+    w1 = fetch(w_in[0, 0])
 
     def where_am_i():
         return lax.axis_index("section"), lax.axis_index("dp")
@@ -146,85 +181,210 @@
             chosen = chosen + jnp.where((row == c) & (col == held[c]), 1.0, 0.0)
         return dot(chosen.astype(BF), value)
 
-    def send_quarters(slab, out_ref):
-        for q in range(QUARTERS):
-            piece = slab[:, q * part:(q + 1) * part]
-            for g in range(groups):
-                out_ref[g * QUARTERS + q] = piece
-
-    def dispatch_body(ids_ref, counts_ref, x_ref, dy_ref, out_ref):
+    by_chip = n == 2 * QUARTERS
+
+    def place_of(home):
+        return jnp.bitwise_xor(home, lax.axis_index("dp")) if by_chip else home
+
+    def send_quarters(slab_ref, slab, mine_ref, theirs_ref):
+        slab_ref[...] = slab
+        own = lax.rem(lax.axis_index("dp"), QUARTERS)
+        for i in range(QUARTERS):
+            at = pl.multiple_of(jnp.bitwise_xor(own, i) * part, LANES)
+            ref = theirs_ref if i % 2 else mine_ref
+            ref[i // 2] = slab_ref[:, pl.ds(at, part)].astype(BF)
+
+    send_shapes = (sds((2, SLAB, part), BF), sds((2, SLAB, part), BF))
+    slab_scratch = pltpu.VMEM((SLAB, width), F32)
+
+    def spread(mine, theirs):
+        if not by_chip:
+            own = lax.rem(lax.axis_index("dp"), QUARTERS)
+            quads = jnp.stack([mine[0], theirs[0], mine[1], theirs[1]])
+            block = quads[jnp.bitwise_xor(jnp.arange(n) % QUARTERS, own)]
+            return (lax.all_to_all(block, "dp", split_axis=0, concat_axis=0, tiled=True),)
+        handed = permuted(theirs, 0)
+        same = jnp.stack([mine[0], handed[0]])
+        cross = jnp.stack([mine[1], handed[1]])
+        return (same, exchanged(cross, 2), exchanged(same, 4), exchanged(cross, 6))
+
+    def joined(refs):
+        return jnp.concatenate([ref[...].reshape(-1, part) for ref in refs], axis=0)
+
+    def dispatch_body(
+        ids_hbm,
+        counts_hbm,
+        x_hbm,
+        dy_hbm,
+        mine_ref,
+        theirs_ref,
+        onward_ref,
+        ids_ref,
+        counts_ref,
+        x_ref,
+        dy_ref,
+        slab_ref,
+        sems,
+    ):
+        wait_all(
+            copy_all(
+                ((ids_hbm, ids_ref), (counts_hbm, counts_ref), (dy_hbm, dy_ref), (x_hbm, x_ref)),
+                sems,
+            )
+        )
         section, dev = where_am_i()
         count = counts_ref[dev]
         held = [slot_tokens(ids_ref, step, step + section < count) for step in range(STEPS)]
-        slab = pick([-1] * (STEPS * CAP) + held[0], dy_ref[...])
+        dy = dy_ref[...]
+        slab = pick([-1] * (STEPS * CAP) + held[0], dy)
         row = iota((SLAB, width), 0)
+        lane = lax.rem(iota((SLAB, width), 1), part)
         for step in range(STEPS):
             for c in range(CAP):
                 value = x_ref[jnp.maximum(held[step][c], 0), step:step + 1, :].astype(F32)
                 wanted = (row == step * CAP + c) & (held[step][c] >= 0)
                 slab = jnp.where(wanted, jnp.broadcast_to(value, (SLAB, width)), slab)
-        send_quarters(slab.astype(BF), out_ref)
-
-    sent = call(
+        send_quarters(slab_ref, slab, mine_ref, theirs_ref)
+        onward = pick(list(range(tokens)), dy)
+        for c in range(CAP):
+            code = (held[0][c] + 1).astype(F32)
+            onward = jnp.where((row == tokens) & (lane == c), code, onward)
+        onward_ref[...] = onward.astype(BF)
+
+    mine, theirs, onward = call(
         dispatch_body,
-        (ids, replica_counts, x_tok, carried_tok),
-        [SMEM, SMEM, VMEM, VMEM],
-        sds((n, SLAB, part), BF),
+        (in_hbm(ids), in_hbm(replica_counts), in_hbm(x_tok), in_hbm(carried_tok)),
+        [ANY] * 4,
+        (*send_shapes, sds((SLAB, width), BF)),
         data=4 * MIB,
-    )
-    carried_next = from_next_section(carried_tok)
-    ids_next = from_next_section(ids)
-    came = lax.all_to_all(sent, "dp", split_axis=0, concat_axis=0, tiled=True)
+        scratch=[
+            pltpu.SMEM(ids.shape, jnp.int32),
+            pltpu.SMEM(replica_counts.shape, jnp.int32),
+            pltpu.VMEM(x_tok.shape, BF),
+            pltpu.VMEM(carried_tok.shape, BF),
+            slab_scratch,
+            pltpu.SemaphoreType.DMA((4,)),
+        ],
+    )
+    onward = from_next_section(onward)
+    came = spread(mine, theirs)
+
+    came, onward = lax.optimization_barrier((came, onward))
 
     wide = half + LANES
 
-    def first_body(came_ref, w1_ref, w2_ref, router_ref, xs_ref, ys_ref, keep_ref, send_ref):
+    def first_body(*refs):
+        w1_ref, w2_hbm, router_hbm, xs_ref, ys_ref, keep_ref, send_ref, w2_ref, router_ref, sems = refs[
+            len(came):
+        ]
         core = lax.rem(lax.axis_index("dp"), 2)
-        flat = came_ref[...].reshape(n * SLAB, part)
+        step = chunk_of(half, 512)
+        router_copy = pltpu.make_async_copy(
+            router_hbm.at[:, quarter_lanes()], router_ref, sems.at[0]
+        )
+        router_copy.start()
+        chunks = [
+            (ref, at, pl.multiple_of(which * half + at, LANES))
+            for ref, which in ((send_ref, 1 - core), (keep_ref, core))
+            for at in range(0, half, step)
+        ]
+        copies = copy_all(
+            [(w2_hbm.at[pl.ds(lane, step)], w2_ref.at[pl.ds(lane, step)]) for _, _, lane in chunks],
+            sems.at[pl.ds(1, len(chunks))],
+        )
+        flat = joined(refs[:len(came)])
         row = iota((STEPS * rows, n * SLAB), 0)
         col = iota((STEPS * rows, n * SLAB), 1)
         slot = row % rows
-        want = (slot // CAP) * SLAB + (row // rows) * CAP + slot % CAP
+        want = place_of(slot // CAP) * SLAB + (row // rows) * CAP + slot % CAP
         xs = dot(one_hot(col == want), flat).astype(BF)
         row = iota((rows, n * SLAB), 0)
         col = iota((rows, n * SLAB), 1)
-        ys = dot(one_hot(col == (row // CAP) * SLAB + 2 * CAP + row % CAP), flat).astype(BF)
+        ys = dot(one_hot(col == place_of(row // CAP) * SLAB + 2 * CAP + row % CAP), flat).astype(BF)
         xs_ref[...] = xs
         ys_ref[...] = ys
-        logits = dot_hi(xs.astype(F32), router_ref[:, quarter_lanes()], NT)
+        router_copy.wait()
+        logits = dot_hi(xs.astype(F32), router_ref[...], NT)
         logits = jnp.concatenate(
             [logits, jnp.zeros((STEPS * rows, LANES - experts), F32)], axis=1
         )
         zero = jnp.zeros((rows, LANES), F32)
         both = STEPS * rows
-        step = chunk_of(half, 512)
-        for ref, which in ((send_ref, 1 - core), (keep_ref, core)):
-            for at in range(0, half, step):
-                lanes = pl.ds(pl.multiple_of(which * half + at, LANES), step)
-                ref[0:both, at:at + step] = dot(xs, w1_ref[:, lanes])
-            for at in range(0, half, step):
-                lanes = pl.ds(pl.multiple_of(which * half + at, LANES), step)
-                ref[both:both + rows, at:at + step] = dot(ys, w2_ref[lanes, :], NT)
+        for ref, at, lane in chunks:
+            ref[0:both, at:at + step] = dot(xs, w1_ref[:, pl.ds(lane, step)])
+        for ref in (send_ref, keep_ref):
             ref[0:both, half:wide] = logits
             ref[both:both + rows, half:wide] = zero
-
-    xs, ys0, keep, send = call(
+        for (ref, at, lane), copy in zip(chunks, copies):
+            copy.wait()
+            ref[both:both + rows, at:at + step] = dot(ys, w2_ref[pl.ds(lane, step), :], NT)
+
+    xs, ys0, keep, send, w2, router_q = call(
         first_body,
-        (came, w1, w2, router_t),
-        [VMEM] * 4,
+        (*came, w1, in_hbm(w_out[0, 0]), in_hbm(router_t)),
+        [VMEM] * (len(came) + 1) + [ANY] * 2,
         (
             sds((STEPS * rows, part), BF),
             sds((rows, part), BF),
             sds((3 * rows, wide), F32),
             sds((3 * rows, wide), F32),
+            pltpu.VMEM((hidden, part), BF),
+            sds((experts, part), F32),
         ),
         flops=2 * 3 * rows * part * hidden,
         data=2 * part * hidden * 2,
+        scratch=[pltpu.SemaphoreType.DMA((1 + 2 * (half // chunk_of(half, 512)),))],
     )
     pair = keep + permuted(send, 0)
     mine0 = jnp.concatenate([pair[0:rows], pair[2 * rows:3 * rows]], axis=0)
     mine1 = pair[rows:2 * rows]
     other0 = permuted(mine0, 1)
+
+    def base_body(
+        ids_hbm,
+        counts_hbm,
+        onward_ref,
+        head_hbm,
+        mine_ref,
+        theirs_ref,
+        ids_ref,
+        counts_ref,
+        head_ref,
+        slab_ref,
+        sems,
+    ):
+        wait_all(
+            copy_all(((ids_hbm, ids_ref), (counts_hbm, counts_ref), (head_hbm, head_ref)), sems)
+        )
+        section, dev = where_am_i()
+        live = 1 + section < counts_ref[dev]
+        last = section == last_section
+        held = slot_tokens(ids_ref, 1, live)
+        onward = onward_ref[...]
+        slab = pick(held, jnp.where(last, head_ref[...], onward[0:tokens]))
+        row = iota((SLAB, width), 0)
+        code = jnp.broadcast_to(onward[tokens:tokens + 1].astype(F32), (SLAB, width))
+        for c in range(CAP):
+            same = (held[c] >= 0) & (code == (held[c] + 1).astype(F32))
+            slab = jnp.where((row == CAP + c) & same, 1.0, slab)
+        send_quarters(slab_ref, slab, mine_ref, theirs_ref)
+
+    base_sent = call(
+        base_body,
+        (in_hbm(ids), in_hbm(replica_counts), onward, in_hbm(head_grad)),
+        [ANY, ANY, VMEM, ANY],
+        send_shapes,
+        data=4 * MIB,
+        scratch=[
+            pltpu.SMEM(ids.shape, jnp.int32),
+            pltpu.SMEM(replica_counts.shape, jnp.int32),
+            pltpu.VMEM(head_grad.shape, BF),
+            slab_scratch,
+            pltpu.SemaphoreType.DMA((3,)),
+        ],
+    )
+    base = spread(*base_sent)
+    other0, base = lax.optimization_barrier((other0, base))
 
     def gated(pre, upper, gate):
         act, slope = silu_parts(pre)
@@ -311,48 +471,27 @@
         prob = prob_ref[...]
         dlog = total[:, part:part + 1] * prob[:, 0:1] * first_minus(prob)
         dlog_ref[...] = dlog
-        back = dot_hi(dlog[:, 0:experts], router_ref[:, quarter_lanes()])
+        back = dot_hi(dlog[:, 0:experts], router_ref[...])
         out_ref[...] = (total[:, 0:part] + back).astype(BF)
 
     dxs0, dlog0 = call(
         sum0_body,
-        (total0, other_total0, prob0, router_t),
+        (total0, other_total0, prob0, router_q),
         [VMEM] * 4,
         (sds((rows, part), BF), sds((rows, LANES), F32)),
     )
     dxs_next = from_next_section(dxs0)
-
-    def base_body(ids_ref, next_ref, counts_ref, dy_ref, head_ref, out_ref):
-        section, dev = where_am_i()
-        live = 1 + section < counts_ref[dev]
-        last = section == last_section
-        held = slot_tokens(ids_ref, 1, live)
-        before = slot_tokens(next_ref, 0, live & jnp.logical_not(last))
-        slab = pick(held, jnp.where(last, head_ref[...], dy_ref[...]))
-        row = iota((SLAB, width), 0)
-        lane = lax.rem(iota((SLAB, width), 1), part)
-        for c in range(CAP):
-            for b in range(CAP):
-                same = (held[c] >= 0) & (held[c] == before[b])
-                slab = jnp.where((row == CAP + c) & (lane == b) & same, 1.0, slab)
-        send_quarters(slab.astype(BF), out_ref)
-
-    base_sent = call(
-        base_body,
-        (ids, ids_next, replica_counts, carried_next, head_grad),
-        [SMEM, SMEM, SMEM, VMEM, VMEM],
-        sds((n, SLAB, part), BF),
-        data=4 * MIB,
-    )
-    base = lax.all_to_all(base_sent, "dp", split_axis=0, concat_axis=0, tiled=True)
     other1 = permuted(mine1, 1)
-
-    def up1_body(base_ref, dxs_ref, w2_ref, ys_ref, keep_ref, send_ref):
+    dxs_next, other1 = lax.optimization_barrier((dxs_next, other1))
+
+
+    def up1_body(*refs):
+        dxs_ref, w2_ref, ys_ref, keep_ref, send_ref = refs[len(base):]
         core = lax.rem(lax.axis_index("dp"), 2)
-        flat = base_ref[...].reshape(n * SLAB, part)
+        flat = joined(refs[:len(base)])
         row = iota((rows, n * SLAB), 0)
         col = iota((rows, n * SLAB), 1)
-        want = (row // CAP) * SLAB + row % CAP
+        want = place_of(row // CAP) * SLAB + row % CAP
         value = dot(one_hot(col == want), flat)
         match = dot(one_hot(col == want + CAP), flat[:, 0:LANES])
         row = iota((rows, rows), 0)
@@ -372,8 +511,8 @@
 
     ys1, keep1, send1 = call(
         up1_body,
-        (base, dxs_next, w2),
-        [VMEM] * 3,
+        (*base, dxs_next, w2),
+        [VMEM] * (len(base) + 2),
         (sds((rows, part), BF), sds((rows, half), F32), sds((rows, half), F32)),
         flops=2 * rows * part * hidden,
         data=2 * part * hidden,
@@ -446,6 +585,8 @@
         2 * both * part * hidden,
     )
 
+    other_up1, grad_out = lax.optimization_barrier((other_up1, grad_out))
+
     def act2_body(a_ref, b_ref, up_ref, other_ref, prob_ref, out_ref, block_ref):
         pre = a_ref[:, 0:half] + b_ref[:, 0:half]
         upper = up_ref[...] + other_ref[...]
@@ -474,7 +615,7 @@
         prob = prob_ref[...]
         dgate = block_sum(block_ref[...], pair_ref).astype(F32)
         dlog = dgate * prob[:, 0:1] * first_minus(prob)
-        dx = (dx + dot_hi(dlog[:, 0:experts], router_ref[:, quarter_lanes()])).astype(BF)
+        dx = (dx + dot_hi(dlog[:, 0:experts], router_ref[...])).astype(BF)
         aux = jnp.where(group == 0, dxs0_ref[...], next_ref[...])
         dlogs = jnp.concatenate(
             [jnp.where(group == 0, dlog0_ref[...], 0.0), dlog], axis=0
@@ -495,7 +636,7 @@
 
     back_sent = call(
         dx1_body,
-        (hid1, hid1_pair, block1, prob1, dlog0, xs, dxs0, dxs_next, router_t, w1),
+        (hid1, hid1_pair, block1, prob1, dlog0, xs, dxs0, dxs_next, router_q, w1),
         [VMEM] * 10,
         sds((n, back_rows, part), BF),
         flops=2 * rows * part * hidden,
@@ -522,7 +663,7 @@
     )
 
     def final_body(
-        ids_ref, next_ids_ref, counts_ref, back_ref, dy_ref, dy_next_ref, head_ref, out_ref, router_out_ref
+        ids_ref, counts_ref, back_ref, dy_ref, onward_ref, head_ref, out_ref, router_out_ref
     ):
         section, dev = where_am_i()
         count = counts_ref[dev]
@@ -531,9 +672,10 @@
         live1 = 1 + section < count
         held0 = slot_tokens(ids_ref, 0, live0)
         held1 = slot_tokens(ids_ref, 1, live1)
-        before = slot_tokens(next_ids_ref, 0, live1 & jnp.logical_not(last))
+        onward = onward_ref[...].astype(F32)
+        before = [onward[tokens:tokens + 1, c:c + 1] - 1.0 for c in range(CAP)]
         wide_dy = jnp.where(live0, dy_ref[...].astype(F32), 0.0)
-        dy1 = jnp.where(last, head_ref[...].astype(F32), dy_next_ref[...].astype(F32))
+        dy1 = jnp.where(last, head_ref[...].astype(F32), onward[0:tokens])
         wide_dy1 = jnp.where(live1, dy1, 0.0)
 
         def put(held, at, value):
@@ -541,7 +683,8 @@
             col = iota((tokens, 2 * SLAB), 1)
             place = jnp.zeros((tokens, 2 * SLAB), F32)
             for c in range(CAP):
-                place = place + jnp.where((row == held[c]) & (col == at + c), 1.0, 0.0)
+                mine = row.astype(F32) == held[c].astype(F32)
+                place = place + jnp.where(mine & (col == at + c), 1.0, 0.0)
             return dot(place.astype(BF), value)
 
         for q in range(QUARTERS):
@@ -566,8 +709,8 @@
 
     grads, router_grad = call(
         final_body,
-        (ids, ids_next, replica_counts, back, carried_tok, carried_next, head_grad),
-        [SMEM, SMEM, SMEM, VMEM, VMEM, VMEM, VMEM],
+        (ids, replica_counts, back, carried_tok, onward, head_grad),
+        [SMEM, SMEM, VMEM, VMEM, VMEM, VMEM],
         (sds((tokens, STEPS, width), BF), sds((experts, width), F32)),
         limit=24,
     )

time: 119 us -> 84.6 us (0.71)
  local copies, waits for them, and re-layouts: 27 us -> 0.06 us
  blocking collectives: 11.2 us -> 0 us
  Pallas kernels: 32.5 us -> 39.1 us
  waiting for transfers between devices: 29.3 us -> 23.7 us
  starting transfers between devices: 17.7 us -> 20.5 us
    unnamed x30 -> x8, local copies, waits for them, and re-layouts: 27 us -> 0.01 us
    all_to_all x1 -> x0, blocking collectives: 11.2 us -> none  [local(): came = lax.all_to_all(sent, 'dp', split_axis=0, concat_axis=0, tiled=True)]
    ppermute x9 -> x17, starting transfers between devices: 6.53 us -> 14.2 us  [exchanged(): return lax.ppermute(array, 'dp', [(i, i ^ mask) for i in range(count)])]
    pallas_call x13 -> x14, Pallas kernels: 32.5 us -> 39.1 us  [call(): pl.pallas_call(body, in_specs=specs, out_specs=out_specs, out_shape=outs,...]
    ppermute x3 -> x2, waiting for transfers between devices: 9.49 us -> 5.12 us  [from_next_section(): lax.ppermute(array, 'section', [(i + 1, i) for i in range(count - 1)])]
    ppermute x9 -> x17, waiting for transfers between devices: 19.8 us -> 15.6 us  [exchanged(): return lax.ppermute(array, 'dp', [(i, i ^ mask) for i in range(count)])]
    all_to_all x1 -> x0, starting transfers between devices: 3.39 us -> none  [local(): lax.all_to_all(base_sent, 'dp', split_axis=0, concat_axis=0, tiled=True)]
    all_to_all x1, waiting for transfers between devices: 0.01 us -> 3.01 us  [local(): lax.all_to_all(back_sent, 'dp', split_axis=0, concat_axis=0, tiled=True)]
  transfers between devices with their start and end apart: 14 -> 20, of which waited for: 9 -> 10; matrix products, arithmetic and copies ran while one was open for 0% -> 0% of each run, Pallas kernels for 13% -> 24%
where the time goes in v2:
time: 84.6 us; the launch traced here: 84.3 us
  Pallas kernels  39.1 us (46%)
  waiting for transfers between devices  23.7 us (28%)
  starting transfers between devices  20.5 us (24%)
  between operations  0.86 us (1%)
    pallas_call x14, Pallas kernels, call(): pl.pallas_call(body, in_specs=specs, out_specs=out_specs, out_shape=outs,...  39.1 us
    ppermute x17, waiting for transfers between devices, exchanged(): return lax.ppermute(array, 'dp', [(i, i ^ mask) for i in range(count)])  15.6 us
    ppermute x17, starting transfers between devices, exchanged(): return lax.ppermute(array, 'dp', [(i, i ^ mask) for i in range(count)])  14.2 us
    ppermute x2, waiting for transfers between devices, from_next_section(): lax.ppermute(array, 'section', [(i + 1, i) for i in range(count - 1)])  5.12 us
    all_to_all x1, starting transfers between devices, local(): lax.all_to_all(back_sent, 'dp', split_axis=0, concat_axis=0, tiled=True)  3.45 us
    all_to_all x1, waiting for transfers between devices, local(): lax.all_to_all(back_sent, 'dp', split_axis=0, concat_axis=0, tiled=True)  3.01 us
    ppermute x2, starting transfers between devices, from_next_section(): lax.ppermute(array, 'section', [(i + 1, i) for i in range(count - 1)])  2.75 us
  transfers between devices with their start and end apart: 20, of which 10 were waited for; matrix products, arithmetic and copies ran while one was open for 0% of the time, Pallas kernels for 24%

profile of v2, /device:TPU:0, one launch (start us, length us, event | category | flops | bytes accessed | tf_op | source)
XLA Modules:
  0.0 84.3 jit_solution(10618073276929725333)
XLA Ops:
  0.6 1.3 %shard_map.111 = (bf16[2,8,1536]{2,1,0:T(8,128)(2,1)S(1)}, bf16[2,8,1536]{2,1,0:T(8,128)(2,1)S(1)}, bf16[8,6144]{1,0:T(8,128)(2,1)S(1)}) custom-call(s32[2,2,6]{2,1,0:T(2,128)} %bitcast.22, s32[8]{0:T(128)} %counts_ref.1, bf16[6,2,6144]{2,1,0:T(2,128)(2,1)} %bitcast.30, bf16[6,6144]{1,0:T(8,128)(2,1)} %bitcast.20), custom_call_target="tpu_custom_call" | custom-call | bytes 4194304 | tf_op jit(solution)/shard_map/pallas_call | solution.py:54
  3.8 2.6 %collective-permute-start.1 = (bf16[2,8,1536]{2,1,0:T(8,128)(2,1)S(1)}, bf16[2,8,1536]{2,1,0:T(8,128)(2,1)S(1)}, u32[]{:S(2)}, u32[]{:S(2)}) collective-permute-start(bf16[2,8,1536]{2,1,0:T(8,128)(2,1)S(1)} %pad_maximum_fusion.2), channel_id=1, source_target_pairs={{0,8},{4,12},{8,0},{12,4},{16,24},{20,28},{24,16},{28,20},{1,9},{5... | collective-permute-start | bytes 147464 | tf_op jit(solution)/shard_map/ppermute | solution.py:109
  6.4 1.5 %collective-permute-start.2 = (bf16[2,8,1536]{2,1,0:T(8,128)(2,1)S(1)}, bf16[2,8,1536]{2,1,0:T(8,128)(2,1)S(1)}, u32[]{:S(2)}, u32[]{:S(2)}) collective-permute-start(bf16[2,8,1536]{2,1,0:T(8,128)(2,1)S(1)} %pad_maximum_fusion.1.refs_0_), channel_id=1, source_target_pairs={{0,16},{4,20},{8,24},{12,28},{16,0},{20,4},{24,8},{28,12},{1,17},{... | collective-permute-start | bytes 147464 | tf_op jit(solution)/shard_map/ppermute | solution.py:109
  7.9 4.6 %shard_map.112.refs_4_.w1_ref = bf16[1536,4096]{1,0:T(8,128)(2,1)S(1)} custom-call(bf16[1536,4096]{1,0:T(8,128)(2,1)} %bitcast.25), custom_call_target="tpu_custom_call" | custom-call | bytes 12582912 | tf_op jit(solution)/shard_map/pallas_call | solution.py:54
  12.9 7.2 %shard_map.113 = (bf16[32,1536]{1,0:T(8,128)(2,1)S(1)}, bf16[16,1536]{1,0:T(8,128)(2,1)S(1)}, f32[48,2176]{1,0:T(8,128)S(1)}, f32[48,2176]{1,0:T(8,128)S(1)}, bf...) custom-call(bf16[2,8,1536]{2,1,0:T(8,128)(2,1)S(1)} %pad_maximum_fusion.1.refs_0_, ...), custom_call_target="tpu_custom_call" | custom-call | flops 603979776 | bytes 25165824 | tf_op jit(solution)/shard_map/pallas_call | solution.py:54
  22.9 1.7 %collective-permute-start.6 = (f32[32,2176]{1,0:T(8,128)S(1)}, f32[32,2176]{1,0:T(8,128)S(1)}, u32[]{:S(2)}, u32[]{:S(2)}) collective-permute-start(f32[32,2176]{1,0:T(8,128)S(1)} %pad_maximum_fusion.a_ref), channel_id=1, source_target_pairs={{0,8},{4,12},{8,0},{12,4},{16,24},{20,28},{24,16},{28,20},{1,9},{5... | collective-permute-start | bytes 835592 | tf_op jit(solution)/shard_map/ppermute | solution.py:109
  25.0 1.6 %collective-permute-start.9 = (bf16[2,8,1536]{2,1,0:T(8,128)(2,1)S(1)}, bf16[2,8,1536]{2,1,0:T(8,128)(2,1)S(1)}, u32[]{:S(2)}, u32[]{:S(2)}) collective-permute-start(bf16[2,8,1536]{2,1,0:T(8,128)(2,1)S(1)} %pad_maximum_fusion.3.refs_0_), channel_id=1, source_target_pairs={{0,16},{4,20},{8,24},{12,28},{16,0},{20,4},{24,8},{28,12},{1,17},{... | collective-permute-start | bytes 147464 | tf_op jit(solution)/shard_map/ppermute | solution.py:109
  26.6 1.4 %collective-permute-start.10 = (bf16[2,8,1536]{2,1,0:T(8,128)(2,1)S(1)}, bf16[2,8,1536]{2,1,0:T(8,128)(2,1)S(1)}, u32[]{:S(2)}, u32[]{:S(2)}) collective-permute-start(bf16[2,8,1536]{2,1,0:T(8,128)(2,1)S(1)} %pad_maximum_fusion.4), channel_id=1, source_target_pairs={{0,24},{4,28},{8,16},{12,20},{16,8},{20,12},{24,0},{28,4},{1,25},{... | collective-permute-start | bytes 147464 | tf_op jit(solution)/shard_map/ppermute | solution.py:109
  28.0 5.4 %collective-permute-done.8.refs_1_ = bf16[2,8,1536]{2,1,0:T(8,128)(2,1)S(1)} collective-permute-done((bf16[2,8,1536]{2,1,0:T(8,128)(2,1)S(1)}, bf16[2,8,1536]{2,1,0:T(8,128)(2,1)S(1)}, u32[]{:S(2)}, u32[]{:S(2)}) %collective-permute-start.8) | collective-permute-done | bytes 49184 | tf_op jit(solution)/shard_map/ppermute | solution.py:109
  33.4 1.6 %collective-permute-done.10.refs_3_ = bf16[2,8,1536]{2,1,0:T(8,128)(2,1)S(1)} collective-permute-done((bf16[2,8,1536]{2,1,0:T(8,128)(2,1)S(1)}, bf16[2,8,1536]{2,1,0:T(8,128)(2,1)S(1)}, u32[]{:S(2)}, u32[]{:S(2)}) %collective-permute-start.10) | collective-permute-done | bytes 49184 | tf_op jit(solution)/shard_map/ppermute | solution.py:109
  35.3 1.6 %collective-permute-start.14 = (f32[16,2176]{1,0:T(8,128)S(1)}, f32[16,2176]{1,0:T(8,128)S(1)}, u32[]{:S(2)}, u32[]{:S(2)}) collective-permute-start(f32[16,2176]{1,0:T(8,128)S(1)} %get-tuple-element.84.a_ref), channel_id=1, source_target_pairs={{0,8},{4,12},{8,0},{12,4},{16,24},{20,28},{24,16},{28,20},{1,9},{5... | collective-permute-start | bytes 417800 | tf_op jit(solution)/shard_map/ppermute | solution.py:109
  36.9 3.3 %shard_map.116.a_ref = bf16[16,1664]{1,0:T(8,128)(2,1)S(1)} custom-call(bf16[16,4224]{1,0:T(8,128)(2,1)S(1)} %get-tuple-element.56.own_ref.own0, bf16[16,4224]{1,0:T(8,128)(2,1)S(1)} %collective-permute-done.11.pair_ref.pair0, f32[16,128]{1,0:T(8,128)S(1)} %get-tuple-element.57.block_ref, bf16[1536,4096]{1,0:T(8,128)(2,1)S(1)} %shard_map.112.refs_4_.w1_ref), custom_call_target="tpu_custom_call" | custom-call | flops 201326592 | bytes 12582912 | tf_op jit(solution)/shard_map/pallas_call | solution.py:54
  40.7 3.6 %collective-permute-done.12.b_ref = bf16[16,1664]{1,0:T(8,128)(2,1)S(1)} collective-permute-done((bf16[16,1664]{1,0:T(8,128)(2,1)S(1)}, bf16[16,1664]{1,0:T(8,128)(2,1)S(1)}, u32[]{:S(2)}, u32[]{:S(2)}) %collective-permute-start.12) | collective-permute-done | bytes 53280 | tf_op jit(solution)/shard_map/ppermute | solution.py:109
  44.7 1.5 %collective-permute-start.13 = (bf16[16,1536]{1,0:T(8,128)(2,1)S(1)}, bf16[16,1536]{1,0:T(8,128)(2,1)S(1)}, u32[]{:S(2)}, u32[]{:S(2)}) collective-permute-start(bf16[16,1536]{1,0:T(8,128)(2,1)S(1)} %get-tuple-element.60.dxs0_ref), channel_id=1, source_target_pairs={{1,0},{2,1},{3,2},{5,4},{6,5},{7,6},{9,8},{10,9},{11,10},{13,12},{... | collective-permute-start | bytes 147464 | tf_op jit(solution)/shard_map/ppermute | solution.py:118
  46.2 5.1 %collective-permute-done.13.refs_4_.next_ref = bf16[16,1536]{1,0:T(8,128)(2,1)S(1)} collective-permute-done((bf16[16,1536]{1,0:T(8,128)(2,1)S(1)}, bf16[16,1536]{1,0:T(8,128)(2,1)S(1)}, u32[]{:S(2)}, u32[]{:S(2)}) %collective-permute-start.13) | collective-permute-done | bytes 49184 | tf_op jit(solution)/shard_map/ppermute | solution.py:118
  51.3 3.6 %shard_map.118 = (bf16[16,1536]{1,0:T(8,128)(2,1)S(1)}, f32[16,2048]{1,0:T(8,128)S(1)}, f32[16,2048]{1,0:T(8,128)S(1)}) custom-call(bf16[2,8,1536]{2,1,0:T(8,128)(2,1)S(1)} %pad_maximum_fusion.3.refs_0_, bf16[2,8,1536]{2,1,0:T(8,128)(2,1)S(1)} %collective-permute-done.8.refs_1_, bf16[2,8,1536]{2,1,0:T(8,128)(2,1)S(1)} %collective-permute-done.9.refs_2_, ...), custom_call_target="tpu_custom_call" | custom-call | flops 201326592 | bytes 12582912 | tf_op jit(solution)/shard_map/pallas_call | solution.py:54
  54.9 1.4 %collective-permute-done.15 = f32[16,2048]{1,0:T(8,128)S(1)} collective-permute-done((f32[16,2048]{1,0:T(8,128)S(1)}, f32[16,2048]{1,0:T(8,128)S(1)}, u32[]{:S(2)}, u32[]{:S(2)}) %collective-permute-start.15) | collective-permute-done | bytes 131104 | tf_op jit(solution)/shard_map/ppermute | solution.py:109
  56.3 1.3 %collective-permute-start.16 = (f32[16,2048]{1,0:T(8,128)S(1)}, f32[16,2048]{1,0:T(8,128)S(1)}, u32[]{:S(2)}, u32[]{:S(2)}) collective-permute-start(f32[16,2048]{1,0:T(8,128)S(1)} %add.7.up_ref), channel_id=1, source_target_pairs={{0,8},{4,12},{8,0},{12,4},{16,24},{20,28},{24,16},{28,20},{1,9},{5... | collective-permute-start | bytes 393224 | tf_op jit(solution)/shard_map/ppermute | solution.py:109
  59.1 5.3 %shard_map.120 = bf16[4096,1536]{1,0:T(8,128)(2,1)} custom-call(bf16[16,4224]{1,0:T(8,128)(2,1)S(1)} %get-tuple-element.56.own_ref.own0, bf16[16,4224]{1,0:T(8,128)(2,1)S(1)} %collective-permute-done.11.pair_ref.pair0, bf16[16,2048]{1,0:T(8,128)(2,1)S(1)} %get-tuple-element.70.own1, bf16[16,2048]{1,0:T(8,128)(2,1)S(1)} %collective-permute-done.17.pair1, ...), custom_call_target="tpu_custom_call" | custom-call | flops 402653184 | bytes 12582912 | tf_op jit(solution)/shard_map/pallas_call | solution.py:54
  65.9 5.0 %shard_map.122 = bf16[8,16,1536]{2,1,0:T(8,128)(2,1)} custom-call(bf16[16,2176]{1,0:T(8,128)(2,1)S(1)} %get-tuple-element.75.own_ref.own1, bf16[16,2176]{1,0:T(8,128)(2,1)S(1)} %collective-permute-done.18.pair_ref.pair1, f32[16,128]{1,0:T(8,128)S(1)} %get-tuple-element.76.block_ref, f32[16,128]{1,0:T(8,128)S(1)} %get-tuple-element.74.prob_ref, ...), custom_call_target="tpu_custom_call" | custom-call | flops 201326592 | bytes 12582912 | tf_op jit(solution)/shard_map/pallas_call | solution.py:54
  70.8 3.5 %all-to-all-start = ((bf16[8,16,1536]{2,1,0:T(8,128)(2,1)}), bf16[8,16,1536]{2,1,0:T(8,128)(2,1)S(1)}, u32[]{:S(2)}, u32[]{:S(2)}) async-start(bf16[8,16,1536]{2,1,0:T(8,128)(2,1)} %shard_map.122), calls=%async_computation | async-start | bytes 786432 | tf_op jit(solution)/shard_map/all_to_all | solution.py:646
  74.3 5.3 %shard_map.124 = bf16[1536,4096]{1,0:T(8,128)(2,1)} custom-call(bf16[16,4224]{1,0:T(8,128)(2,1)S(1)} %get-tuple-element.56.own_ref.own0, bf16[16,4224]{1,0:T(8,128)(2,1)S(1)} %collective-permute-done.11.pair_ref.pair0, bf16[16,2176]{1,0:T(8,128)(2,1)S(1)} %get-tuple-element.75.own_ref.own1, bf16[16,2176]{1,0:T(8,128)(2,1)S(1)} %collective-permute-done.18.pair_ref.pair1, ...), custom_call_target="tpu_custom_call" | custom-call | flops 402653184 | bytes 12582912 | tf_op jit(solution)/shard_map/pallas_call | solution.py:54
  79.6 3.0 %all-to-all-done.back_ref = bf16[8,16,1536]{2,1,0:T(8,128)(2,1)S(1)} async-done(((bf16[8,16,1536]{2,1,0:T(8,128)(2,1)}), bf16[8,16,1536]{2,1,0:T(8,128)(2,1)S(1)}, u32[]{:S(2)}, u32[]{:S(2)}) %all-to-all-start) | async-done | bytes 393248 | tf_op jit(solution)/shard_map/all_to_all | solution.py:646
  82.6 1.7 %shard_map.123 = (bf16[6,2,6144]{2,1,0:T(2,128)(2,1)}, f32[8,6144]{1,0:T(8,128)}) custom-call(s32[2,2,6]{2,1,0:T(2,128)S(1)} %bitcast.24, s32[8]{0:T(128)S(1)} %copy-done.3, bf16[8,16,1536]{2,1,0:T(8,128)(2,1)S(1)} %all-to-all-done.back_ref, bf16[6,6144]{1,0:T(8,128)(2,1)S(1)} %bitcast.21, bf16[8,6144]{1,0:T(8,128)(2,1)S(1)} %collective-permute-done.4.onward_ref, ...), custom_call_target="tpu_custom_call" | custom-call | tf_op jit(solution)/shard_map/pallas_call | solution.py:54
  (50 shorter events, 9.5 us)
Async XLA Ops:
  1.9 1.8 %collective-permute-start = (bf16[2,8,1536]{2,1,0:T(8,128)(2,1)S(1)}, bf16[2,8,1536]{2,1,0:T(8,128)(2,1)S(1)}, u32[]{:S(2)}, u32[]{:S(2)}) collective-permute-start(bf16[2,8,1536]{2,1,0:T(8,128)(2,1)S(1)} %get-tuple-element.44), channel_id=1, source_target_pairs={{0,4},{4,0},{8,12},{12,8},{16,20},{20,16},{24,28},{28,24},{1,5},{5... | collective-permute-start | bytes 147464 | tf_op jit(solution)/shard_map/ppermute | solution.py:109
  2.5 10.4 %collective-permute-start.4 = (bf16[8,6144]{1,0:T(8,128)(2,1)S(1)}, bf16[8,6144]{1,0:T(8,128)(2,1)S(1)}, u32[]{:S(2)}, u32[]{:S(2)}) collective-permute-start(bf16[8,6144]{1,0:T(8,128)(2,1)S(1)} %get-tuple-element.45), channel_id=1, source_target_pairs={{1,0},{2,1},{3,2},{5,4},{6,5},{7,6},{9,8},{10,9},{11,10},{13,12},{... | collective-permute-start | bytes 294920 | tf_op jit(solution)/shard_map/ppermute | solution.py:118
  3.8 8.7 %collective-permute-start.1 = (bf16[2,8,1536]{2,1,0:T(8,128)(2,1)S(1)}, bf16[2,8,1536]{2,1,0:T(8,128)(2,1)S(1)}, u32[]{:S(2)}, u32[]{:S(2)}) collective-permute-start(bf16[2,8,1536]{2,1,0:T(8,128)(2,1)S(1)} %pad_maximum_fusion.2), channel_id=1, source_target_pairs={{0,8},{4,12},{8,0},{12,4},{16,24},{20,28},{24,16},{28,20},{1,9},{5... | collective-permute-start | bytes 147464 | tf_op jit(solution)/shard_map/ppermute | solution.py:109
  6.4 6.2 %collective-permute-start.2 = (bf16[2,8,1536]{2,1,0:T(8,128)(2,1)S(1)}, bf16[2,8,1536]{2,1,0:T(8,128)(2,1)S(1)}, u32[]{:S(2)}, u32[]{:S(2)}) collective-permute-start(bf16[2,8,1536]{2,1,0:T(8,128)(2,1)S(1)} %pad_maximum_fusion.1.refs_0_), channel_id=1, source_target_pairs={{0,16},{4,20},{8,24},{12,28},{16,0},{20,4},{24,8},{28,12},{1,17},{... | collective-permute-start | bytes 147464 | tf_op jit(solution)/shard_map/ppermute | solution.py:109
  7.9 5.0 %collective-permute-start.3 = (bf16[2,8,1536]{2,1,0:T(8,128)(2,1)S(1)}, bf16[2,8,1536]{2,1,0:T(8,128)(2,1)S(1)}, u32[]{:S(2)}, u32[]{:S(2)}) collective-permute-start(bf16[2,8,1536]{2,1,0:T(8,128)(2,1)S(1)} %pad_maximum_fusion.2), channel_id=1, source_target_pairs={{0,24},{4,28},{8,16},{12,20},{16,8},{20,12},{24,0},{28,4},{1,25},{... | collective-permute-start | bytes 147464 | tf_op jit(solution)/shard_map/ppermute | solution.py:109
  20.1 2.7 %collective-permute-start.5 = (f32[48,2176]{1,0:T(8,128)S(1)}, f32[48,2176]{1,0:T(8,128)S(1)}, u32[]{:S(2)}, u32[]{:S(2)}) collective-permute-start(f32[48,2176]{1,0:T(8,128)S(1)} %get-tuple-element.51), channel_id=1, source_target_pairs={{0,4},{4,0},{8,12},{12,8},{16,20},{20,16},{24,28},{28,24},{1,5},{5... | collective-permute-start | bytes 1253384 | tf_op jit(solution)/shard_map/ppermute | solution.py:109
  21.3 1.4 %collective-permute-start.7 = (bf16[2,8,1536]{2,1,0:T(8,128)(2,1)S(1)}, bf16[2,8,1536]{2,1,0:T(8,128)(2,1)S(1)}, u32[]{:S(2)}, u32[]{:S(2)}) collective-permute-start(bf16[2,8,1536]{2,1,0:T(8,128)(2,1)S(1)} %get-tuple-element.54), channel_id=1, source_target_pairs={{0,4},{4,0},{8,12},{12,8},{16,20},{20,16},{24,28},{28,24},{1,5},{5... | collective-permute-start | bytes 147464 | tf_op jit(solution)/shard_map/ppermute | solution.py:109
  22.9 12.2 %collective-permute-start.6 = (f32[32,2176]{1,0:T(8,128)S(1)}, f32[32,2176]{1,0:T(8,128)S(1)}, u32[]{:S(2)}, u32[]{:S(2)}) collective-permute-start(f32[32,2176]{1,0:T(8,128)S(1)} %pad_maximum_fusion.a_ref), channel_id=1, source_target_pairs={{0,8},{4,12},{8,0},{12,4},{16,24},{20,28},{24,16},{28,20},{1,9},{5... | collective-permute-start | bytes 835592 | tf_op jit(solution)/shard_map/ppermute | solution.py:109
  24.5 8.9 %collective-permute-start.8 = (bf16[2,8,1536]{2,1,0:T(8,128)(2,1)S(1)}, bf16[2,8,1536]{2,1,0:T(8,128)(2,1)S(1)}, u32[]{:S(2)}, u32[]{:S(2)}) collective-permute-start(bf16[2,8,1536]{2,1,0:T(8,128)(2,1)S(1)} %pad_maximum_fusion.4), channel_id=1, source_target_pairs={{0,8},{4,12},{8,0},{12,4},{16,24},{20,28},{24,16},{28,20},{1,9},{5... | collective-permute-start | bytes 147464 | tf_op jit(solution)/shard_map/ppermute | solution.py:109
  25.0 8.4 %collective-permute-start.9 = (bf16[2,8,1536]{2,1,0:T(8,128)(2,1)S(1)}, bf16[2,8,1536]{2,1,0:T(8,128)(2,1)S(1)}, u32[]{:S(2)}, u32[]{:S(2)}) collective-permute-start(bf16[2,8,1536]{2,1,0:T(8,128)(2,1)S(1)} %pad_maximum_fusion.3.refs_0_), channel_id=1, source_target_pairs={{0,16},{4,20},{8,24},{12,28},{16,0},{20,4},{24,8},{28,12},{1,17},{... | collective-permute-start | bytes 147464 | tf_op jit(solution)/shard_map/ppermute | solution.py:109
  26.6 8.4 %collective-permute-start.10 = (bf16[2,8,1536]{2,1,0:T(8,128)(2,1)S(1)}, bf16[2,8,1536]{2,1,0:T(8,128)(2,1)S(1)}, u32[]{:S(2)}, u32[]{:S(2)}) collective-permute-start(bf16[2,8,1536]{2,1,0:T(8,128)(2,1)S(1)} %pad_maximum_fusion.4), channel_id=1, source_target_pairs={{0,24},{4,28},{8,16},{12,20},{16,8},{20,12},{24,0},{28,4},{1,25},{... | collective-permute-start | bytes 147464 | tf_op jit(solution)/shard_map/ppermute | solution.py:109
  35.2 1.7 %collective-permute-start.11 = (bf16[16,4224]{1,0:T(8,128)(2,1)S(1)}, bf16[16,4224]{1,0:T(8,128)(2,1)S(1)}, u32[]{:S(2)}, u32[]{:S(2)}) collective-permute-start(bf16[16,4224]{1,0:T(8,128)(2,1)S(1)} %get-tuple-element.56.own_ref.own0), channel_id=1, source_target_pairs={{0,4},{4,0},{8,12},{12,8},{16,20},{20,16},{24,28},{28,24},{1,5},{5... | collective-permute-start | bytes 405512 | tf_op jit(solution)/shard_map/ppermute | solution.py:109
  35.3 10.9 %collective-permute-start.14 = (f32[16,2176]{1,0:T(8,128)S(1)}, f32[16,2176]{1,0:T(8,128)S(1)}, u32[]{:S(2)}, u32[]{:S(2)}) collective-permute-start(f32[16,2176]{1,0:T(8,128)S(1)} %get-tuple-element.84.a_ref), channel_id=1, source_target_pairs={{0,8},{4,12},{8,0},{12,4},{16,24},{20,28},{24,16},{28,20},{1,9},{5... | collective-permute-start | bytes 417800 | tf_op jit(solution)/shard_map/ppermute | solution.py:109
  40.2 4.2 %collective-permute-start.12 = (bf16[16,1664]{1,0:T(8,128)(2,1)S(1)}, bf16[16,1664]{1,0:T(8,128)(2,1)S(1)}, u32[]{:S(2)}, u32[]{:S(2)}) collective-permute-start(bf16[16,1664]{1,0:T(8,128)(2,1)S(1)} %shard_map.116.a_ref), channel_id=1, source_target_pairs={{0,16},{4,20},{8,24},{12,28},{16,0},{20,4},{24,8},{28,12},{1,17},{... | collective-permute-start | bytes 159752 | tf_op jit(solution)/shard_map/ppermute | solution.py:109
  44.7 6.6 %collective-permute-start.13 = (bf16[16,1536]{1,0:T(8,128)(2,1)S(1)}, bf16[16,1536]{1,0:T(8,128)(2,1)S(1)}, u32[]{:S(2)}, u32[]{:S(2)}) collective-permute-start(bf16[16,1536]{1,0:T(8,128)(2,1)S(1)} %get-tuple-element.60.dxs0_ref), channel_id=1, source_target_pairs={{1,0},{2,1},{3,2},{5,4},{6,5},{7,6},{9,8},{10,9},{11,10},{13,12},{... | collective-permute-start | bytes 147464 | tf_op jit(solution)/shard_map/ppermute | solution.py:118
  54.9 1.4 %collective-permute-start.15 = (f32[16,2048]{1,0:T(8,128)S(1)}, f32[16,2048]{1,0:T(8,128)S(1)}, u32[]{:S(2)}, u32[]{:S(2)}) collective-permute-start(f32[16,2048]{1,0:T(8,128)S(1)} %get-tuple-element.69), channel_id=1, source_target_pairs={{0,4},{4,0},{8,12},{12,8},{16,20},{20,16},{24,28},{28,24},{1,5},{5... | collective-permute-start | bytes 393224 | tf_op jit(solution)/shard_map/ppermute | solution.py:109
  56.3 8.1 %collective-permute-start.16 = (f32[16,2048]{1,0:T(8,128)S(1)}, f32[16,2048]{1,0:T(8,128)S(1)}, u32[]{:S(2)}, u32[]{:S(2)}) collective-permute-start(f32[16,2048]{1,0:T(8,128)S(1)} %add.7.up_ref), channel_id=1, source_target_pairs={{0,8},{4,12},{8,0},{12,4},{16,24},{20,28},{24,16},{28,20},{1,9},{5... | collective-permute-start | bytes 393224 | tf_op jit(solution)/shard_map/ppermute | solution.py:109
  57.8 1.3 %collective-permute-start.17 = (bf16[16,2048]{1,0:T(8,128)(2,1)S(1)}, bf16[16,2048]{1,0:T(8,128)(2,1)S(1)}, u32[]{:S(2)}, u32[]{:S(2)}) collective-permute-start(bf16[16,2048]{1,0:T(8,128)(2,1)S(1)} %get-tuple-element.70.own1), channel_id=1, source_target_pairs={{0,4},{4,0},{8,12},{12,8},{16,20},{20,16},{24,28},{28,24},{1,5},{5... | collective-permute-start | bytes 196616 | tf_op jit(solution)/shard_map/ppermute | solution.py:109
  64.5 1.3 %collective-permute-start.18 = (bf16[16,2176]{1,0:T(8,128)(2,1)S(1)}, bf16[16,2176]{1,0:T(8,128)(2,1)S(1)}, u32[]{:S(2)}, u32[]{:S(2)}) collective-permute-start(bf16[16,2176]{1,0:T(8,128)(2,1)S(1)} %get-tuple-element.75.own_ref.own1), channel_id=1, source_target_pairs={{0,4},{4,0},{8,12},{12,8},{16,20},{20,16},{24,28},{28,24},{1,5},{5... | collective-permute-start | bytes 208904 | tf_op jit(solution)/shard_map/ppermute | solution.py:109
  65.8 16.7 %copy-start = (bf16[1,6,6144]{2,1,0:T(8,128)(2,1)S(1)}, bf16[1,6,6144]{2,1,0:T(8,128)(2,1)}, u32[]{:S(2)}) copy-start(bf16[1,6,6144]{2,1,0:T(8,128)(2,1)} %param.9) | copy-start | bytes 221188
  65.8 16.7 %copy-start.1 = (bf16[6,6144]{1,0:T(8,128)(2,1)S(1)}, bf16[6,6144]{1,0:T(8,128)(2,1)}, u32[]{:S(2)}) copy-start(bf16[6,6144]{1,0:T(8,128)(2,1)} %head_ref.1) | copy-start | bytes 221188
  65.8 16.7 %copy-start.2 = (s32[1,2,6,2]{2,3,1,0:T(2,128)S(1)}, s32[1,2,6,2]{2,3,1,0:T(2,128)}, u32[]{:S(2)}) copy-start(s32[1,2,6,2]{2,3,1,0:T(2,128)} %param.11) | copy-start | bytes 292
  65.8 16.7 %copy-start.3 = (s32[8]{0:T(128)S(1)}, s32[8]{0:T(128)}, u32[]{:S(2)}) copy-start(s32[8]{0:T(128)} %counts_ref.1) | copy-start | bytes 100
  70.8 11.7 %all-to-all-start = ((bf16[8,16,1536]{2,1,0:T(8,128)(2,1)}), bf16[8,16,1536]{2,1,0:T(8,128)(2,1)S(1)}, u32[]{:S(2)}, u32[]{:S(2)}) async-start(bf16[8,16,1536]{2,1,0:T(8,128)(2,1)} %shard_map.122), calls=%async_computation | async-start | bytes 786432 | tf_op jit(solution)/shard_map/all_to_all | solution.py:646

commit v3 on v2

v3 whole, which is shorter than its diff:
```python
import functools

import jax
import jax.numpy as jnp
from jax import lax
from jax.experimental import pallas as pl
from jax.experimental.pallas import tpu as pltpu
from jax.sharding import PartitionSpec as P

STEPS = 2
CAP = 2
QUARTERS = 4
LANES = 128
SLAB = 8
BF = jnp.bfloat16
F32 = jnp.float32
MIB = 1 << 20

NN = (((1,), (0,)), ((), ()))
NT = (((1,), (1,)), ((), ()))
TN = (((0,), (0,)), ((), ()))

VMEM = pl.BlockSpec(memory_space=pltpu.VMEM)
SMEM = pl.BlockSpec(memory_space=pltpu.SMEM)
ANY = pl.BlockSpec(memory_space=pl.ANY)


def dot(a, b, dims=NN):
    return lax.dot_general(a, b, dims, preferred_element_type=F32)


def split3(a):
    high = a.astype(BF)
    rest = a - high.astype(F32)
    mid = rest.astype(BF)
    return high, mid, (rest - mid.astype(F32)).astype(BF)


def dot_split(a, b, dims):
    at_a, at_b = dims[0][0][0], dims[0][1][0]
    a0, a1, a2 = split3(a)
    b0, b1, b2 = split3(b)
    return dot(
        jnp.concatenate([a0, a0, a1, a0, a1, a2], axis=at_a),
        jnp.concatenate([b0, b1, b0, b2, b1, b0], axis=at_b),
        dims,
    )


def iota(shape, dim):
    return lax.broadcasted_iota(jnp.int32, shape, dim)


def one_hot(cond):
    return jnp.where(cond, 1.0, 0.0).astype(BF)


def sds(shape, dtype):
    return jax.ShapeDtypeStruct(shape, dtype)


def call(body, args, specs, outs, flops=0, data=0, limit=12, scratch=(), out_specs=None, aliases=None):
    many = isinstance(outs, tuple)
    if out_specs is None:
        out_specs = tuple(VMEM for _ in outs) if many else VMEM
    return pl.pallas_call(
        body,
        in_specs=specs,
        out_specs=out_specs,
        out_shape=outs,
        scratch_shapes=scratch,
        input_output_aliases=aliases or {},
        cost_estimate=pl.CostEstimate(flops=flops, bytes_accessed=data, transcendentals=0),
        compiler_params=pltpu.CompilerParams(vmem_limit_bytes=limit * MIB),
    )(*args)


def in_hbm(array):
    return pltpu.with_memory_space_constraint(array, pltpu.HBM)


def copy_all(pairs, sems):
    copies = [
        pltpu.make_async_copy(source, target, sems.at[i])
        for i, (source, target) in enumerate(pairs)
    ]
    for copy in copies:
        copy.start()
    return copies


def wait_all(copies):
    for copy in copies:
        copy.wait()


def fetch(weight):
    def body(source, target, sem):
        copy = pltpu.make_async_copy(source, target, sem)
        copy.start()
        copy.wait()

    return call(
        body,
        (in_hbm(weight),),
        [ANY],
        pltpu.VMEM(weight.shape, weight.dtype),
        data=2 * weight.size,
        limit=4,
        scratch=[pltpu.SemaphoreType.DMA],
    )


def chunk_of(size, most):
    while size % most:
        most //= 2
    return most


def exchanged(array, mask):
    count = lax.axis_size("dp")
    return lax.ppermute(array, "dp", [(i, i ^ mask) for i in range(count)])


def permuted(array, bit):
    return exchanged(array, 1 << bit)


def from_next_section(array, mask=0):
    count, devices = lax.axis_size("section"), lax.axis_size("dp")
    pairs = [
        (d * count + i + 1, (d ^ mask) * count + i) for d in range(devices) for i in range(count - 1)
    ]
    return lax.ppermute(array, ("dp", "section"), pairs)


def slot_tokens(ids, step, live):
    tokens = ids.shape[2]
    count = jnp.int32(0)
    held = [jnp.int32(-1)] * CAP
    for t in range(tokens):
        routed = ((ids[step, 0, t] == 0) | (ids[step, 1, t] == 0)) & live
        for c in range(CAP):
            held[c] = jnp.where(routed & (count == c), jnp.int32(t), held[c])
        count = count + routed.astype(jnp.int32)
    return held


def silu_parts(pre):
    sig = jax.nn.sigmoid(pre)
    return pre * sig, sig * (1.0 + pre * (1.0 - sig))


def softmax_rows(logits):
    expo = jnp.exp(logits)
    prob = expo / jnp.sum(expo, axis=1, keepdims=True)
    rows, experts = logits.shape
    return jnp.concatenate([prob, jnp.zeros((rows, LANES - experts), F32)], axis=1)


def first_minus(prob):
    lane = iota(prob.shape, 1)
    return jnp.where(lane == 0, 1.0, 0.0) - prob


def local(saved_inputs, carried, head_grad, routing, replica_counts, router, w_in, w_out):
    sections = lax.axis_size("section")
    n = lax.axis_size("dp")
    groups = n // QUARTERS
    width = head_grad.shape[1]
    tokens = head_grad.shape[0]
    part = w_in.shape[2]
    hidden = w_in.shape[3]
    half = hidden // 2
    experts = router.shape[2]
    rows = n * CAP
    router_t = router[0].T
    x_tok = saved_inputs[0].transpose(1, 0, 2)
    carried_tok = carried[0]
    ids = routing[0].transpose(0, 2, 1)
    last_section = sections - 1
    w1 = fetch(w_in[0, 0])

    def where_am_i():
        return lax.axis_index("section"), lax.axis_index("dp")

    def quarter_lanes():
        return pl.ds(pl.multiple_of(lax.rem(lax.axis_index("dp"), QUARTERS) * part, LANES), part)

    def half_lanes(core):
        return pl.ds(pl.multiple_of(core * half, LANES), half)

    def pick(held, value):
        row = iota((SLAB, value.shape[0]), 0)
        col = iota((SLAB, value.shape[0]), 1)
        chosen = jnp.zeros((SLAB, value.shape[0]), F32)
        for c in range(len(held)):
            chosen = chosen + jnp.where((row == c) & (col == held[c]), 1.0, 0.0)
        return dot(chosen.astype(BF), value)

    by_chip = n == 2 * QUARTERS

    def place_of(home):
        return jnp.bitwise_xor(home, lax.axis_index("dp")) if by_chip else home

    def send_quarters(slab_ref, slab, mine_ref, theirs_ref):
        slab_ref[...] = slab
        own = lax.rem(lax.axis_index("dp"), QUARTERS)
        for i in range(QUARTERS):
            at = pl.multiple_of(jnp.bitwise_xor(own, i) * part, LANES)
            ref = theirs_ref if i % 2 else mine_ref
            ref[i // 2] = slab_ref[:, pl.ds(at, part)].astype(BF)

    send_shapes = (sds((2, SLAB, part), BF), sds((2, SLAB, part), BF))
    slab_scratch = pltpu.VMEM((SLAB, width), F32)

    def spread_whole(mine, theirs):
        own = lax.rem(lax.axis_index("dp"), QUARTERS)
        quads = jnp.stack([mine[0], theirs[0], mine[1], theirs[1]])
        block = quads[jnp.bitwise_xor(jnp.arange(n) % QUARTERS, own)]
        return (lax.all_to_all(block, "dp", split_axis=0, concat_axis=0, tiled=True),)

    def spread_in_chip(mine, theirs):
        handed = permuted(theirs, 0)
        return jnp.stack([mine[0], handed[0]]), jnp.stack([mine[1], handed[1]])

    def joined(refs):
        return jnp.concatenate([ref[...].reshape(-1, part) for ref in refs], axis=0)

    def dispatch_body(
        ids_hbm,
        counts_hbm,
        x_hbm,
        dy_hbm,
        mine_ref,
        theirs_ref,
        onward_ref,
        ids_ref,
        counts_ref,
        x_ref,
        dy_ref,
        slab_ref,
        sems,
    ):
        wait_all(
            copy_all(
                ((ids_hbm, ids_ref), (counts_hbm, counts_ref), (dy_hbm, dy_ref), (x_hbm, x_ref)),
                sems,
            )
        )
        section, dev = where_am_i()
        count = counts_ref[dev]
        held = [slot_tokens(ids_ref, step, step + section < count) for step in range(STEPS)]
        dy = dy_ref[...]
        slab = pick([-1] * (STEPS * CAP) + held[0], dy)
        row = iota((SLAB, width), 0)
        lane = lax.rem(iota((SLAB, width), 1), part)
        for step in range(STEPS):
            for c in range(CAP):
                value = x_ref[jnp.maximum(held[step][c], 0), step:step + 1, :].astype(F32)
                wanted = (row == step * CAP + c) & (held[step][c] >= 0)
                slab = jnp.where(wanted, jnp.broadcast_to(value, (SLAB, width)), slab)
        send_quarters(slab_ref, slab, mine_ref, theirs_ref)
        onward = pick(list(range(tokens)), dy)
        for c in range(CAP):
            code = (held[0][c] + 1).astype(F32)
            onward = jnp.where((row == tokens) & (lane == c), code, onward)
        onward_ref[...] = onward.astype(BF)

    mine, theirs, onward = call(
        dispatch_body,
        (in_hbm(ids), in_hbm(replica_counts), in_hbm(x_tok), in_hbm(carried_tok)),
        [ANY] * 4,
        (*send_shapes, sds((SLAB, width), BF)),
        data=4 * MIB,
        scratch=[
            pltpu.SMEM(ids.shape, jnp.int32),
            pltpu.SMEM(replica_counts.shape, jnp.int32),
            pltpu.VMEM(x_tok.shape, BF),
            pltpu.VMEM(carried_tok.shape, BF),
            slab_scratch,
            pltpu.SemaphoreType.DMA((4,)),
        ],
    )
    onward = from_next_section(onward)
    if by_chip:
        same, cross = spread_in_chip(mine, theirs)
        came = (same, exchanged(cross, 2), exchanged(same, 4), exchanged(cross, 6))
    else:
        came = spread_whole(mine, theirs)
    came, onward = lax.optimization_barrier((came, onward))

    wide = half + LANES

    def first_body(*refs):
        w1_ref, w2_hbm, router_hbm, xs_ref, ys_ref, keep_ref, send_ref, w2_ref, router_ref, sems = refs[
            len(came):
        ]
        core = lax.rem(lax.axis_index("dp"), 2)
        step = chunk_of(half, 512)
        router_copy = pltpu.make_async_copy(
            router_hbm.at[:, quarter_lanes()], router_ref, sems.at[0]
        )
        router_copy.start()
        chunks = [
            (ref, at, pl.multiple_of(which * half + at, LANES))
            for ref, which in ((send_ref, 1 - core), (keep_ref, core))
            for at in range(0, half, step)
        ]
        copies = copy_all(
            [(w2_hbm.at[pl.ds(lane, step)], w2_ref.at[pl.ds(lane, step)]) for _, _, lane in chunks],
            sems.at[pl.ds(1, len(chunks))],
        )

        @pl.when(lax.axis_index("dp") >= 0)
        def _():
            flat = joined(refs[:len(came)])
            row = iota((STEPS * rows, n * SLAB), 0)
            col = iota((STEPS * rows, n * SLAB), 1)
            slot = row % rows
            want = place_of(slot // CAP) * SLAB + (row // rows) * CAP + slot % CAP
            xs = dot(one_hot(col == want), flat).astype(BF)
            row = iota((rows, n * SLAB), 0)
            col = iota((rows, n * SLAB), 1)
            ys = dot(one_hot(col == place_of(row // CAP) * SLAB + 2 * CAP + row % CAP), flat).astype(BF)
            xs_ref[...] = xs
            ys_ref[...] = ys
            router_copy.wait()
            parts = jnp.concatenate(
                [
                    jnp.concatenate([p, jnp.zeros((LANES - experts, part), BF)], axis=0)
                    for p in split3(router_ref[...])
                ],
                axis=0,
            )
            logits = dot(xs, parts, NT)
            logits = logits[:, 0:LANES] + logits[:, LANES:2 * LANES] + logits[:, 2 * LANES:3 * LANES]
            zero = jnp.zeros((rows, LANES), F32)
            both = STEPS * rows
            for ref, at, lane in chunks:
                ref[0:both, at:at + step] = dot(xs, w1_ref[:, pl.ds(lane, step)])
            for ref in (send_ref, keep_ref):
                ref[0:both, half:wide] = logits
                ref[both:both + rows, half:wide] = zero
            for (ref, at, lane), copy in zip(chunks, copies):
                copy.wait()
                ref[both:both + rows, at:at + step] = dot(ys, w2_ref[pl.ds(lane, step), :], NT)

    xs, ys0, keep, send, w2, router_q = call(
        first_body,
        (*came, w1, in_hbm(w_out[0, 0]), in_hbm(router_t)),
        [VMEM] * (len(came) + 1) + [ANY] * 2,
        (
            sds((STEPS * rows, part), BF),
            sds((rows, part), BF),
            sds((3 * rows, wide), F32),
            sds((3 * rows, wide), F32),
            pltpu.VMEM((hidden, part), BF),
            sds((experts, part), F32),
        ),
        flops=2 * 3 * rows * part * hidden,
        data=2 * part * hidden * 2,
        scratch=[pltpu.SemaphoreType.DMA((1 + 2 * (half // chunk_of(half, 512)),))],
    )
    send, onward = lax.optimization_barrier((send, onward))
    send_other = permuted(send, 0)

    def base_body(
        ids_hbm,
        counts_hbm,
        onward_ref,
        head_hbm,
        mine_ref,
        theirs_ref,
        ids_ref,
        counts_ref,
        head_ref,
        slab_ref,
        sems,
    ):
        wait_all(
            copy_all(((ids_hbm, ids_ref), (counts_hbm, counts_ref), (head_hbm, head_ref)), sems)
        )
        section, dev = where_am_i()
        live = 1 + section < counts_ref[dev]
        last = section == last_section
        held = slot_tokens(ids_ref, 1, live)
        onward = onward_ref[...]
        slab = pick(held, jnp.where(last, head_ref[...], onward[0:tokens]))
        row = iota((SLAB, width), 0)
        code = jnp.broadcast_to(onward[tokens:tokens + 1].astype(F32), (SLAB, width))
        for c in range(CAP):
            same = (held[c] >= 0) & (code == (held[c] + 1).astype(F32))
            slab = jnp.where((row == CAP + c) & same, 1.0, slab)
        send_quarters(slab_ref, slab, mine_ref, theirs_ref)

    base_sent = call(
        base_body,
        (in_hbm(ids), in_hbm(replica_counts), onward, in_hbm(head_grad)),
        [ANY, ANY, VMEM, ANY],
        send_shapes,
        data=4 * MIB,
        scratch=[
            pltpu.SMEM(ids.shape, jnp.int32),
            pltpu.SMEM(replica_counts.shape, jnp.int32),
            pltpu.VMEM(head_grad.shape, BF),
            slab_scratch,
            pltpu.SemaphoreType.DMA((3,)),
        ],
    )
    send_other, base_sent = lax.optimization_barrier((send_other, base_sent))

    def pair_body(keep_ref, other_ref, mine0_ref, mine1_ref, narrow0_ref, narrow1_ref):
        both = STEPS * rows
        for at, ref, narrow, to in (
            (0, mine0_ref, narrow0_ref, 0),
            (both, mine0_ref, narrow0_ref, rows),
            (rows, mine1_ref, narrow1_ref, 0),
        ):
            total = keep_ref[at:at + rows, :] + other_ref[at:at + rows, :]
            ref[to:to + rows, :] = total
            narrow[to:to + rows, 0:half] = total[:, 0:half].astype(BF)
            pieces = split3(total[:, half:half + experts])
            spare = jnp.zeros((rows, LANES - 3 * experts), BF)
            narrow[to:to + rows, half:wide] = jnp.concatenate([*pieces, spare], axis=1)

    mine0, mine1, narrow0, narrow1 = call(
        pair_body,
        (keep, send_other),
        [VMEM] * 2,
        (
            sds((2 * rows, wide), F32),
            sds((rows, wide), F32),
            sds((2 * rows, wide), BF),
            sds((rows, wide), BF),
        ),
    )
    other0 = permuted(narrow0, 1)

    used = 2 * CAP
    if by_chip:
        base_handed = permuted(base_sent[1], 0)

        def join_body(mine_ref, handed_ref, same_ref, cross_ref):
            for i, ref in enumerate((same_ref, cross_ref)):
                ref[...] = jnp.concatenate([mine_ref[i, 0:used], handed_ref[i, 0:used]], axis=0)

        base_same, base_cross = call(
            join_body,
            (base_sent[0], base_handed),
            [VMEM] * 2,
            (sds((2 * used, part), BF), sds((2 * used, part), BF)),
        )
        base_beside = exchanged(base_cross, 2)
        other0, base_beside = lax.optimization_barrier((other0, base_beside))

        def four_body(same_ref, beside_ref, out_ref):
            out_ref[...] = jnp.concatenate([same_ref[...], beside_ref[...]], axis=0)

        base_four = call(four_body, (base_same, base_beside), [VMEM] * 2, sds((4 * used, part), BF))
    else:
        base_whole = spread_whole(*base_sent)[0][:, 0:used]

    def all_logits(own, other):
        at = half + experts
        pieces = [other[:, half + i * experts:at + i * experts].astype(F32) for i in range(3)]
        return own[:, half:at] + (pieces[0] + pieces[1] + pieces[2])

    def gated(pre, upper, gate):
        act, slope = silu_parts(pre)
        dpre = (gate * upper * slope).astype(BF)
        block = jnp.sum(act * upper, axis=1, keepdims=True)
        return act, dpre, block

    def split_sum(block):
        high = block.astype(BF)
        low = (block - high.astype(F32)).astype(BF)
        lane = iota((rows, LANES), 1)
        zero = jnp.zeros((rows, LANES), BF)
        return jnp.where(lane == 0, high, jnp.where(lane == 1, low, zero))

    def gate_of(prob):
        return prob[:, 0:1].astype(BF).astype(F32)

    def act0_body(a_ref, b_ref, out_ref, prob_ref, block_ref):
        total = a_ref[:, 0:half] + b_ref[:, 0:half].astype(F32)
        prob = softmax_rows(all_logits(a_ref[0:rows, :], b_ref[0:rows, :]))
        gate = gate_of(prob)
        pre = total[0:rows]
        upper = total[rows:2 * rows]
        act, dpre, block = gated(pre, upper, gate)
        out_ref[:, 0:half] = dpre
        out_ref[:, half:wide] = split_sum(block)
        out_ref[:, wide:wide + half] = (gate * act).astype(BF)
        prob_ref[...] = prob
        block_ref[...] = jnp.broadcast_to(block, (rows, LANES))

    hid0, prob0, block0 = call(
        act0_body,
        (mine0, other0),
        [VMEM] * 2,
        (sds((rows, wide + half), BF), sds((rows, LANES), F32), sds((rows, LANES), F32)),
    )
    hid0_pair = permuted(hid0, 0)

    def block_sum(block, pair_ref):
        extra = pair_ref[:, half:half + 1].astype(F32) + pair_ref[:, half + 1:half + 2].astype(F32)
        return (block[:, 0:1] + extra).astype(BF)

    def in_order(own, pair, core):
        return (
            jnp.where(core == 0, own, pair),
            jnp.where(core == 0, pair, own),
        )

    def dx_of(own_ref, pair_ref, w1_ref, core):
        low, high = in_order(own_ref[:, 0:half], pair_ref[:, 0:half], core)
        step = chunk_of(part, 256)
        pieces = []
        for at in range(0, part, step):
            pieces.append(
                dot(low, w1_ref[at:at + step, 0:half], NT)
                + dot(high, w1_ref[at:at + step, half:hidden], NT)
            )
        return jnp.concatenate(pieces, axis=1)

    def routed_back(dx, block_ref, pair_ref, prob, router_ref):
        dgate = block_sum(block_ref[...], pair_ref).astype(F32)
        dlog = dgate * prob[:, 0:1] * first_minus(prob)
        return (dx + dot_split(dlog[:, 0:experts], router_ref[...], NN)).astype(BF), dlog

    def dx0_body(own_ref, pair_ref, block_ref, prob_ref, router_ref, w1_ref, out_ref, dlog_ref):
        core = lax.rem(lax.axis_index("dp"), 2)
        dx = dx_of(own_ref, pair_ref, w1_ref, core)
        out_ref[...], dlog_ref[...] = routed_back(dx, block_ref, pair_ref, prob_ref[...], router_ref)

    dx0, dlog0 = call(
        dx0_body,
        (hid0, hid0_pair, block0, prob0, router_q, w1),
        [VMEM] * 6,
        (sds((rows, part), BF), sds((rows, LANES), F32)),
        flops=2 * rows * part * hidden,
        data=2 * part * hidden,
    )
    if by_chip:
        dx0, narrow1, base_four = lax.optimization_barrier((dx0, narrow1, base_four))
        base = (base_four, exchanged(base_four, 4))
    else:
        base = (base_whole.reshape(n * used, part),)
    cut = half // 2
    other1 = (permuted(narrow1[:, 0:cut], 1), permuted(narrow1[:, cut:wide], 1))
    if groups == 2:
        nexts = (from_next_section(dx0), from_next_section(dx0, QUARTERS))
        next_back = nexts[0]
    else:
        total0 = dx0.astype(F32)
        for bit in range(2, groups.bit_length() + 1):
            total0 = total0 + permuted(total0, bit)
        nexts = (from_next_section(total0.astype(BF)),)
        next_back = jnp.where(lax.axis_index("dp") < QUARTERS, nexts[0], 0)

    def up1_body(*refs):
        next_refs, rest = refs[len(base):][:len(nexts)], refs[len(base) + len(nexts):]
        w2_ref, ys_ref, keep_ref, send_ref = rest
        core = lax.rem(lax.axis_index("dp"), 2)
        flat = joined(refs[:len(base)])
        row = iota((rows, n * used), 0)
        col = iota((rows, n * used), 1)
        want = place_of(row // CAP) * used + row % CAP
        value = dot(one_hot(col == want), flat)
        match = dot(one_hot(col == want + CAP), flat[:, 0:LANES])
        row = iota((rows, rows), 0)
        col = iota((rows, rows), 1)
        place = jnp.zeros((rows, rows), F32)
        for b in range(CAP):
            place = place + jnp.where(
                (row // CAP == col // CAP) & (col % CAP == b), match[:, b:b + 1], 0.0
            )
        for ref in next_refs:
            value = value + dot(place.astype(BF), ref[...])
        ys = value.astype(BF)
        ys_ref[...] = ys
        step = chunk_of(half, 512)
        for ref, which in ((send_ref, 1 - core), (keep_ref, core)):
            for at in range(0, half, step):
                lanes = pl.ds(pl.multiple_of(which * half + at, LANES), step)
                ref[:, at:at + step] = dot(ys, w2_ref[lanes, :], NT)

    ys1, keep1, send1 = call(
        up1_body,
        (*base, *nexts, w2),
        [VMEM] * (len(base) + len(nexts) + 1),
        (sds((rows, part), BF), sds((rows, half), F32), sds((rows, half), F32)),
        flops=2 * rows * part * hidden,
        data=2 * part * hidden,
    )
    send1, other1 = lax.optimization_barrier((send1, other1))
    up1 = keep1 + permuted(send1, 0)

    def act1_body(a_ref, low_ref, high_ref, out_ref, pre_ref, prob_ref):
        other = jnp.concatenate([low_ref[...], high_ref[...]], axis=1)
        prob = softmax_rows(all_logits(a_ref[...], other))
        pre = a_ref[:, 0:half] + other[:, 0:half].astype(F32)
        act, _ = silu_parts(pre)
        pre_ref[...] = pre
        out_ref[...] = (gate_of(prob) * act).astype(BF)
        prob_ref[...] = prob

    scaled1, pre1, prob1 = call(
        act1_body,
        (mine1, *other1),
        [VMEM] * 3,
        (sds((rows, half), BF), sds((rows, half), F32), sds((rows, LANES), F32)),
    )
    scaled1_pair = permuted(scaled1, 0)

    other_up1 = permuted(up1.astype(BF), 1)

    both = STEPS * rows

    def outer(body, args, height, across, rest):
        written = height - rest

        def write(*refs):
            a, b = body(*refs[:len(args)])
            out_ref, *rest_refs, held_ref, sems = refs[len(args):]
            step = written // SLAB
            copies = []
            for i in range(SLAB):
                at = pl.ds(i * step, step)
                held_ref[at, :] = dot(a[:, i * step:(i + 1) * step], b, TN).astype(BF)
                copies += copy_all(((held_ref.at[at], out_ref.at[at]),), sems.at[pl.ds(i, 1)])
            for ref in rest_refs:
                step = chunk_of(rest, 256)
                for i in range(0, rest, step):
                    ref[i:i + step, :] = dot(a[:, written + i:written + i + step], b, TN).astype(BF)
            wait_all(copies)

        result = call(
            write,
            args,
            [VMEM] * len(args),
            (sds((height, across), BF),) + ((pltpu.VMEM((rest, across), BF),) if rest else ()),
            flops=2 * both * height * across,
            data=2 * written * across,
            limit=16,
            out_specs=(ANY,) + ((VMEM,) if rest else ()),
            scratch=[pltpu.VMEM((written, across), BF), pltpu.SemaphoreType.DMA((SLAB,))],
        )
        return result if rest else result[0]

    def copy_rest(rest_ref, out_ref, sems):
        step = rest_ref.shape[0] // SLAB
        begin = out_ref.shape[0] - rest_ref.shape[0]
        return copy_all(
            [
                (rest_ref.at[pl.ds(i * step, step)], out_ref.at[pl.ds(begin + i * step, step)])
                for i in range(SLAB)
            ],
            sems,
        )

    def grad_out_body(own0, pair0, own1, pair1, ys0_ref, ys1_ref):
        core = lax.rem(lax.axis_index("dp"), 2)
        a0, b0 = in_order(own0[:, wide:wide + half], pair0[:, wide:wide + half], core)
        a1, b1 = in_order(own1[...], pair1[...], core)
        scaled = jnp.concatenate(
            [jnp.concatenate([a0, b0], axis=1), jnp.concatenate([a1, b1], axis=1)], axis=0
        )
        return scaled, jnp.concatenate([ys0_ref[...], ys1_ref[...]], axis=0)

    out_args = (hid0, hid0_pair, scaled1, scaled1_pair, ys0, ys1)
    grad_out, rest_out = outer(grad_out_body, out_args, hidden, part, half)

    other_up1, grad_out = lax.optimization_barrier((other_up1, grad_out))

    def act2_body(pre_ref, up_ref, other_ref, prob_ref, out_ref, block_ref):
        pre = pre_ref[...]
        upper = up_ref[...] + other_ref[...].astype(F32)
        _, dpre, block = gated(pre, upper, gate_of(prob_ref[...]))
        out_ref[:, 0:half] = dpre
        out_ref[:, half:wide] = split_sum(block)
        block_ref[...] = jnp.broadcast_to(block, (rows, LANES))

    hid1, block1 = call(
        act2_body,
        (pre1, up1, other_up1, prob1),
        [VMEM] * 4,
        (sds((rows, wide), BF), sds((rows, LANES), F32)),
    )
    hid1_pair = permuted(hid1, 0)

    back_rows = 2 * SLAB

    def dx1_body(
        own_ref, pair_ref, block_ref, prob_ref, dlog0_ref, dx0_ref, next_ref, xs_ref, router_ref, w1_ref, rest_ref, _, *refs
    ):
        grad_ref, *out_refs, sems = refs
        copies = copy_rest(rest_ref, grad_ref, sems)

        @pl.when(lax.axis_index("dp") >= 0)
        def _():
            core = lax.rem(lax.axis_index("dp"), 2)
            dx = dx_of(own_ref, pair_ref, w1_ref, core)
            dx, dlog = routed_back(dx, block_ref, pair_ref, prob_ref[...], router_ref)
            dlogs = jnp.concatenate([dlog0_ref[...], dlog], axis=0)
            grad = dot(
                jnp.concatenate(split3(dlogs), axis=0), jnp.concatenate([xs_ref[...]] * 3, axis=0), TN
            )[0:experts, :].astype(BF)
            source = jnp.concatenate([dx, dx0_ref[...], next_ref[...], grad], axis=0)
            count = 3 * rows + experts
            slabs = n // len(out_refs)
            row = iota((n * back_rows, count), 0)
            col = iota((n * back_rows, count), 1)
            home = row // back_rows
            if by_chip:
                home = place_of(home % slabs * 2 + home // slabs)
            kind = row % back_rows
            want = jnp.where(
                kind < 3 * CAP,
                (kind // CAP) * rows + home * CAP + kind % CAP,
                jnp.where(kind >= SLAB, 3 * rows + kind - SLAB, -1),
            )
            out = dot(one_hot(col == want), source).astype(BF)
            for i, ref in enumerate(out_refs):
                at = i * slabs * back_rows
                ref[...] = out[at:at + slabs * back_rows].reshape(slabs, back_rows, part)

        wait_all(copies)

    back_shapes = (sds((n // 2, back_rows, part), BF),) * 2 if by_chip else (sds((n, back_rows, part), BF),)
    grad_out, *back_sent = call(
        dx1_body,
        (hid1, hid1_pair, block1, prob1, dlog0, dx0, next_back, xs, router_q, w1, rest_out, grad_out),
        [VMEM] * 11 + [ANY],
        (sds((hidden, part), BF), *back_shapes),
        flops=2 * rows * part * hidden,
        data=2 * part * hidden,
        limit=12,
        out_specs=(ANY, *(VMEM for _ in back_shapes)),
        scratch=[pltpu.SemaphoreType.DMA((SLAB,))],
        aliases={11: 0},
    )
    if by_chip:
        back_handed = permuted(back_sent[1], 0)

        def pairs_body(mine_ref, handed_ref, *out_refs):
            for k, ref in enumerate(out_refs):
                ref[0] = mine_ref[k]
                ref[1] = handed_ref[k]

        chips = call(
            pairs_body,
            (back_sent[0], back_handed),
            [VMEM] * 2,
            tuple(sds((2, back_rows, part), BF) for _ in range(n // 2)),
        )
        back = tuple(exchanged(chip, 2 * k) if k else chip for k, chip in enumerate(chips))
    else:
        back = (lax.all_to_all(back_sent[0], "dp", split_axis=0, concat_axis=0, tiled=True),)

    def grad_in_body(own0, pair0, own1, pair1, xs_ref):
        core = lax.rem(lax.axis_index("dp"), 2)
        a0, b0 = in_order(own0[:, 0:half], pair0[:, 0:half], core)
        a1, b1 = in_order(own1[:, 0:half], pair1[:, 0:half], core)
        dpre = jnp.concatenate(
            [jnp.concatenate([a0, b0], axis=1), jnp.concatenate([a1, b1], axis=1)], axis=0
        )
        return xs_ref[...], dpre

    in_args = (hid0, hid0_pair, hid1, hid1_pair, xs)
    grad_in = outer(grad_in_body, in_args, part, hidden, 0)

    def final_body(ids_ref, counts_ref, dy_ref, onward_ref, head_ref, *refs):
        back_refs, (out_ref, router_out_ref) = refs[:-2], refs[-2:]
        section, dev = where_am_i()
        own = lax.rem(dev, QUARTERS)
        count = counts_ref[dev]
        last = section == last_section
        live0 = section < count
        live1 = 1 + section < count
        held0 = slot_tokens(ids_ref, 0, live0)
        held1 = slot_tokens(ids_ref, 1, live1)
        codes = onward_ref[tokens:tokens + 1, 0:LANES].astype(F32)
        before = [codes[:, c:c + 1] - 1.0 for c in range(CAP)]

        shape = (4 * SLAB, groups * back_rows)
        row = iota(shape, 0).astype(F32)
        col = lax.rem(iota(shape, 1), back_rows)
        place = (row - 3 * SLAB == (col - SLAB).astype(F32)) & (col >= SLAB)
        for i, (held, at) in enumerate(((held0, CAP), (before, 2 * CAP), (held1, 0))):
            for c in range(CAP):
                token = held[c].astype(F32)
                place = place | ((token >= 0) & (row == token + i * SLAB) & (col == at + c))
        place = one_hot(place)

        for i in range(QUARTERS):
            if by_chip:
                quarter = jnp.bitwise_xor(own, i)
                blocks = [back_refs[i // 2 + 2 * g][i % 2] for g in range(groups)]
            else:
                quarter = i
                blocks = [back_refs[0][g * QUARTERS + i] for g in range(groups)]
            lanes = pl.ds(pl.multiple_of(quarter * part, LANES), part)
            sums = dot(place, jnp.concatenate(blocks, axis=0))
            router_out_ref[:, lanes] = sums[3 * SLAB:3 * SLAB + experts]
            out0 = jnp.where(live0, dy_ref[:, lanes].astype(F32), 0.0) + sums[0:tokens]
            out1 = jnp.where(last, head_ref[:, lanes], onward_ref[0:tokens, lanes]).astype(F32)
            out1 = jnp.where(live1, out1, 0.0) + sums[SLAB:SLAB + tokens]
            out1 = out1.astype(BF).astype(F32) + sums[2 * SLAB:2 * SLAB + tokens]
            out0 = out0.astype(BF)
            out1 = out1.astype(BF)
            for t in range(tokens):
                out_ref[t, 0:1, lanes] = out0[t:t + 1]
                out_ref[t, 1:2, lanes] = out1[t:t + 1]

    grads, router_grad = call(
        final_body,
        (ids, replica_counts, carried_tok, onward, head_grad, *back),
        [SMEM, SMEM] + [VMEM] * (3 + len(back)),
        (sds((tokens, STEPS, width), BF), sds((experts, width), F32)),
        limit=24,
    )
    input_grad = grads.transpose(1, 0, 2)[:, None]
    return (input_grad, grad_in[None, None], grad_out[None, None], router_grad.T[None])


def solution(mesh):
    in_specs = (
        P("section", None, "dp", None),
        P("section", "dp", None),
        P("dp", None),
        P("section", None, "dp", None),
        P(),
        P("section", None, None),
        P("section", "dp", None, None),
        P("section", "dp", None, None),
    )
    out_specs = (
        P(None, "section", "dp", None),
        P("section", "dp", None, None),
        P("section", "dp", None, None),
        P("section", None, None),
    )
    return jax.shard_map(local, mesh=mesh, in_specs=in_specs, out_specs=out_specs, check_vma=False)
```

time: 84.6 us -> 71.6 us (0.85)
  waiting for transfers between devices: 23.7 us -> 13.6 us
  Pallas kernels: 39.1 us -> 36.3 us
    ppermute x17 -> x20, waiting for transfers between devices: 15.6 us -> 9.91 us  [exchanged(): return lax.ppermute(array, 'dp', [(i, i ^ mask) for i in range(count)])]
    all_to_all x1 -> x0, starting transfers between devices: 3.45 us -> none  [local(): lax.all_to_all(back_sent, 'dp', split_axis=0, concat_axis=0, tiled=True)]
    all_to_all x1 -> x0, waiting for transfers between devices: 3.01 us -> none  [local(): lax.all_to_all(back_sent, 'dp', split_axis=0, concat_axis=0, tiled=True)]
    pallas_call x14 -> x17, Pallas kernels: 39.1 us -> 36.3 us  [call(): pl.pallas_call(body, in_specs=specs, out_specs=out_specs, out_shape=outs,...]
    ppermute x17 -> x20, starting transfers between devices: 14.2 us -> 16.3 us  [exchanged(): return lax.ppermute(array, 'dp', [(i, i ^ mask) for i in range(count)])]
    ppermute x2 -> x3, waiting for transfers between devices: 5.12 us -> 3.65 us  [from_next_section(): return lax.ppermute(array, ('dp', 'section'), pairs)]
    ppermute x2 -> x3, starting transfers between devices: 2.75 us -> 4.03 us  [from_next_section(): return lax.ppermute(array, ('dp', 'section'), pairs)]
  transfers between devices with their start and end apart: 20 -> 23, of which waited for: 10 -> 9; matrix products, arithmetic and copies ran while one was open for 0% -> 0% of each run, Pallas kernels for 24% -> 26%
where the time goes in v3:
time: 71.6 us; the launch traced here: 71.3 us
  Pallas kernels  36.3 us (51%)
  starting transfers between devices  20.4 us (28%)
  waiting for transfers between devices  13.6 us (19%)
  between operations  0.98 us (1%)
    pallas_call x17, Pallas kernels, call(): pl.pallas_call(body, in_specs=specs, out_specs=out_specs, out_shape=outs,...  36.3 us
    ppermute x20, starting transfers between devices, exchanged(): return lax.ppermute(array, 'dp', [(i, i ^ mask) for i in range(count)])  16.3 us
    ppermute x20, waiting for transfers between devices, exchanged(): return lax.ppermute(array, 'dp', [(i, i ^ mask) for i in range(count)])  9.91 us
    ppermute x3, starting transfers between devices, from_next_section(): return lax.ppermute(array, ('dp', 'section'), pairs)  4.03 us
    ppermute x3, waiting for transfers between devices, from_next_section(): return lax.ppermute(array, ('dp', 'section'), pairs)  3.65 us
  transfers between devices with their start and end apart: 23, of which 9 were waited for; matrix products, arithmetic and copies ran while one was open for 0% of the time, Pallas kernels for 26%

profile of v3, /device:TPU:0, one launch (start us, length us, event | category | flops | bytes accessed | tf_op | source)
XLA Modules:
  0.0 71.3 jit_solution(17089660777949412519)
XLA Ops:
  0.6 1.3 %shard_map.111 = (bf16[2,8,1536]{2,1,0:T(8,128)(2,1)S(1)}, bf16[2,8,1536]{2,1,0:T(8,128)(2,1)S(1)}, bf16[8,6144]{1,0:T(8,128)(2,1)S(1)}) custom-call(s32[2,2,6]{2,1,0:T(2,128)} %bitcast.22, s32[8]{0:T(128)} %counts_ref.1, bf16[6,2,6144]{2,1,0:T(2,128)(2,1)} %bitcast.30, bf16[6,6144]{1,0:T(8,128)(2,1)} %bitcast.20), custom_call_target="tpu_custom_call" | custom-call | bytes 4194304 | tf_op jit(solution)/shard_map/pallas_call | solution.py:66
  2.5 1.3 %collective-permute-start.4 = (bf16[8,6144]{1,0:T(8,128)(2,1)S(1)}, bf16[8,6144]{1,0:T(8,128)(2,1)S(1)}, u32[]{:S(2)}, u32[]{:S(2)}) collective-permute-start(bf16[8,6144]{1,0:T(8,128)(2,1)S(1)} %get-tuple-element.67), channel_id=1, source_target_pairs={{1,0},{2,1},{3,2},{5,4},{6,5},{7,6},{9,8},{10,9},{11,10},{13,12},{... | collective-permute-start | bytes 294920 | tf_op jit(solution)/shard_map/ppermute | solution.py:134
  3.8 2.6 %collective-permute-start.2 = (bf16[2,8,1536]{2,1,0:T(8,128)(2,1)S(1)}, bf16[2,8,1536]{2,1,0:T(8,128)(2,1)S(1)}, u32[]{:S(2)}, u32[]{:S(2)}) collective-permute-start(bf16[2,8,1536]{2,1,0:T(8,128)(2,1)S(1)} %pad_maximum_fusion.refs_0_), channel_id=1, source_target_pairs={{0,16},{4,20},{8,24},{12,28},{16,0},{20,4},{24,8},{28,12},{1,17},{... | collective-permute-start | bytes 147464 | tf_op jit(solution)/shard_map/ppermute | solution.py:122
  6.4 1.4 %collective-permute-start.3 = (bf16[2,8,1536]{2,1,0:T(8,128)(2,1)S(1)}, bf16[2,8,1536]{2,1,0:T(8,128)(2,1)S(1)}, u32[]{:S(2)}, u32[]{:S(2)}) collective-permute-start(bf16[2,8,1536]{2,1,0:T(8,128)(2,1)S(1)} %pad_maximum_fusion.1), channel_id=1, source_target_pairs={{0,24},{4,28},{8,16},{12,20},{16,8},{20,12},{24,0},{28,4},{1,25},{... | collective-permute-start | bytes 147464 | tf_op jit(solution)/shard_map/ppermute | solution.py:122
  8.0 4.6 %shard_map.112.refs_4_.w1_ref = bf16[1536,4096]{1,0:T(8,128)(2,1)S(1)} custom-call(bf16[1536,4096]{1,0:T(8,128)(2,1)} %bitcast.26), custom_call_target="tpu_custom_call" | custom-call | bytes 12582912 | tf_op jit(solution)/shard_map/pallas_call | solution.py:66
  12.6 7.4 %shard_map.113 = (bf16[32,1536]{1,0:T(8,128)(2,1)S(1)}, bf16[16,1536]{1,0:T(8,128)(2,1)S(1)}, f32[48,2176]{1,0:T(8,128)S(1)}, f32[48,2176]{1,0:T(8,128)S(1)}, bf...) custom-call(bf16[2,8,1536]{2,1,0:T(8,128)(2,1)S(1)} %pad_maximum_fusion.refs_0_, ...), custom_call_target="tpu_custom_call" | custom-call | flops 603979776 | bytes 25165824 | tf_op jit(solution)/shard_map/pallas_call | solution.py:66
  21.9 1.9 %collective-permute-start.6 = (bf16[32,2176]{1,0:T(8,128)(2,1)S(1)}, bf16[32,2176]{1,0:T(8,128)(2,1)S(1)}, u32[]{:S(2)}, u32[]{:S(2)}) collective-permute-start(bf16[32,2176]{1,0:T(8,128)(2,1)S(1)} %get-tuple-element.82), channel_id=1, source_target_pairs={{0,8},{4,12},{8,0},{12,4},{16,24},{20,28},{24,16},{28,20},{1,9},{5... | collective-permute-start | bytes 417800 | tf_op jit(solution)/shard_map/ppermute | solution.py:122
  23.8 1.2 %collective-permute-done.7.handed_ref = bf16[2,8,1536]{2,1,0:T(8,128)(2,1)S(1)} collective-permute-done((bf16[2,8,1536]{2,1,0:T(8,128)(2,1)S(1)}, bf16[2,8,1536]{2,1,0:T(8,128)(2,1)S(1)}, u32[]{:S(2)}, u32[]{:S(2)}) %collective-permute-start.7) | collective-permute-done | bytes 49184 | tf_op jit(solution)/shard_map/ppermute | solution.py:122
  25.3 3.7 %collective-permute-done.8.beside_ref = bf16[8,1536]{1,0:T(8,128)(2,1)S(1)} collective-permute-done((bf16[8,1536]{1,0:T(8,128)(2,1)S(1)}, bf16[8,1536]{1,0:T(8,128)(2,1)S(1)}, u32[]{:S(2)}, u32[]{:S(2)}) %collective-permute-start.8) | collective-permute-done | bytes 24608 | tf_op jit(solution)/shard_map/ppermute | solution.py:122
  29.3 1.3 %collective-permute-done.9.pair_ref.refs_1_ = bf16[16,4224]{1,0:T(8,128)(2,1)S(1)} collective-permute-done((bf16[16,4224]{1,0:T(8,128)(2,1)S(1)}, bf16[16,4224]{1,0:T(8,128)(2,1)S(1)}, u32[]{:S(2)}, u32[]{:S(2)}) %collective-permute-start.9) | collective-permute-done | bytes 135200 | tf_op jit(solution)/shard_map/ppermute | solution.py:122
  30.7 3.4 %shard_map.118 = (bf16[16,1536]{1,0:T(8,128)(2,1)S(1)}, f32[16,128]{1,0:T(8,128)S(1)}) custom-call(bf16[16,4224]{1,0:T(8,128)(2,1)S(1)} %get-tuple-element.87.own_ref.refs_0_, bf16[16,4224]{1,0:T(8,128)(2,1)S(1)} %collective-permute-done.9.pair_ref.refs_1_, f32[16,128]{1,0:T(8,128)S(1)} %get-tuple-element.88.block_ref, ...), custom_call_target="tpu_custom_call" | custom-call | flops 201326592 | bytes 12582912 | tf_op jit(solution)/shard_map/pallas_call | solution.py:66
  34.0 1.6 %collective-permute-start.10 = (bf16[16,1536]{1,0:T(8,128)(2,1)S(1)}, bf16[16,1536]{1,0:T(8,128)(2,1)S(1)}, u32[]{:S(2)}, u32[]{:S(2)}) collective-permute-start(bf16[16,1536]{1,0:T(8,128)(2,1)S(1)} %shard_map.119.refs_0_), channel_id=1, source_target_pairs={{0,16},{4,20},{8,24},{12,28},{16,0},{20,4},{24,8},{28,12},{1,17},{... | collective-permute-start | bytes 147464 | tf_op jit(solution)/shard_map/ppermute | solution.py:122
  35.6 1.3 %collective-permute-start.12 = (bf16[16,1536]{1,0:T(8,128)(2,1)S(1)}, bf16[16,1536]{1,0:T(8,128)(2,1)S(1)}, u32[]{:S(2)}, u32[]{:S(2)}) collective-permute-start(bf16[16,1536]{1,0:T(8,128)(2,1)S(1)} %get-tuple-element.96.dx0_ref), channel_id=1, source_target_pairs={{1,16},{2,17},{3,18},{5,20},{6,21},{7,22},{9,24},{10,25},{11,26},{... | collective-permute-start | bytes 147464 | tf_op jit(solution)/shard_map/ppermute | solution.py:134
  36.9 1.5 %collective-permute-start.11 = (bf16[16,1536]{1,0:T(8,128)(2,1)S(1)}, bf16[16,1536]{1,0:T(8,128)(2,1)S(1)}, u32[]{:S(2)}, u32[]{:S(2)}) collective-permute-start(bf16[16,1536]{1,0:T(8,128)(2,1)S(1)} %get-tuple-element.96.dx0_ref), channel_id=1, source_target_pairs={{1,0},{2,1},{3,2},{5,4},{6,5},{7,6},{9,8},{10,9},{11,10},{13,12},{... | collective-permute-start | bytes 147464 | tf_op jit(solution)/shard_map/ppermute | solution.py:134
  40.5 2.0 %collective-permute-done.12.refs_3_ = bf16[16,1536]{1,0:T(8,128)(2,1)S(1)} collective-permute-done((bf16[16,1536]{1,0:T(8,128)(2,1)S(1)}, bf16[16,1536]{1,0:T(8,128)(2,1)S(1)}, u32[]{:S(2)}, u32[]{:S(2)}) %collective-permute-start.12) | collective-permute-done | bytes 49184 | tf_op jit(solution)/shard_map/ppermute | solution.py:134
  42.5 1.7 %collective-permute-done.11.refs_2_.next_ref = bf16[16,1536]{1,0:T(8,128)(2,1)S(1)} collective-permute-done((bf16[16,1536]{1,0:T(8,128)(2,1)S(1)}, bf16[16,1536]{1,0:T(8,128)(2,1)S(1)}, u32[]{:S(2)}, u32[]{:S(2)}) %collective-permute-start.11) | collective-permute-done | bytes 49184 | tf_op jit(solution)/shard_map/ppermute | solution.py:134
  44.2 3.6 %shard_map.120 = (bf16[16,1536]{1,0:T(8,128)(2,1)S(1)}, f32[16,2048]{1,0:T(8,128)S(1)}, f32[16,2048]{1,0:T(8,128)S(1)}) custom-call(bf16[16,1536]{1,0:T(8,128)(2,1)S(1)} %shard_map.119.refs_0_, bf16[16,1536]{1,0:T(8,128)(2,1)S(1)} %collective-permute-done.10.refs_1_, bf16[16,1536]{1,0:T(8,128)(2,1)S(1)} %collective-permute-done.11.refs_2_.next_ref, ...), custom_call_target="tpu_custom_call" | custom-call | flops 201326592 | bytes 12582912 | tf_op jit(solution)/shard_map/pallas_call | solution.py:66
  50.4 3.6 %shard_map.122 = (bf16[4096,1536]{1,0:T(8,128)(2,1)}, bf16[2048,1536]{1,0:T(8,128)(2,1)S(1)}) custom-call(bf16[16,4224]{1,0:T(8,128)(2,1)S(1)} %get-tuple-element.87.own_ref.refs_0_, bf16[16,4224]{1,0:T(8,128)(2,1)S(1)} %collective-permute-done.9.pair_ref.refs_1_, bf16[16,2048]{1,0:T(8,128)(2,1)S(1)} %get-tuple-element.105.refs_2_, ...), custom_call_target="tpu_custom_call" | custom-call | flops 402653184 | bytes 6291456 | tf_op jit(solution)/shard_map/pallas_call | solution.py:66
  54.2 1.2 %collective-permute-done.18.pair_ref.refs_3_ = bf16[16,2176]{1,0:T(8,128)(2,1)S(1)} collective-permute-done((bf16[16,2176]{1,0:T(8,128)(2,1)S(1)}, bf16[16,2176]{1,0:T(8,128)(2,1)S(1)}, u32[]{:S(2)}, u32[]{:S(2)}) %collective-permute-start.18) | collective-permute-done | bytes 69664 | tf_op jit(solution)/shard_map/ppermute | solution.py:122
  55.4 3.7 %shard_map.124 = (bf16[4096,1536]{1,0:T(8,128)(2,1)}, bf16[4,16,1536]{2,1,0:T(8,128)(2,1)S(1)}, bf16[4,16,1536]{2,1,0:T(8,128)(2,1)S(1)}) custom-call(bf16[16,2176]{1,0:T(8,128)(2,1)S(1)} %get-tuple-element.111.own_ref.refs_2_, bf16[16,2176]{1,0:T(8,128)(2,1)S(1)} %collective-permute-done.18.pair_ref.refs_3_, ...), custom_call_target="tpu_custom_call", output_to_operand_aliasing={{0}: (11, {})} | custom-call | flops 201326592 | bytes 12582912 | tf_op jit(solution)/shard_map/pallas_call | solution.py:66
  59.4 1.3 %collective-permute-done.19.handed_ref = bf16[4,16,1536]{2,1,0:T(8,128)(2,1)S(1)} collective-permute-done((bf16[4,16,1536]{2,1,0:T(8,128)(2,1)S(1)}, bf16[4,16,1536]{2,1,0:T(8,128)(2,1)S(1)}, u32[]{:S(2)}, u32[]{:S(2)}) %collective-permute-start.19) | collective-permute-done | bytes 196640 | tf_op jit(solution)/shard_map/ppermute | solution.py:122
  62.6 1.7 %collective-permute-start.22 = (bf16[2,16,1536]{2,1,0:T(8,128)(2,1)S(1)}, bf16[2,16,1536]{2,1,0:T(8,128)(2,1)S(1)}, u32[]{:S(2)}, u32[]{:S(2)}) collective-permute-start(bf16[2,16,1536]{2,1,0:T(8,128)(2,1)S(1)} %get-tuple-element.122), channel_id=1, source_target_pairs={{0,24},{4,28},{8,16},{12,20},{16,8},{20,12},{24,0},{28,4},{1,25},{... | collective-permute-start | bytes 294920 | tf_op jit(solution)/shard_map/ppermute | solution.py:122
  64.3 5.3 %shard_map.127 = bf16[1536,4096]{1,0:T(8,128)(2,1)} custom-call(bf16[16,4224]{1,0:T(8,128)(2,1)S(1)} %get-tuple-element.87.own_ref.refs_0_, bf16[16,4224]{1,0:T(8,128)(2,1)S(1)} %collective-permute-done.9.pair_ref.refs_1_, bf16[16,2176]{1,0:T(8,128)(2,1)S(1)} %get-tuple-element.111.own_ref.refs_2_, ...), custom_call_target="tpu_custom_call" | custom-call | flops 402653184 | bytes 12582912 | tf_op jit(solution)/shard_map/pallas_call | solution.py:66
  69.6 1.7 %shard_map.126 = (bf16[6,2,6144]{2,1,0:T(2,128)(2,1)}, f32[8,6144]{1,0:T(8,128)}) custom-call(s32[2,2,6]{2,1,0:T(2,128)S(1)} %bitcast.24, s32[8]{0:T(128)S(1)} %copy-done.3, bf16[6,6144]{1,0:T(8,128)(2,1)S(1)} %bitcast.21, bf16[8,6144]{1,0:T(8,128)(2,1)S(1)} %collective-permute-done.4.onward_ref, bf16[6,6144]{1,0:T(8,128)(2,1)S(1)} %copy-done.1, ...), custom_call_target="tpu_custom_call" | custom-call | tf_op jit(solution)/shard_map/pallas_call | solution.py:66
  (54 shorter events, 10.2 us)
Async XLA Ops:
  1.9 1.8 %collective-permute-start = (bf16[2,8,1536]{2,1,0:T(8,128)(2,1)S(1)}, bf16[2,8,1536]{2,1,0:T(8,128)(2,1)S(1)}, u32[]{:S(2)}, u32[]{:S(2)}) collective-permute-start(bf16[2,8,1536]{2,1,0:T(8,128)(2,1)S(1)} %get-tuple-element.66), channel_id=1, source_target_pairs={{0,4},{4,0},{8,12},{12,8},{16,20},{20,16},{24,28},{28,24},{1,5},{5... | collective-permute-start | bytes 147464 | tf_op jit(solution)/shard_map/ppermute | solution.py:122
  2.5 10.2 %collective-permute-start.4 = (bf16[8,6144]{1,0:T(8,128)(2,1)S(1)}, bf16[8,6144]{1,0:T(8,128)(2,1)S(1)}, u32[]{:S(2)}, u32[]{:S(2)}) collective-permute-start(bf16[8,6144]{1,0:T(8,128)(2,1)S(1)} %get-tuple-element.67), channel_id=1, source_target_pairs={{1,0},{2,1},{3,2},{5,4},{6,5},{7,6},{9,8},{10,9},{11,10},{13,12},{... | collective-permute-start | bytes 294920 | tf_op jit(solution)/shard_map/ppermute | solution.py:134
  3.8 8.8 %collective-permute-start.2 = (bf16[2,8,1536]{2,1,0:T(8,128)(2,1)S(1)}, bf16[2,8,1536]{2,1,0:T(8,128)(2,1)S(1)}, u32[]{:S(2)}, u32[]{:S(2)}) collective-permute-start(bf16[2,8,1536]{2,1,0:T(8,128)(2,1)S(1)} %pad_maximum_fusion.refs_0_), channel_id=1, source_target_pairs={{0,16},{4,20},{8,24},{12,28},{16,0},{20,4},{24,8},{28,12},{1,17},{... | collective-permute-start | bytes 147464 | tf_op jit(solution)/shard_map/ppermute | solution.py:122
  6.4 6.2 %collective-permute-start.3 = (bf16[2,8,1536]{2,1,0:T(8,128)(2,1)S(1)}, bf16[2,8,1536]{2,1,0:T(8,128)(2,1)S(1)}, u32[]{:S(2)}, u32[]{:S(2)}) collective-permute-start(bf16[2,8,1536]{2,1,0:T(8,128)(2,1)S(1)} %pad_maximum_fusion.1), channel_id=1, source_target_pairs={{0,24},{4,28},{8,16},{12,20},{16,8},{20,12},{24,0},{28,4},{1,25},{... | collective-permute-start | bytes 147464 | tf_op jit(solution)/shard_map/ppermute | solution.py:122
  7.8 4.8 %collective-permute-start.1 = (bf16[2,8,1536]{2,1,0:T(8,128)(2,1)S(1)}, bf16[2,8,1536]{2,1,0:T(8,128)(2,1)S(1)}, u32[]{:S(2)}, u32[]{:S(2)}) collective-permute-start(bf16[2,8,1536]{2,1,0:T(8,128)(2,1)S(1)} %pad_maximum_fusion.1), channel_id=1, source_target_pairs={{0,8},{4,12},{8,0},{12,4},{16,24},{20,28},{24,16},{28,20},{1,9},{5... | collective-permute-start | bytes 147464 | tf_op jit(solution)/shard_map/ppermute | solution.py:122
  20.0 1.8 %collective-permute-start.5 = (f32[48,2176]{1,0:T(8,128)S(1)}, f32[48,2176]{1,0:T(8,128)S(1)}, u32[]{:S(2)}, u32[]{:S(2)}) collective-permute-start(f32[48,2176]{1,0:T(8,128)S(1)} %get-tuple-element.76), channel_id=1, source_target_pairs={{0,4},{4,0},{8,12},{12,8},{16,20},{20,16},{24,28},{28,24},{1,5},{5... | collective-permute-start | bytes 1253384 | tf_op jit(solution)/shard_map/ppermute | solution.py:122
  21.9 7.1 %collective-permute-start.6 = (bf16[32,2176]{1,0:T(8,128)(2,1)S(1)}, bf16[32,2176]{1,0:T(8,128)(2,1)S(1)}, u32[]{:S(2)}, u32[]{:S(2)}) collective-permute-start(bf16[32,2176]{1,0:T(8,128)(2,1)S(1)} %get-tuple-element.82), channel_id=1, source_target_pairs={{0,8},{4,12},{8,0},{12,4},{16,24},{20,28},{24,16},{28,20},{1,9},{5... | collective-permute-start | bytes 417800 | tf_op jit(solution)/shard_map/ppermute | solution.py:122
  23.8 1.2 %collective-permute-start.7 = (bf16[2,8,1536]{2,1,0:T(8,128)(2,1)S(1)}, bf16[2,8,1536]{2,1,0:T(8,128)(2,1)S(1)}, u32[]{:S(2)}, u32[]{:S(2)}) collective-permute-start(bf16[2,8,1536]{2,1,0:T(8,128)(2,1)S(1)} %get-tuple-element.84), channel_id=1, source_target_pairs={{0,4},{4,0},{8,12},{12,8},{16,20},{20,16},{24,28},{28,24},{1,5},{5... | collective-permute-start | bytes 147464 | tf_op jit(solution)/shard_map/ppermute | solution.py:122
  25.1 3.9 %collective-permute-start.8 = (bf16[8,1536]{1,0:T(8,128)(2,1)S(1)}, bf16[8,1536]{1,0:T(8,128)(2,1)S(1)}, u32[]{:S(2)}, u32[]{:S(2)}) collective-permute-start(bf16[8,1536]{1,0:T(8,128)(2,1)S(1)} %get-tuple-element.85), channel_id=1, source_target_pairs={{0,8},{4,12},{8,0},{12,4},{16,24},{20,28},{24,16},{28,20},{1,9},{5... | collective-permute-start | bytes 73736 | tf_op jit(solution)/shard_map/ppermute | solution.py:122
  29.2 1.4 %collective-permute-start.9 = (bf16[16,4224]{1,0:T(8,128)(2,1)S(1)}, bf16[16,4224]{1,0:T(8,128)(2,1)S(1)}, u32[]{:S(2)}, u32[]{:S(2)}) collective-permute-start(bf16[16,4224]{1,0:T(8,128)(2,1)S(1)} %get-tuple-element.87.own_ref.refs_0_), channel_id=1, source_target_pairs={{0,4},{4,0},{8,12},{12,8},{16,20},{20,16},{24,28},{28,24},{1,5},{5... | collective-permute-start | bytes 405512 | tf_op jit(solution)/shard_map/ppermute | solution.py:122
  34.0 6.5 %collective-permute-start.10 = (bf16[16,1536]{1,0:T(8,128)(2,1)S(1)}, bf16[16,1536]{1,0:T(8,128)(2,1)S(1)}, u32[]{:S(2)}, u32[]{:S(2)}) collective-permute-start(bf16[16,1536]{1,0:T(8,128)(2,1)S(1)} %shard_map.119.refs_0_), channel_id=1, source_target_pairs={{0,16},{4,20},{8,24},{12,28},{16,0},{20,4},{24,8},{28,12},{1,17},{... | collective-permute-start | bytes 147464 | tf_op jit(solution)/shard_map/ppermute | solution.py:122
  35.6 6.9 %collective-permute-start.12 = (bf16[16,1536]{1,0:T(8,128)(2,1)S(1)}, bf16[16,1536]{1,0:T(8,128)(2,1)S(1)}, u32[]{:S(2)}, u32[]{:S(2)}) collective-permute-start(bf16[16,1536]{1,0:T(8,128)(2,1)S(1)} %get-tuple-element.96.dx0_ref), channel_id=1, source_target_pairs={{1,16},{2,17},{3,18},{5,20},{6,21},{7,22},{9,24},{10,25},{11,26},{... | collective-permute-start | bytes 147464 | tf_op jit(solution)/shard_map/ppermute | solution.py:134
  36.9 7.2 %collective-permute-start.11 = (bf16[16,1536]{1,0:T(8,128)(2,1)S(1)}, bf16[16,1536]{1,0:T(8,128)(2,1)S(1)}, u32[]{:S(2)}, u32[]{:S(2)}) collective-permute-start(bf16[16,1536]{1,0:T(8,128)(2,1)S(1)} %get-tuple-element.96.dx0_ref), channel_id=1, source_target_pairs={{1,0},{2,1},{3,2},{5,4},{6,5},{7,6},{9,8},{10,9},{11,10},{13,12},{... | collective-permute-start | bytes 147464 | tf_op jit(solution)/shard_map/ppermute | solution.py:134
  38.4 9.4 %collective-permute-start.14 = (bf16[16,1152]{1,0:T(8,128)(2,1)S(1)}, bf16[16,1152]{1,0:T(8,128)(2,1)S(1)}, u32[]{:S(2)}, u32[]{:S(2)}) collective-permute-start(bf16[16,1152]{1,0:T(8,128)(2,1)S(1)} %slice.23), channel_id=1, source_target_pairs={{0,8},{4,12},{8,0},{12,4},{16,24},{20,28},{24,16},{28,20},{1,9},{5... | collective-permute-start | bytes 110600 | tf_op jit(solution)/shard_map/ppermute | solution.py:122
  39.6 8.2 %collective-permute-start.13 = (bf16[16,1024]{1,0:T(8,128)(2,1)S(1)}, bf16[16,1024]{1,0:T(8,128)(2,1)S(1)}, u32[]{:S(2)}, u32[]{:S(2)}) collective-permute-start(bf16[16,1024]{1,0:T(8,128)(2,1)S(1)} %slice.22), channel_id=1, source_target_pairs={{0,8},{4,12},{8,0},{12,4},{16,24},{20,28},{24,16},{28,20},{1,9},{5... | collective-permute-start | bytes 98312 | tf_op jit(solution)/shard_map/ppermute | solution.py:122
  47.8 1.4 %collective-permute-start.15 = (f32[16,2048]{1,0:T(8,128)S(1)}, f32[16,2048]{1,0:T(8,128)S(1)}, u32[]{:S(2)}, u32[]{:S(2)}) collective-permute-start(f32[16,2048]{1,0:T(8,128)S(1)} %get-tuple-element.104), channel_id=1, source_target_pairs={{0,4},{4,0},{8,12},{12,8},{16,20},{20,16},{24,28},{28,24},{1,5},{5... | collective-permute-start | bytes 393224 | tf_op jit(solution)/shard_map/ppermute | solution.py:122
  48.1 2.3 %collective-permute-start.17 = (bf16[16,2048]{1,0:T(8,128)(2,1)S(1)}, bf16[16,2048]{1,0:T(8,128)(2,1)S(1)}, u32[]{:S(2)}, u32[]{:S(2)}) collective-permute-start(bf16[16,2048]{1,0:T(8,128)(2,1)S(1)} %get-tuple-element.105.refs_2_), channel_id=1, source_target_pairs={{0,4},{4,0},{8,12},{12,8},{16,20},{20,16},{24,28},{28,24},{1,5},{5... | collective-permute-start | bytes 196616 | tf_op jit(solution)/shard_map/ppermute | solution.py:122
  49.3 4.7 %collective-permute-start.16 = (bf16[16,2048]{1,0:T(8,128)(2,1)S(1)}, bf16[16,2048]{1,0:T(8,128)(2,1)S(1)}, u32[]{:S(2)}, u32[]{:S(2)}) collective-permute-start(bf16[16,2048]{1,0:T(8,128)(2,1)S(1)} %get-tuple-element.126), channel_id=1, source_target_pairs={{0,8},{4,12},{8,0},{12,4},{16,24},{20,28},{24,16},{28,20},{1,9},{5... | collective-permute-start | bytes 196616 | tf_op jit(solution)/shard_map/ppermute | solution.py:122
  54.1 1.3 %collective-permute-start.18 = (bf16[16,2176]{1,0:T(8,128)(2,1)S(1)}, bf16[16,2176]{1,0:T(8,128)(2,1)S(1)}, u32[]{:S(2)}, u32[]{:S(2)}) collective-permute-start(bf16[16,2176]{1,0:T(8,128)(2,1)S(1)} %get-tuple-element.111.own_ref.refs_2_), channel_id=1, source_target_pairs={{0,4},{4,0},{8,12},{12,8},{16,20},{20,16},{24,28},{28,24},{1,5},{5... | collective-permute-start | bytes 208904 | tf_op jit(solution)/shard_map/ppermute | solution.py:122
  59.2 10.4 %copy-start = (bf16[1,6,6144]{2,1,0:T(8,128)(2,1)S(1)}, bf16[1,6,6144]{2,1,0:T(8,128)(2,1)}, u32[]{:S(2)}) copy-start(bf16[1,6,6144]{2,1,0:T(8,128)(2,1)} %param.9) | copy-start | bytes 221188
  59.2 1.5 %collective-permute-start.19 = (bf16[4,16,1536]{2,1,0:T(8,128)(2,1)S(1)}, bf16[4,16,1536]{2,1,0:T(8,128)(2,1)S(1)}, u32[]{:S(2)}, u32[]{:S(2)}) collective-permute-start(bf16[4,16,1536]{2,1,0:T(8,128)(2,1)S(1)} %get-tuple-element.118), channel_id=1, source_target_pairs={{0,4},{4,0},{8,12},{12,8},{16,20},{20,16},{24,28},{28,24},{1,5},{5... | collective-permute-start | bytes 589832 | tf_op jit(solution)/shard_map/ppermute | solution.py:122
  60.7 8.8 %collective-permute-start.20 = (bf16[2,16,1536]{2,1,0:T(8,128)(2,1)S(1)}, bf16[2,16,1536]{2,1,0:T(8,128)(2,1)S(1)}, u32[]{:S(2)}, u32[]{:S(2)}) collective-permute-start(bf16[2,16,1536]{2,1,0:T(8,128)(2,1)S(1)} %get-tuple-element.120), channel_id=1, source_target_pairs={{0,8},{4,12},{8,0},{12,4},{16,24},{20,28},{24,16},{28,20},{1,9},{5... | collective-permute-start | bytes 294920 | tf_op jit(solution)/shard_map/ppermute | solution.py:122
  61.7 7.8 %collective-permute-start.21 = (bf16[2,16,1536]{2,1,0:T(8,128)(2,1)S(1)}, bf16[2,16,1536]{2,1,0:T(8,128)(2,1)S(1)}, u32[]{:S(2)}, u32[]{:S(2)}) collective-permute-start(bf16[2,16,1536]{2,1,0:T(8,128)(2,1)S(1)} %get-tuple-element.121), channel_id=1, source_target_pairs={{0,16},{4,20},{8,24},{12,28},{16,0},{20,4},{24,8},{28,12},{1,17},{... | collective-permute-start | bytes 294920 | tf_op jit(solution)/shard_map/ppermute | solution.py:122
  62.6 7.0 %collective-permute-start.22 = (bf16[2,16,1536]{2,1,0:T(8,128)(2,1)S(1)}, bf16[2,16,1536]{2,1,0:T(8,128)(2,1)S(1)}, u32[]{:S(2)}, u32[]{:S(2)}) collective-permute-start(bf16[2,16,1536]{2,1,0:T(8,128)(2,1)S(1)} %get-tuple-element.122), channel_id=1, source_target_pairs={{0,24},{4,28},{8,16},{12,20},{16,8},{20,12},{24,0},{28,4},{1,25},{... | collective-permute-start | bytes 294920 | tf_op jit(solution)/shard_map/ppermute | solution.py:122
  (3 other events, 31.3 us)

commit v4 on v3

--- a/solution.py
+++ b/solution.py
@@ -94,11 +94,10 @@
         copy.wait()
 
 
-def fetch(weight):
-    def body(source, target, sem):
-        copy = pltpu.make_async_copy(source, target, sem)
-        copy.start()
-        copy.wait()
+def fetch(weight, columns):
+    def body(source, target, sems):
+        pieces = [pl.ds(start, size) for start, size in columns()]
+        wait_all(copy_all([(source.at[:, at], target.at[:, at]) for at in pieces], sems))
 
     return call(
         body,
@@ -107,7 +106,7 @@
         pltpu.VMEM(weight.shape, weight.dtype),
         data=2 * weight.size,
         limit=4,
-        scratch=[pltpu.SemaphoreType.DMA],
+        scratch=[pltpu.SemaphoreType.DMA((SLAB,))],
     )
 
 
@@ -179,7 +178,16 @@
     carried_tok = carried[0]
     ids = routing[0].transpose(0, 2, 1)
     last_section = sections - 1
-    w1 = fetch(w_in[0, 0])
+    step = chunk_of(half, 512)
+    late = half // step // 2 * step
+
+    def early_columns():
+        core = lax.rem(lax.axis_index("dp"), 2)
+        send = pl.multiple_of((1 - core) * half, LANES)
+        keep = pl.multiple_of(core * half, LANES)
+        return [(send, half)] + ([(keep, half - late)] if late < half else [])
+
+    w1 = fetch(w_in[0, 0], early_columns)
 
     def where_am_i():
         return lax.axis_index("section"), lax.axis_index("dp")
@@ -293,15 +301,17 @@
     wide = half + LANES
 
     def first_body(*refs):
-        w1_ref, w2_hbm, router_hbm, xs_ref, ys_ref, keep_ref, send_ref, w2_ref, router_ref, sems = refs[
-            len(came):
-        ]
+        w1_hbm, _, w2_hbm, router_hbm, *refs_out = refs[len(came):]
+        w1_ref, xs_ref, ys_ref, keep_ref, send_ref, w2_ref, router_ref, sems = refs_out
         core = lax.rem(lax.axis_index("dp"), 2)
-        step = chunk_of(half, 512)
         router_copy = pltpu.make_async_copy(
             router_hbm.at[:, quarter_lanes()], router_ref, sems.at[0]
         )
         router_copy.start()
+        late_at = pl.ds(pl.multiple_of(core * half + half - late, LANES), late) if late else None
+        late_copies = copy_all(
+            [(w1_hbm.at[:, late_at], w1_ref.at[:, late_at])] if late else [], sems.at[pl.ds(1, 1)]
+        )
         chunks = [
             (ref, at, pl.multiple_of(which * half + at, LANES))
             for ref, which in ((send_ref, 1 - core), (keep_ref, core))
@@ -309,7 +319,7 @@
         ]
         copies = copy_all(
             [(w2_hbm.at[pl.ds(lane, step)], w2_ref.at[pl.ds(lane, step)]) for _, _, lane in chunks],
-            sems.at[pl.ds(1, len(chunks))],
+            sems.at[pl.ds(2, len(chunks))],
         )
 
         @pl.when(lax.axis_index("dp") >= 0)
@@ -337,7 +347,9 @@
             logits = logits[:, 0:LANES] + logits[:, LANES:2 * LANES] + logits[:, 2 * LANES:3 * LANES]
             zero = jnp.zeros((rows, LANES), F32)
             both = STEPS * rows
-            for ref, at, lane in chunks:
+            for i, (ref, at, lane) in enumerate(chunks):
+                if i == len(chunks) - late // step:
+                    wait_all(late_copies)
                 ref[0:both, at:at + step] = dot(xs, w1_ref[:, pl.ds(lane, step)])
             for ref in (send_ref, keep_ref):
                 ref[0:both, half:wide] = logits
@@ -346,11 +358,12 @@
                 copy.wait()
                 ref[both:both + rows, at:at + step] = dot(ys, w2_ref[pl.ds(lane, step), :], NT)
 
-    xs, ys0, keep, send, w2, router_q = call(
+    w1, xs, ys0, keep, send, w2, router_q = call(
         first_body,
-        (*came, w1, in_hbm(w_out[0, 0]), in_hbm(router_t)),
-        [VMEM] * (len(came) + 1) + [ANY] * 2,
+        (*came, in_hbm(w_in[0, 0]), w1, in_hbm(w_out[0, 0]), in_hbm(router_t)),
+        [VMEM] * len(came) + [ANY, VMEM, ANY, ANY],
         (
+            pltpu.VMEM((part, hidden), BF),
             sds((STEPS * rows, part), BF),
             sds((rows, part), BF),
             sds((3 * rows, wide), F32),
@@ -360,7 +373,8 @@
         ),
         flops=2 * 3 * rows * part * hidden,
         data=2 * part * hidden * 2,
-        scratch=[pltpu.SemaphoreType.DMA((1 + 2 * (half // chunk_of(half, 512)),))],
+        scratch=[pltpu.SemaphoreType.DMA((2 + 2 * (half // step),))],
+        aliases={len(came) + 1: 0},
     )
     send, onward = lax.optimization_barrier((send, onward))
     send_other = permuted(send, 0)
@@ -543,8 +557,9 @@
         data=2 * part * hidden,
     )
     if by_chip:
-        dx0, narrow1, base_four = lax.optimization_barrier((dx0, narrow1, base_four))
-        base = (base_four, exchanged(base_four, 4))
+        base_far = exchanged(base_four, 4)
+        dx0, narrow1, base_far = lax.optimization_barrier((dx0, narrow1, base_far))
+        base = (base_four, base_far)
     else:
         base = (base_whole.reshape(n * used, part),)
     cut = half // 2
@@ -690,13 +705,36 @@
     )
     hid1_pair = permuted(hid1, 0)
 
+    first_rows = part // 2
+
+    def early_in_body(own0, own1, xs_ref, out_ref):
+        dpre = jnp.concatenate([own0[:, 0:half], own1[:, 0:half]], axis=0)
+        rows_at = chunk_of(first_rows, 256)
+        for i in range(0, first_rows, rows_at):
+            out_ref[i:i + rows_at, :] = dot(xs_ref[:, i:i + rows_at], dpre, TN).astype(BF)
+
+    early_in = call(
+        early_in_body,
+        (hid0, hid1, xs),
+        [VMEM] * 3,
+        pltpu.VMEM((first_rows, half), BF),
+        flops=2 * both * first_rows * half,
+        data=2 * first_rows * half,
+    )
+
     back_rows = 2 * SLAB
 
     def dx1_body(
         own_ref, pair_ref, block_ref, prob_ref, dlog0_ref, dx0_ref, next_ref, xs_ref, router_ref, w1_ref, rest_ref, _, *refs
     ):
-        grad_ref, *out_refs, sems = refs
-        copies = copy_rest(rest_ref, grad_ref, sems)
+        early_ref, grad_ref, grad_in_ref, *out_refs, sems = refs
+        copies = copy_rest(rest_ref, grad_ref, sems.at[pl.ds(0, SLAB)])
+        own_lanes = half_lanes(lax.rem(lax.axis_index("dp"), 2))
+        step = first_rows // SLAB
+        some = [pl.ds(i * step, step) for i in range(SLAB)]
+        copies += copy_all(
+            [(early_ref.at[at], grad_in_ref.at[at, own_lanes]) for at in some], sems.at[pl.ds(SLAB, SLAB)]
+        )
 
         @pl.when(lax.axis_index("dp") >= 0)
         def _():
@@ -729,16 +767,16 @@
         wait_all(copies)
 
     back_shapes = (sds((n // 2, back_rows, part), BF),) * 2 if by_chip else (sds((n, back_rows, part), BF),)
-    grad_out, *back_sent = call(
+    grad_out, grad_in, *back_sent = call(
         dx1_body,
-        (hid1, hid1_pair, block1, prob1, dlog0, dx0, next_back, xs, router_q, w1, rest_out, grad_out),
-        [VMEM] * 11 + [ANY],
-        (sds((hidden, part), BF), *back_shapes),
+        (hid1, hid1_pair, block1, prob1, dlog0, dx0, next_back, xs, router_q, w1, rest_out, grad_out, early_in),
+        [VMEM] * 11 + [ANY, VMEM],
+        (sds((hidden, part), BF), sds((part, hidden), BF), *back_shapes),
         flops=2 * rows * part * hidden,
         data=2 * part * hidden,
         limit=12,
-        out_specs=(ANY, *(VMEM for _ in back_shapes)),
-        scratch=[pltpu.SemaphoreType.DMA((SLAB,))],
+        out_specs=(ANY, ANY, *(VMEM for _ in back_shapes)),
+        scratch=[pltpu.SemaphoreType.DMA((2 * SLAB,))],
         aliases={11: 0},
     )
     if by_chip:
@@ -759,17 +797,46 @@
     else:
         back = (lax.all_to_all(back_sent[0], "dp", split_axis=0, concat_axis=0, tiled=True),)
 
-    def grad_in_body(own0, pair0, own1, pair1, xs_ref):
+    def grad_in_body(own0, pair0, own1, pair1, xs_ref, _, out_ref, held_ref, narrow_ref, sems):
         core = lax.rem(lax.axis_index("dp"), 2)
-        a0, b0 = in_order(own0[:, 0:half], pair0[:, 0:half], core)
-        a1, b1 = in_order(own1[:, 0:half], pair1[:, 0:half], core)
-        dpre = jnp.concatenate(
-            [jnp.concatenate([a0, b0], axis=1), jnp.concatenate([a1, b1], axis=1)], axis=0
-        )
-        return xs_ref[...], dpre
-
-    in_args = (hid0, hid0_pair, hid1, hid1_pair, xs)
-    grad_in = outer(grad_in_body, in_args, part, hidden, 0)
+        pair = jnp.concatenate([pair0[:, 0:half], pair1[:, 0:half]], axis=0)
+        own = jnp.concatenate([own0[:, 0:half], own1[:, 0:half]], axis=0)
+        dpre = jnp.concatenate(in_order(own, pair, core), axis=1)
+        step = first_rows // (SLAB // 2)
+        copies = []
+        for i in range(SLAB // 2):
+            begin = i * step
+            narrow_ref[begin:begin + step, :] = dot(xs_ref[:, begin:begin + step], pair, TN).astype(BF)
+            at = pl.ds(begin, step)
+            target = out_ref.at[at, half_lanes(1 - core)]
+            copies += copy_all([(narrow_ref.at[at], target)], sems.at[pl.ds(i, 1)])
+        step = (part - first_rows) // (SLAB // 2)
+        for i in range(SLAB // 2):
+            begin = i * step
+            rows_at = first_rows + begin
+            held_ref[begin:begin + step, :] = dot(
+                xs_ref[:, rows_at:rows_at + step], dpre, TN
+            ).astype(BF)
+            pair_of = (held_ref.at[pl.ds(begin, step)], out_ref.at[pl.ds(rows_at, step)])
+            copies += copy_all([pair_of], sems.at[pl.ds(SLAB // 2 + i, 1)])
+        wait_all(copies)
+
+    grad_in = call(
+        grad_in_body,
+        (hid0, hid0_pair, hid1, hid1_pair, xs, grad_in),
+        [VMEM] * 5 + [ANY],
+        sds((part, hidden), BF),
+        flops=2 * both * part * hidden,
+        data=2 * part * hidden,
+        limit=16,
+        out_specs=ANY,
+        scratch=[
+            pltpu.VMEM((part - first_rows, hidden), BF),
+            pltpu.VMEM((first_rows, half), BF),
+            pltpu.SemaphoreType.DMA((SLAB,)),
+        ],
+        aliases={5: 0},
+    )
 
     def final_body(ids_ref, counts_ref, dy_ref, onward_ref, head_ref, *refs):
         back_refs, (out_ref, router_out_ref) = refs[:-2], refs[-2:]

time: 71.6 us -> 68.8 us (0.961)
  waiting for transfers between devices: 13.6 us -> 11.3 us
    ppermute x20, waiting for transfers between devices: 9.91 us -> 7.55 us  [exchanged(): return lax.ppermute(array, 'dp', [(i, i ^ mask) for i in range(count)])]
    pallas_call x17 -> x18, Pallas kernels: 36.3 us -> 35.7 us  [call(): pl.pallas_call(body, in_specs=specs, out_specs=out_specs, out_shape=outs,...]
  transfers between devices with their start and end apart: 23 -> 23, of which waited for: 9 -> 10; matrix products, arithmetic and copies ran while one was open for 0% -> 0% of each run, Pallas kernels for 26% -> 31%
where the time goes in v4:
time: 68.8 us; the launch traced here: 68.4 us
  Pallas kernels  35.7 us (52%)
  starting transfers between devices  20.5 us (30%)
  waiting for transfers between devices  11.3 us (16%)
  between operations  0.93 us (1%)
    pallas_call x18, Pallas kernels, call(): pl.pallas_call(body, in_specs=specs, out_specs=out_specs, out_shape=outs,...  35.7 us
    ppermute x20, starting transfers between devices, exchanged(): return lax.ppermute(array, 'dp', [(i, i ^ mask) for i in range(count)])  16.4 us
    ppermute x20, waiting for transfers between devices, exchanged(): return lax.ppermute(array, 'dp', [(i, i ^ mask) for i in range(count)])  7.55 us
    ppermute x3, starting transfers between devices, from_next_section(): return lax.ppermute(array, ('dp', 'section'), pairs)  4.04 us
    ppermute x3, waiting for transfers between devices, from_next_section(): return lax.ppermute(array, ('dp', 'section'), pairs)  3.71 us
  transfers between devices with their start and end apart: 23, of which 10 were waited for; matrix products, arithmetic and copies ran while one was open for 0% of the time, Pallas kernels for 31%

profile of v4, /device:TPU:0, one launch (start us, length us, event | category | flops | bytes accessed | tf_op | source)
XLA Modules:
  0.0 68.4 jit_solution(14911908079637698692)
XLA Ops:
  0.6 1.3 %shard_map.111 = (bf16[2,8,1536]{2,1,0:T(8,128)(2,1)S(1)}, bf16[2,8,1536]{2,1,0:T(8,128)(2,1)S(1)}, bf16[8,6144]{1,0:T(8,128)(2,1)S(1)}) custom-call(s32[2,2,6]{2,1,0:T(2,128)} %bitcast.22, s32[8]{0:T(128)} %counts_ref.1, bf16[6,2,6144]{2,1,0:T(2,128)(2,1)} %bitcast.31, bf16[6,6144]{1,0:T(8,128)(2,1)} %bitcast.20), custom_call_target="tpu_custom_call" | custom-call | bytes 4194304 | tf_op jit(solution)/shard_map/pallas_call | solution.py:66
  2.5 1.3 %collective-permute-start.4 = (bf16[8,6144]{1,0:T(8,128)(2,1)S(1)}, bf16[8,6144]{1,0:T(8,128)(2,1)S(1)}, u32[]{:S(2)}, u32[]{:S(2)}) collective-permute-start(bf16[8,6144]{1,0:T(8,128)(2,1)S(1)} %get-tuple-element.69), channel_id=1, source_target_pairs={{1,0},{2,1},{3,2},{5,4},{6,5},{7,6},{9,8},{10,9},{11,10},{13,12},{... | collective-permute-start | bytes 294920 | tf_op jit(solution)/shard_map/ppermute | solution.py:133
  3.8 2.6 %collective-permute-start.2 = (bf16[2,8,1536]{2,1,0:T(8,128)(2,1)S(1)}, bf16[2,8,1536]{2,1,0:T(8,128)(2,1)S(1)}, u32[]{:S(2)}, u32[]{:S(2)}) collective-permute-start(bf16[2,8,1536]{2,1,0:T(8,128)(2,1)S(1)} %pad_maximum_fusion.refs_0_), channel_id=1, source_target_pairs={{0,16},{4,20},{8,24},{12,28},{16,0},{20,4},{24,8},{28,12},{1,17},{... | collective-permute-start | bytes 147464 | tf_op jit(solution)/shard_map/ppermute | solution.py:121
  6.4 1.4 %collective-permute-start.3 = (bf16[2,8,1536]{2,1,0:T(8,128)(2,1)S(1)}, bf16[2,8,1536]{2,1,0:T(8,128)(2,1)S(1)}, u32[]{:S(2)}, u32[]{:S(2)}) collective-permute-start(bf16[2,8,1536]{2,1,0:T(8,128)(2,1)S(1)} %pad_maximum_fusion.1), channel_id=1, source_target_pairs={{0,24},{4,28},{8,16},{12,20},{16,8},{20,12},{24,0},{28,4},{1,25},{... | collective-permute-start | bytes 147464 | tf_op jit(solution)/shard_map/ppermute | solution.py:121
  8.0 3.8 %shard_map.112.refs_5_ = bf16[1536,4096]{1,0:T(8,128)(2,1)S(1)} custom-call(bf16[1536,4096]{1,0:T(8,128)(2,1)} %bitcast.25), custom_call_target="tpu_custom_call" | custom-call | bytes 12582912 | tf_op jit(solution)/shard_map/pallas_call | solution.py:66
  11.9 7.5 %shard_map.113 = (bf16[1536,4096]{1,0:T(8,128)(2,1)S(1)}, bf16[32,1536]{1,0:T(8,128)(2,1)S(1)}, bf16[16,1536]{1,0:T(8,128)(2,1)S(1)}, f32[48,2176]{1,0:T(8,128)S...) custom-call(bf16[2,8,1536]{2,1,0:T(8,128)(2,1)S(1)} %pad_maximum_fus, ...), custom_call_target="tpu_custom_call", output_to_operand_aliasing={{0}: (5, {})} | custom-call | flops 603979776 | bytes 25165824 | tf_op jit(solution)/shard_map/pallas_call | solution.py:66
  21.4 1.8 %collective-permute-start.7 = (bf16[32,2176]{1,0:T(8,128)(2,1)S(1)}, bf16[32,2176]{1,0:T(8,128)(2,1)S(1)}, u32[]{:S(2)}, u32[]{:S(2)}) collective-permute-start(bf16[32,2176]{1,0:T(8,128)(2,1)S(1)} %get-tuple-element.86), channel_id=1, source_target_pairs={{0,8},{4,12},{8,0},{12,4},{16,24},{20,28},{24,16},{28,20},{1,9},{5... | collective-permute-start | bytes 417800 | tf_op jit(solution)/shard_map/ppermute | solution.py:121
  23.2 1.2 %collective-permute-done.6.handed_ref = bf16[2,8,1536]{2,1,0:T(8,128)(2,1)S(1)} collective-permute-done((bf16[2,8,1536]{2,1,0:T(8,128)(2,1)S(1)}, bf16[2,8,1536]{2,1,0:T(8,128)(2,1)S(1)}, u32[]{:S(2)}, u32[]{:S(2)}) %collective-permute-start.6) | collective-permute-done | bytes 49184 | tf_op jit(solution)/shard_map/ppermute | solution.py:121
  24.8 3.6 %collective-permute-done.8.beside_ref = bf16[8,1536]{1,0:T(8,128)(2,1)S(1)} collective-permute-done((bf16[8,1536]{1,0:T(8,128)(2,1)S(1)}, bf16[8,1536]{1,0:T(8,128)(2,1)S(1)}, u32[]{:S(2)}, u32[]{:S(2)}) %collective-permute-start.8) | collective-permute-done | bytes 24608 | tf_op jit(solution)/shard_map/ppermute | solution.py:121
  28.7 1.6 %collective-permute-start.10 = (bf16[16,1536]{1,0:T(8,128)(2,1)S(1)}, bf16[16,1536]{1,0:T(8,128)(2,1)S(1)}, u32[]{:S(2)}, u32[]{:S(2)}) collective-permute-start(bf16[16,1536]{1,0:T(8,128)(2,1)S(1)} %shard_map.117.refs_0_), channel_id=1, source_target_pairs={{0,16},{4,20},{8,24},{12,28},{16,0},{20,4},{24,8},{28,12},{1,17},{... | collective-permute-start | bytes 147464 | tf_op jit(solution)/shard_map/ppermute | solution.py:121
  30.3 3.4 %shard_map.119 = (bf16[16,1536]{1,0:T(8,128)(2,1)S(1)}, f32[16,128]{1,0:T(8,128)S(1)}) custom-call(bf16[16,4224]{1,0:T(8,128)(2,1)S(1)} %get-tuple-element.91.own_ref.refs_0_.own0, bf16[16,4224]{1,0:T(8,128)(2,1)S(1)} %collective-permute-done.9.pair_ref.refs_1_.pair0, f32[16,128]{1,0:T(8,128)S(1)} %get-tuple-element.92.block_ref, ...), custom_call_target="tpu_custom_call" | custom-call | flops 201326592 | bytes 12582912 | tf_op jit(solution)/shard_map/pallas_call | solution.py:66
  33.7 1.3 %collective-permute-start.12 = (bf16[16,1536]{1,0:T(8,128)(2,1)S(1)}, bf16[16,1536]{1,0:T(8,128)(2,1)S(1)}, u32[]{:S(2)}, u32[]{:S(2)}) collective-permute-start(bf16[16,1536]{1,0:T(8,128)(2,1)S(1)} %get-tuple-element.99.dx0_ref), channel_id=1, source_target_pairs={{1,16},{2,17},{3,18},{5,20},{6,21},{7,22},{9,24},{10,25},{11,26},{... | collective-permute-start | bytes 147464 | tf_op jit(solution)/shard_map/ppermute | solution.py:133
  35.0 1.5 %collective-permute-start.11 = (bf16[16,1536]{1,0:T(8,128)(2,1)S(1)}, bf16[16,1536]{1,0:T(8,128)(2,1)S(1)}, u32[]{:S(2)}, u32[]{:S(2)}) collective-permute-start(bf16[16,1536]{1,0:T(8,128)(2,1)S(1)} %get-tuple-element.99.dx0_ref), channel_id=1, source_target_pairs={{1,0},{2,1},{3,2},{5,4},{6,5},{7,6},{9,8},{10,9},{11,10},{13,12},{... | collective-permute-start | bytes 147464 | tf_op jit(solution)/shard_map/ppermute | solution.py:133
  36.5 1.2 %collective-permute-start.14 = (bf16[16,1152]{1,0:T(8,128)(2,1)S(1)}, bf16[16,1152]{1,0:T(8,128)(2,1)S(1)}, u32[]{:S(2)}, u32[]{:S(2)}) collective-permute-start(bf16[16,1152]{1,0:T(8,128)(2,1)S(1)} %slice.23), channel_id=1, source_target_pairs={{0,8},{4,12},{8,0},{12,4},{16,24},{20,28},{24,16},{28,20},{1,9},{5... | collective-permute-start | bytes 110600 | tf_op jit(solution)/shard_map/ppermute | solution.py:121
  38.6 2.4 %collective-permute-done.12.refs_3_ = bf16[16,1536]{1,0:T(8,128)(2,1)S(1)} collective-permute-done((bf16[16,1536]{1,0:T(8,128)(2,1)S(1)}, bf16[16,1536]{1,0:T(8,128)(2,1)S(1)}, u32[]{:S(2)}, u32[]{:S(2)}) %collective-permute-start.12) | collective-permute-done | bytes 49184 | tf_op jit(solution)/shard_map/ppermute | solution.py:133
  41.0 1.3 %collective-permute-done.11.refs_2_.next_ref = bf16[16,1536]{1,0:T(8,128)(2,1)S(1)} collective-permute-done((bf16[16,1536]{1,0:T(8,128)(2,1)S(1)}, bf16[16,1536]{1,0:T(8,128)(2,1)S(1)}, u32[]{:S(2)}, u32[]{:S(2)}) %collective-permute-start.11) | collective-permute-done | bytes 49184 | tf_op jit(solution)/shard_map/ppermute | solution.py:133
  42.3 3.6 %shard_map.120 = (bf16[16,1536]{1,0:T(8,128)(2,1)S(1)}, f32[16,2048]{1,0:T(8,128)S(1)}, f32[16,2048]{1,0:T(8,128)S(1)}) custom-call(bf16[16,1536]{1,0:T(8,128)(2,1)S(1)} %shard_map.117.refs_0_, bf16[16,1536]{1,0:T(8,128)(2,1)S(1)} %collective-permute-done.10.refs_1_, bf16[16,1536]{1,0:T(8,128)(2,1)S(1)} %collective-permute-done.11.refs_2_.next_ref, ...), custom_call_target="tpu_custom_call" | custom-call | flops 201326592 | bytes 12582912 | tf_op jit(solution)/shard_map/pallas_call | solution.py:66
  47.4 1.2 %collective-permute-start.16 = (bf16[16,2048]{1,0:T(8,128)(2,1)S(1)}, bf16[16,2048]{1,0:T(8,128)(2,1)S(1)}, u32[]{:S(2)}, u32[]{:S(2)}) collective-permute-start(bf16[16,2048]{1,0:T(8,128)(2,1)S(1)} %get-tuple-element.130), channel_id=1, source_target_pairs={{0,8},{4,12},{8,0},{12,4},{16,24},{20,28},{24,16},{28,20},{1,9},{5... | collective-permute-start | bytes 196616 | tf_op jit(solution)/shard_map/ppermute | solution.py:121
  48.6 3.6 %shard_map.122 = (bf16[4096,1536]{1,0:T(8,128)(2,1)}, bf16[2048,1536]{1,0:T(8,128)(2,1)S(1)}) custom-call(bf16[16,4224]{1,0:T(8,128)(2,1)S(1)} %get-tuple-element.91.own_ref.refs_0_.own0, bf16[16,4224]{1,0:T(8,128)(2,1)S(1)} %collective-permute-done.9.pair_ref.refs_1_.pair0, bf16[16,2048]{1,0:T(8,128)(2,1)S(1)} %get-tuple-element.108.refs_2_, ...), custom_call_target="tpu_custom_call" | custom-call | flops 402653184 | bytes 6291456 | tf_op jit(solution)/shard_map/pallas_call | solution.py:66
  53.6 3.8 %shard_map.125 = (bf16[4096,1536]{1,0:T(8,128)(2,1)}, bf16[1536,4096]{1,0:T(8,128)(2,1)}, bf16[4,16,1536]{2,1,0:T(8,128)(2,1)S(1)}, bf16[4,16,1536]{2,1,0:T(8,128)(2,1)S(1)}) custom-call(bf16[16,2176]{1,0:T(8,128)(2,1)S(1)} %get-tuple-element.114.own1.own_ref, ...), custom_call_target="tpu_custom_call", output_to_operand_aliasing={{0}: (11, {})} | custom-call | flops 201326592 | bytes 12582912 | tf_op jit(solution)/shard_map/pallas_call | solution.py:66
  59.9 1.2 %collective-permute-start.21 = (bf16[2,16,1536]{2,1,0:T(8,128)(2,1)S(1)}, bf16[2,16,1536]{2,1,0:T(8,128)(2,1)S(1)}, u32[]{:S(2)}, u32[]{:S(2)}) collective-permute-start(bf16[2,16,1536]{2,1,0:T(8,128)(2,1)S(1)} %get-tuple-element.124), channel_id=1, source_target_pairs={{0,16},{4,20},{8,24},{12,28},{16,0},{20,4},{24,8},{28,12},{1,17},{... | collective-permute-start | bytes 294920 | tf_op jit(solution)/shard_map/ppermute | solution.py:121
  61.1 1.4 %collective-permute-start.22 = (bf16[2,16,1536]{2,1,0:T(8,128)(2,1)S(1)}, bf16[2,16,1536]{2,1,0:T(8,128)(2,1)S(1)}, u32[]{:S(2)}, u32[]{:S(2)}) collective-permute-start(bf16[2,16,1536]{2,1,0:T(8,128)(2,1)S(1)} %get-tuple-element.125), channel_id=1, source_target_pairs={{0,24},{4,28},{8,16},{12,20},{16,8},{20,12},{24,0},{28,4},{1,25},{... | collective-permute-start | bytes 294920 | tf_op jit(solution)/shard_map/ppermute | solution.py:121
  62.5 4.1 %shard_map.128 = bf16[1536,4096]{1,0:T(8,128)(2,1)} custom-call(bf16[16,4224]{1,0:T(8,128)(2,1)S(1)} %get-tuple-element.91.own_ref.refs_0_.own0, bf16[16,4224]{1,0:T(8,128)(2,1)S(1)} %collective-permute-done.9.pair_ref.refs_1_.pair0, bf16[16,2176]{1,0:T(8,128)(2,1)S(1)} %get-tuple-element.114.own1.own_ref, ...), custom_call_target="tpu_custom_call", output_to_operand_aliasing={{}: (5, {})} | custom-call | flops 402653184 | bytes 12582912 | tf_op jit(solution)/shard_map/pallas_call | solution.py:66
  66.8 1.7 %shard_map.127 = (bf16[6,2,6144]{2,1,0:T(2,128)(2,1)}, f32[8,6144]{1,0:T(8,128)}) custom-call(s32[2,2,6]{2,1,0:T(2,128)S(1)} %bitcast.24, s32[8]{0:T(128)S(1)} %copy-done.3, bf16[6,6144]{1,0:T(8,128)(2,1)S(1)} %bitcast.21, bf16[8,6144]{1,0:T(8,128)(2,1)S(1)} %collective-permute-done.4.onward_ref, bf16[6,6144]{1,0:T(8,128)(2,1)S(1)} %copy-done.1, ...), custom_call_target="tpu_custom_call" | custom-call | tf_op jit(solution)/shard_map/pallas_call | solution.py:66
  (55 shorter events, 9.8 us)
Async XLA Ops:
  1.9 1.8 %collective-permute-start = (bf16[2,8,1536]{2,1,0:T(8,128)(2,1)S(1)}, bf16[2,8,1536]{2,1,0:T(8,128)(2,1)S(1)}, u32[]{:S(2)}, u32[]{:S(2)}) collective-permute-start(bf16[2,8,1536]{2,1,0:T(8,128)(2,1)S(1)} %get-tuple-element.68), channel_id=1, source_target_pairs={{0,4},{4,0},{8,12},{12,8},{16,20},{20,16},{24,28},{28,24},{1,5},{5... | collective-permute-start | bytes 147464 | tf_op jit(solution)/shard_map/ppermute | solution.py:121
  2.5 9.5 %collective-permute-start.4 = (bf16[8,6144]{1,0:T(8,128)(2,1)S(1)}, bf16[8,6144]{1,0:T(8,128)(2,1)S(1)}, u32[]{:S(2)}, u32[]{:S(2)}) collective-permute-start(bf16[8,6144]{1,0:T(8,128)(2,1)S(1)} %get-tuple-element.69), channel_id=1, source_target_pairs={{1,0},{2,1},{3,2},{5,4},{6,5},{7,6},{9,8},{10,9},{11,10},{13,12},{... | collective-permute-start | bytes 294920 | tf_op jit(solution)/shard_map/ppermute | solution.py:133
  3.8 8.0 %collective-permute-start.2 = (bf16[2,8,1536]{2,1,0:T(8,128)(2,1)S(1)}, bf16[2,8,1536]{2,1,0:T(8,128)(2,1)S(1)}, u32[]{:S(2)}, u32[]{:S(2)}) collective-permute-start(bf16[2,8,1536]{2,1,0:T(8,128)(2,1)S(1)} %pad_maximum_fusion.refs_0_), channel_id=1, source_target_pairs={{0,16},{4,20},{8,24},{12,28},{16,0},{20,4},{24,8},{28,12},{1,17},{... | collective-permute-start | bytes 147464 | tf_op jit(solution)/shard_map/ppermute | solution.py:121
  6.4 5.4 %collective-permute-start.3 = (bf16[2,8,1536]{2,1,0:T(8,128)(2,1)S(1)}, bf16[2,8,1536]{2,1,0:T(8,128)(2,1)S(1)}, u32[]{:S(2)}, u32[]{:S(2)}) collective-permute-start(bf16[2,8,1536]{2,1,0:T(8,128)(2,1)S(1)} %pad_maximum_fusion.1), channel_id=1, source_target_pairs={{0,24},{4,28},{8,16},{12,20},{16,8},{20,12},{24,0},{28,4},{1,25},{... | collective-permute-start | bytes 147464 | tf_op jit(solution)/shard_map/ppermute | solution.py:121
  7.8 4.1 %collective-permute-start.1 = (bf16[2,8,1536]{2,1,0:T(8,128)(2,1)S(1)}, bf16[2,8,1536]{2,1,0:T(8,128)(2,1)S(1)}, u32[]{:S(2)}, u32[]{:S(2)}) collective-permute-start(bf16[2,8,1536]{2,1,0:T(8,128)(2,1)S(1)} %pad_maximum_fusion.1), channel_id=1, source_target_pairs={{0,8},{4,12},{8,0},{12,4},{16,24},{20,28},{24,16},{28,20},{1,9},{5... | collective-permute-start | bytes 147464 | tf_op jit(solution)/shard_map/ppermute | solution.py:121
  19.5 1.8 %collective-permute-start.5 = (f32[48,2176]{1,0:T(8,128)S(1)}, f32[48,2176]{1,0:T(8,128)S(1)}, u32[]{:S(2)}, u32[]{:S(2)}) collective-permute-start(f32[48,2176]{1,0:T(8,128)S(1)} %get-tuple-element.78), channel_id=1, source_target_pairs={{0,4},{4,0},{8,12},{12,8},{16,20},{20,16},{24,28},{28,24},{1,5},{5... | collective-permute-start | bytes 1253384 | tf_op jit(solution)/shard_map/ppermute | solution.py:121
  21.4 7.0 %collective-permute-start.7 = (bf16[32,2176]{1,0:T(8,128)(2,1)S(1)}, bf16[32,2176]{1,0:T(8,128)(2,1)S(1)}, u32[]{:S(2)}, u32[]{:S(2)}) collective-permute-start(bf16[32,2176]{1,0:T(8,128)(2,1)S(1)} %get-tuple-element.86), channel_id=1, source_target_pairs={{0,8},{4,12},{8,0},{12,4},{16,24},{20,28},{24,16},{28,20},{1,9},{5... | collective-permute-start | bytes 417800 | tf_op jit(solution)/shard_map/ppermute | solution.py:121
  23.2 1.2 %collective-permute-start.6 = (bf16[2,8,1536]{2,1,0:T(8,128)(2,1)S(1)}, bf16[2,8,1536]{2,1,0:T(8,128)(2,1)S(1)}, u32[]{:S(2)}, u32[]{:S(2)}) collective-permute-start(bf16[2,8,1536]{2,1,0:T(8,128)(2,1)S(1)} %get-tuple-element.84), channel_id=1, source_target_pairs={{0,4},{4,0},{8,12},{12,8},{16,20},{20,16},{24,28},{28,24},{1,5},{5... | collective-permute-start | bytes 147464 | tf_op jit(solution)/shard_map/ppermute | solution.py:121
  24.5 3.9 %collective-permute-start.8 = (bf16[8,1536]{1,0:T(8,128)(2,1)S(1)}, bf16[8,1536]{1,0:T(8,128)(2,1)S(1)}, u32[]{:S(2)}, u32[]{:S(2)}) collective-permute-start(bf16[8,1536]{1,0:T(8,128)(2,1)S(1)} %get-tuple-element.87), channel_id=1, source_target_pairs={{0,8},{4,12},{8,0},{12,4},{16,24},{20,28},{24,16},{28,20},{1,9},{5... | collective-permute-start | bytes 73736 | tf_op jit(solution)/shard_map/ppermute | solution.py:121
  28.6 1.7 %collective-permute-start.9 = (bf16[16,4224]{1,0:T(8,128)(2,1)S(1)}, bf16[16,4224]{1,0:T(8,128)(2,1)S(1)}, u32[]{:S(2)}, u32[]{:S(2)}) collective-permute-start(bf16[16,4224]{1,0:T(8,128)(2,1)S(1)} %get-tuple-element.91.own_ref.refs_0_.own0), channel_id=1, source_target_pairs={{0,4},{4,0},{8,12},{12,8},{16,20},{20,16},{24,28},{28,24},{1,5},{5... | collective-permute-start | bytes 405512 | tf_op jit(solution)/shard_map/ppermute | solution.py:121
  28.7 5.0 %collective-permute-start.10 = (bf16[16,1536]{1,0:T(8,128)(2,1)S(1)}, bf16[16,1536]{1,0:T(8,128)(2,1)S(1)}, u32[]{:S(2)}, u32[]{:S(2)}) collective-permute-start(bf16[16,1536]{1,0:T(8,128)(2,1)S(1)} %shard_map.117.refs_0_), channel_id=1, source_target_pairs={{0,16},{4,20},{8,24},{12,28},{16,0},{20,4},{24,8},{28,12},{1,17},{... | collective-permute-start | bytes 147464 | tf_op jit(solution)/shard_map/ppermute | solution.py:121
  33.7 7.3 %collective-permute-start.12 = (bf16[16,1536]{1,0:T(8,128)(2,1)S(1)}, bf16[16,1536]{1,0:T(8,128)(2,1)S(1)}, u32[]{:S(2)}, u32[]{:S(2)}) collective-permute-start(bf16[16,1536]{1,0:T(8,128)(2,1)S(1)} %get-tuple-element.99.dx0_ref), channel_id=1, source_target_pairs={{1,16},{2,17},{3,18},{5,20},{6,21},{7,22},{9,24},{10,25},{11,26},{... | collective-permute-start | bytes 147464 | tf_op jit(solution)/shard_map/ppermute | solution.py:133
  35.0 7.3 %collective-permute-start.11 = (bf16[16,1536]{1,0:T(8,128)(2,1)S(1)}, bf16[16,1536]{1,0:T(8,128)(2,1)S(1)}, u32[]{:S(2)}, u32[]{:S(2)}) collective-permute-start(bf16[16,1536]{1,0:T(8,128)(2,1)S(1)} %get-tuple-element.99.dx0_ref), channel_id=1, source_target_pairs={{1,0},{2,1},{3,2},{5,4},{6,5},{7,6},{9,8},{10,9},{11,10},{13,12},{... | collective-permute-start | bytes 147464 | tf_op jit(solution)/shard_map/ppermute | solution.py:133
  36.5 9.4 %collective-permute-start.14 = (bf16[16,1152]{1,0:T(8,128)(2,1)S(1)}, bf16[16,1152]{1,0:T(8,128)(2,1)S(1)}, u32[]{:S(2)}, u32[]{:S(2)}) collective-permute-start(bf16[16,1152]{1,0:T(8,128)(2,1)S(1)} %slice.23), channel_id=1, source_target_pairs={{0,8},{4,12},{8,0},{12,4},{16,24},{20,28},{24,16},{28,20},{1,9},{5... | collective-permute-start | bytes 110600 | tf_op jit(solution)/shard_map/ppermute | solution.py:121
  37.7 8.3 %collective-permute-start.13 = (bf16[16,1024]{1,0:T(8,128)(2,1)S(1)}, bf16[16,1024]{1,0:T(8,128)(2,1)S(1)}, u32[]{:S(2)}, u32[]{:S(2)}) collective-permute-start(bf16[16,1024]{1,0:T(8,128)(2,1)S(1)} %slice.22), channel_id=1, source_target_pairs={{0,8},{4,12},{8,0},{12,4},{16,24},{20,28},{24,16},{28,20},{1,9},{5... | collective-permute-start | bytes 98312 | tf_op jit(solution)/shard_map/ppermute | solution.py:121
  46.0 1.4 %collective-permute-start.15 = (f32[16,2048]{1,0:T(8,128)S(1)}, f32[16,2048]{1,0:T(8,128)S(1)}, u32[]{:S(2)}, u32[]{:S(2)}) collective-permute-start(f32[16,2048]{1,0:T(8,128)S(1)} %get-tuple-element.107), channel_id=1, source_target_pairs={{0,4},{4,0},{8,12},{12,8},{16,20},{20,16},{24,28},{28,24},{1,5},{5... | collective-permute-start | bytes 393224 | tf_op jit(solution)/shard_map/ppermute | solution.py:121
  46.3 2.3 %collective-permute-start.17 = (bf16[16,2048]{1,0:T(8,128)(2,1)S(1)}, bf16[16,2048]{1,0:T(8,128)(2,1)S(1)}, u32[]{:S(2)}, u32[]{:S(2)}) collective-permute-start(bf16[16,2048]{1,0:T(8,128)(2,1)S(1)} %get-tuple-element.108.refs_2_), channel_id=1, source_target_pairs={{0,4},{4,0},{8,12},{12,8},{16,20},{20,16},{24,28},{28,24},{1,5},{5... | collective-permute-start | bytes 196616 | tf_op jit(solution)/shard_map/ppermute | solution.py:121
  47.4 4.7 %collective-permute-start.16 = (bf16[16,2048]{1,0:T(8,128)(2,1)S(1)}, bf16[16,2048]{1,0:T(8,128)(2,1)S(1)}, u32[]{:S(2)}, u32[]{:S(2)}) collective-permute-start(bf16[16,2048]{1,0:T(8,128)(2,1)S(1)} %get-tuple-element.130), channel_id=1, source_target_pairs={{0,8},{4,12},{8,0},{12,4},{16,24},{20,28},{24,16},{28,20},{1,9},{5... | collective-permute-start | bytes 196616 | tf_op jit(solution)/shard_map/ppermute | solution.py:121
  52.3 1.3 %collective-permute-start.18 = (bf16[16,2176]{1,0:T(8,128)(2,1)S(1)}, bf16[16,2176]{1,0:T(8,128)(2,1)S(1)}, u32[]{:S(2)}, u32[]{:S(2)}) collective-permute-start(bf16[16,2176]{1,0:T(8,128)(2,1)S(1)} %get-tuple-element.114.own1.own_ref), channel_id=1, source_target_pairs={{0,4},{4,0},{8,12},{12,8},{16,20},{20,16},{24,28},{28,24},{1,5},{5... | collective-permute-start | bytes 208904 | tf_op jit(solution)/shard_map/ppermute | solution.py:121
  57.4 1.5 %collective-permute-start.19 = (bf16[4,16,1536]{2,1,0:T(8,128)(2,1)S(1)}, bf16[4,16,1536]{2,1,0:T(8,128)(2,1)S(1)}, u32[]{:S(2)}, u32[]{:S(2)}) collective-permute-start(bf16[4,16,1536]{2,1,0:T(8,128)(2,1)S(1)} %get-tuple-element.121), channel_id=1, source_target_pairs={{0,4},{4,0},{8,12},{12,8},{16,20},{20,16},{24,28},{28,24},{1,5},{5... | collective-permute-start | bytes 589832 | tf_op jit(solution)/shard_map/ppermute | solution.py:121
  58.9 7.7 %collective-permute-start.20 = (bf16[2,16,1536]{2,1,0:T(8,128)(2,1)S(1)}, bf16[2,16,1536]{2,1,0:T(8,128)(2,1)S(1)}, u32[]{:S(2)}, u32[]{:S(2)}) collective-permute-start(bf16[2,16,1536]{2,1,0:T(8,128)(2,1)S(1)} %get-tuple-element.123), channel_id=1, source_target_pairs={{0,8},{4,12},{8,0},{12,4},{16,24},{20,28},{24,16},{28,20},{1,9},{5... | collective-permute-start | bytes 294920 | tf_op jit(solution)/shard_map/ppermute | solution.py:121
  59.9 6.7 %collective-permute-start.21 = (bf16[2,16,1536]{2,1,0:T(8,128)(2,1)S(1)}, bf16[2,16,1536]{2,1,0:T(8,128)(2,1)S(1)}, u32[]{:S(2)}, u32[]{:S(2)}) collective-permute-start(bf16[2,16,1536]{2,1,0:T(8,128)(2,1)S(1)} %get-tuple-element.124), channel_id=1, source_target_pairs={{0,16},{4,20},{8,24},{12,28},{16,0},{20,4},{24,8},{28,12},{1,17},{... | collective-permute-start | bytes 294920 | tf_op jit(solution)/shard_map/ppermute | solution.py:121
  61.1 5.6 %collective-permute-start.22 = (bf16[2,16,1536]{2,1,0:T(8,128)(2,1)S(1)}, bf16[2,16,1536]{2,1,0:T(8,128)(2,1)S(1)}, u32[]{:S(2)}, u32[]{:S(2)}) collective-permute-start(bf16[2,16,1536]{2,1,0:T(8,128)(2,1)S(1)} %get-tuple-element.125), channel_id=1, source_target_pairs={{0,24},{4,28},{8,16},{12,20},{16,8},{20,12},{24,0},{28,4},{1,25},{... | collective-permute-start | bytes 294920 | tf_op jit(solution)/shard_map/ppermute | solution.py:121
  62.5 4.3 %copy-start.3 = (s32[8]{0:T(128)S(1)}, s32[8]{0:T(128)}, u32[]{:S(2)}) copy-start(s32[8]{0:T(128)} %counts_ref.1) | copy-start | bytes 100
  (3 other events, 12.7 us)
